TPU v7x, 32 devices: a whole 2x2x4 slice. The times are simulated.
32 devices in a mesh: bag: 8 (over z, core), ulysses: 4 (over y, x).
Axes of the slice: x: 2, y: 2, z: 4, core: 2. Of those that a mesh axis runs over, the one named last changes fastest.
Arguments:
- queries: bfloat16 [2048, 4096], P(('bag', 'ulysses')), may hold values from -13 to 13
- keys: bfloat16 [2048, 4096], P(('bag', 'ulysses')), may hold values from -13 to 13
- values: bfloat16 [2048, 4096], P(('bag', 'ulysses')), may hold values from -6 to 6
- span_route: int32 [8, 4, 8], P('bag'), may hold values from 0 to 7, each once within a row
- seq_lengths: int32 [8, 4], P('bag'), may hold values from 1 to 128, 256 in all within a row
Outputs:
- attended: bfloat16 [2048, 4096], P(('bag', 'ulysses'))
Inputs may be any that keep to these rules, and one draw needn't show every extreme that they name: For each b and u, span_route[b, u, 0 to 7] is a permutation of the bags. `seq_lengths`: row B lists bag B's 4 sequence lengths in packed order; each row sums to 256 and its largest entry is 128.
All inputs are finite; a program needn't handle non-finite values.
Results may differ from a plain program's by a relative error of at most 0.0049.
Values may be sent and summed in bfloat16 or wider, within the bound.
No kernel may reach another device: no remote copies, remote signals or barrier semaphores. Data moves between devices by JAX's collectives and lax.ppermute only.
A program may use at most 64 MiB of HBM per device.

v0:
```python
import math

import jax
import jax.numpy as jnp
from jax import lax
from jax.sharding import PartitionSpec as P

HEADS = 32
HDIM = 128


def build_sequence(lengths, bag_tok):
    seq_ends = jnp.cumsum(lengths)
    positions = jnp.arange(bag_tok, dtype=jnp.int32)
    return jnp.sum((positions[:, None] >= seq_ends[None, :]).astype(jnp.int32), axis=1)


def attend_local(query_rows, key_rows, value_rows, sequence, heads_here):
    bag_tok = query_rows.shape[0]
    head_cols = heads_here * HDIM
    block_rows = min(512, bag_tok)
    block_count = bag_tok // block_rows
    score_scale = 1.0 / math.sqrt(HDIM)
    query_heads = query_rows.reshape(bag_tok, heads_here, HDIM)
    key_heads = key_rows.reshape(bag_tok, heads_here, HDIM)
    value_heads = value_rows.reshape(bag_tok, heads_here, HDIM)

    def one_block(block_index, result):
        first_row = block_index * block_rows
        query_block = lax.dynamic_slice_in_dim(query_heads, first_row, block_rows, 0)
        query_seq = lax.dynamic_slice_in_dim(sequence, first_row, block_rows, 0)
        scores = (
            jnp.einsum("qhd,khd->hqk", query_block, key_heads, preferred_element_type=jnp.float32)
            * score_scale
        )
        scores = jnp.where((query_seq[:, None] == sequence[None, :])[None, :, :], scores, -jnp.inf)
        row_max = jnp.max(scores, axis=-1, keepdims=True)
        expo = jnp.exp(scores - row_max)
        weights = (expo / jnp.sum(expo, axis=-1, keepdims=True)).astype(jnp.bfloat16)
        output = jnp.einsum(
            "hqk,khd->qhd", weights, value_heads, preferred_element_type=jnp.float32
        )
        output = output.astype(jnp.bfloat16).reshape(block_rows, head_cols)
        return lax.dynamic_update_slice_in_dim(result, output, first_row, 0)

    return lax.fori_loop(0, block_count, one_block, jnp.zeros((bag_tok, head_cols), jnp.bfloat16))


def shards(queries, keys, values, span_route, seq_lengths):
    bag_count = lax.axis_size("bag")
    group_count = lax.axis_size("ulysses")
    tok_dev, row_width = queries.shape
    span_len = tok_dev // bag_count
    heads_here = HEADS // group_count
    head_cols = heads_here * HDIM
    bag_tok = tok_dev * group_count
    route_rows = span_route[0]
    column = jnp.arange(bag_count, dtype=jnp.int32)
    inverse_all = jnp.sum(
        jnp.where(route_rows[:, None, :] == column[None, :, None], column[None, None, :], 0), axis=2
    )
    my_group = lax.axis_index("ulysses")
    route_mine = lax.dynamic_index_in_dim(route_rows, my_group, 0, keepdims=False)
    inverse_mine = lax.dynamic_index_in_dim(inverse_all, my_group, 0, keepdims=False)

    def to_slots(rows):
        return jnp.take(rows.reshape(bag_count, span_len, row_width), inverse_mine, axis=0)

    arrived = (
        lax.all_to_all(to_slots(queries), "bag", split_axis=0, concat_axis=0, tiled=True),
        lax.all_to_all(to_slots(keys), "bag", split_axis=0, concat_axis=0, tiled=True),
        lax.all_to_all(to_slots(values), "bag", split_axis=0, concat_axis=0, tiled=True),
    )

    def split_cols(rows):
        return rows.reshape(bag_count * span_len, group_count, head_cols)

    packed = (
        lax.all_to_all(split_cols(arrived[0]), "ulysses", split_axis=1, concat_axis=0, tiled=True),
        lax.all_to_all(split_cols(arrived[1]), "ulysses", split_axis=1, concat_axis=0, tiled=True),
        lax.all_to_all(split_cols(arrived[2]), "ulysses", split_axis=1, concat_axis=0, tiled=True),
    )
    sequence = build_sequence(seq_lengths[0], bag_tok)
    attended_bag = attend_local(
        packed[0].reshape(bag_tok, head_cols),
        packed[1].reshape(bag_tok, head_cols),
        packed[2].reshape(bag_tok, head_cols),
        sequence,
        heads_here,
    )
    merged = lax.all_to_all(
        attended_bag.reshape(group_count, bag_count * span_len, head_cols),
        "ulysses",
        split_axis=0,
        concat_axis=2,
        tiled=True,
    )
    returned = lax.all_to_all(
        merged.reshape(bag_count, span_len, row_width),
        "bag",
        split_axis=0,
        concat_axis=0,
        tiled=True,
    )
    result = jnp.take(returned, route_mine, axis=0)
    return result.reshape(tok_dev, row_width)


def solution(mesh):
    placed = (
        P(("bag", "ulysses"), None),
        P(("bag", "ulysses"), None),
        P(("bag", "ulysses"), None),
        P("bag", None, None),
        P("bag", None),
    )
    return jax.shard_map(
        shards, mesh=mesh, in_specs=placed, out_specs=P(("bag", "ulysses"), None), check_vma=False
    )
```

profile of v0, /device:TPU:0, one launch (start us, length us, event | category | flops | bytes accessed | tf_op | source)
XLA Modules:
  0.0 131.3 jit_solution(15317281154229234446)
XLA Ops:
  0.0 0.9 select_reduce_fusion
  1.1 0.6 gather_fusion
  1.6 1.6 %gather_fusion.1 = bf16[8,8,4096]{2,1,0:T(8,128)(2,1)S(1)} fusion(bf16[8,8,4096]{2,1,0:T(8,128)(2,1)} %bitcast.51, s32[1024]{0:T(1024)S(1)} %pad_clamp_fusion.1), kind=kCustom, calls=%fused_computation.1.clone | custom fusion | bytes 1048608 | tf_op jit(solution)/shard_map/jit(_take)/gather | solution.py:67
  3.3 0.6 gather_fusion.2
  3.9 1.0 broadcast_select_fusion.2
  4.9 21.5 %all_to_all.80 = bf16[8,8,4096]{2,1,0:T(8,128)(2,1)S(1)} all-to-all(bf16[8,8,4096]{2,1,0:T(8,128)(2,1)S(1)} %get-tuple-element.32), channel_id=1, replica_groups=mesh['bag'=8,'ulysses'=4] {'bag'}, dimensions={0} | all-to-all | bytes 1048576 | tf_op jit(solution)/shard_map/all_to_all | solution.py:70
  26.4 17.8 %all_to_all.81 = bf16[8,8,4096]{2,1,0:T(8,128)(2,1)S(1)} all-to-all(bf16[8,8,4096]{2,1,0:T(8,128)(2,1)S(1)} %get-tuple-element.33), channel_id=1, replica_groups=mesh['bag'=8,'ulysses'=4] {'bag'}, dimensions={0} | all-to-all | bytes 1048576 | tf_op jit(solution)/shard_map/all_to_all | solution.py:71
  44.1 3.5 %all-to-all-start = ((bf16[8,8,4096]{2,1,0:T(8,128)(2,1)}), bf16[8,8,4096]{2,1,0:T(8,128)(2,1)S(1)}, u32[]{:S(2)}, u32[]{:S(2)}) async-start(bf16[8,8,4096]{2,1,0:T(8,128)(2,1)} %get-tuple-element.30), calls=%async_computation | async-start | bytes 1048576 | tf_op jit(solution)/shard_map/all_to_all | solution.py:72
  47.7 0.4 reshape.100
  48.0 1.0 copy.33
  49.0 13.9 %all-to-all-done = bf16[8,8,4096]{2,1,0:T(8,128)(2,1)S(1)} async-done(((bf16[8,8,4096]{2,1,0:T(8,128)(2,1)}), bf16[8,8,4096]{2,1,0:T(8,128)(2,1)S(1)}, u32[]{:S(2)}, u32[]{:S(2)}) %all-to-all-start) | async-done | bytes 524320 | tf_op jit(solution)/shard_map/all_to_all | solution.py:72
  62.9 3.7 %all-to-all-start.3 = ((bf16[64,4,1024]{2,0,1:T(8,128)(2,1)}), bf16[64,4,1024]{2,0,1:T(8,128)(2,1)S(1)}, u32[]{:S(2)}, u32[]{:S(2)}) async-start(bf16[64,4,1024]{2,0,1:T(8,128)(2,1)} %copy.33), calls=%async_computation.3 | async-start | bytes 1048576 | tf_op jit(solution)/shard_map/all_to_all | solution.py:79
  66.6 0.4 reshape.102
  67.0 1.0 copy.34
  68.0 6.5 %all-to-all-done.3 = bf16[64,4,1024]{2,0,1:T(8,128)(2,1)S(1)} async-done(((bf16[64,4,1024]{2,0,1:T(8,128)(2,1)}), bf16[64,4,1024]{2,0,1:T(8,128)(2,1)S(1)}, u32[]{:S(2)}, u32[]{:S(2)}) %all-to-all-start.3) | async-done | bytes 524320 | tf_op jit(solution)/shard_map/all_to_all | solution.py:79
  74.5 3.5 %all-to-all-start.5 = ((bf16[64,4,1024]{2,0,1:T(8,128)(2,1)}), bf16[64,4,1024]{2,0,1:T(8,128)(2,1)S(1)}, u32[]{:S(2)}, u32[]{:S(2)}) async-start(bf16[64,4,1024]{2,0,1:T(8,128)(2,1)} %copy.34), calls=%async_computation.5 | async-start | bytes 1048576 | tf_op jit(solution)/shard_map/all_to_all | solution.py:80
  78.0 0.4 reshape.96
  78.3 1.0 copy.32
  79.3 5.6 %all-to-all-done.5 = bf16[64,4,1024]{2,0,1:T(8,128)(2,1)S(1)} async-done(((bf16[64,4,1024]{2,0,1:T(8,128)(2,1)}), bf16[64,4,1024]{2,0,1:T(8,128)(2,1)S(1)}, u32[]{:S(2)}, u32[]{:S(2)}) %all-to-all-start.5) | async-done | bytes 524320 | tf_op jit(solution)/shard_map/all_to_all | solution.py:80
  84.9 3.5 %all-to-all-start.1 = ((bf16[64,4,1024]{2,0,1:T(8,128)(2,1)}), bf16[64,4,1024]{2,0,1:T(8,128)(2,1)S(1)}, u32[]{:S(2)}, u32[]{:S(2)}) async-start(bf16[64,4,1024]{2,0,1:T(8,128)(2,1)} %copy.32), calls=%async_computation.1 | async-start | bytes 1048576 | tf_op jit(solution)/shard_map/all_to_all | solution.py:81
  89.0 5.9 %all-to-all-done.1 = bf16[64,4,1024]{2,0,1:T(8,128)(2,1)S(1)} async-done(((bf16[64,4,1024]{2,0,1:T(8,128)(2,1)}), bf16[64,4,1024]{2,0,1:T(8,128)(2,1)S(1)}, u32[]{:S(2)}, u32[]{:S(2)}) %all-to-all-start.1) | async-done | bytes 524320 | tf_op jit(solution)/shard_map/all_to_all | solution.py:81
  95.0 2.2 %fusion.24 = (f32[8,256]{1,0:T(8,128)S(1)}, f32[8,256,256]{1,2,0:T(8,128)}) fusion(pred[256,256]{0,1:T(8,128)(4,1)S(1)} %broadcast_compare_fusion, bf16[256,8,128]{2,1,0:T(8,128)(2,1)S(1)} %bitcast.49, bf16[256,8,128]{2,1,0:T(8,128)(2,1)S(1)} %bitcast.48), kind=kOutput, calls=%fused_computation.35 | convolution fusion | flops 136315136 | bytes 3219456 | tf_op jit(solution)/shard_map/while/body/eval_jaxpr/sub | solution.py:38
  97.2 1.9 %fusion.2 = bf16[256,8,128]{0,2,1:T(8,128)(2,1)S(1)} fusion(f32[8,256,256]{1,2,0:T(8,128)} %get-tuple-element.35, f32[8,256]{1,0:T(8,128)S(1)} %get-tuple-element.34, bf16[256,8,128]{2,1,0:T(8,128)(2,1)S(1)} %bitcast.50), kind=kOutput, calls=%fused_computation.10 | convolution fusion | flops 135528448 | bytes 3153920 | tf_op jit(solution)/shard_map/while/body/eval_jaxpr/hqk,khd->qhd/dot_general | solution.py:40
  99.1 0.3 copy.39
  99.7 9.7 %all_to_all.82 = bf16[4,64,1024]{2,1,0:T(8,128)(2,1)S(1)} all-to-all(bf16[4,64,1024]{2,1,0:T(8,128)(2,1)S(1)} %reshape.103), channel_id=1, replica_groups=mesh['bag'=8,'ulysses'=4] {'ulysses'}, dimensions={0} | all-to-all | bytes 1048576 | tf_op jit(solution)/shard_map/all_to_all | solution.py:91
  109.4 0.4 copy.40
  109.8 1.2 reshape.104
  111.0 3.5 %all-to-all-start.7 = ((bf16[8,8,4096]{2,1,0:T(8,128)(2,1)}), bf16[8,8,4096]{2,1,0:T(8,128)(2,1)S(1)}, u32[]{:S(2)}, u32[]{:S(2)}) async-start(bf16[8,8,4096]{2,1,0:T(8,128)(2,1)} %reshape.104), calls=%async_computation.7 | async-start | bytes 1048576 | tf_op jit(solution)/shard_map/all_to_all | solution.py:98
  114.5 0.7 compare_and_fusion
  115.2 14.6 %all-to-all-done.7 = bf16[8,8,4096]{2,1,0:T(8,128)(2,1)S(1)} async-done(((bf16[8,8,4096]{2,1,0:T(8,128)(2,1)}), bf16[8,8,4096]{2,1,0:T(8,128)(2,1)S(1)}, u32[]{:S(2)}, u32[]{:S(2)}) %all-to-all-start.7) | async-done | bytes 524320 | tf_op jit(solution)/shard_map/all_to_all | solution.py:98
  129.8 0.6 gather_fusion.3
  130.3 0.9 select_bitcast_fusion
  (16 shorter events, 1.0 us)
Async XLA Ops:
  0.0 1.1 copy-start
  0.0 3.3 %copy-start.1 = (bf16[64,4096]{1,0:T(8,128)(2,1)S(1)}, bf16[64,4096]{1,0:T(8,128)(2,1)}, u32[]{:S(2)}) copy-start(bf16[64,4096]{1,0:T(8,128)(2,1)} %param.8) | copy-start | bytes 1572868
  44.1 18.8 %all-to-all-start = ((bf16[8,8,4096]{2,1,0:T(8,128)(2,1)}), bf16[8,8,4096]{2,1,0:T(8,128)(2,1)S(1)}, u32[]{:S(2)}, u32[]{:S(2)}) async-start(bf16[8,8,4096]{2,1,0:T(8,128)(2,1)} %get-tuple-element.30), calls=%async_computation | async-start | bytes 1048576 | tf_op jit(solution)/shard_map/all_to_all | solution.py:72
  62.9 11.5 %all-to-all-start.3 = ((bf16[64,4,1024]{2,0,1:T(8,128)(2,1)}), bf16[64,4,1024]{2,0,1:T(8,128)(2,1)S(1)}, u32[]{:S(2)}, u32[]{:S(2)}) async-start(bf16[64,4,1024]{2,0,1:T(8,128)(2,1)} %copy.33), calls=%async_computation.3 | async-start | bytes 1048576 | tf_op jit(solution)/shard_map/all_to_all | solution.py:79
  68.0 20.4 %copy-start.2 = (s32[1,4]{1,0:T(1,128)S(1)}, s32[1,4]{1,0:T(1,128)}, u32[]{:S(2)}) copy-start(s32[1,4]{1,0:T(1,128)} %param.11) | copy-start | bytes 52
  74.5 10.4 %all-to-all-start.5 = ((bf16[64,4,1024]{2,0,1:T(8,128)(2,1)}), bf16[64,4,1024]{2,0,1:T(8,128)(2,1)S(1)}, u32[]{:S(2)}, u32[]{:S(2)}) async-start(bf16[64,4,1024]{2,0,1:T(8,128)(2,1)} %copy.34), calls=%async_computation.5 | async-start | bytes 1048576 | tf_op jit(solution)/shard_map/all_to_all | solution.py:80
  84.9 10.0 %all-to-all-start.1 = ((bf16[64,4,1024]{2,0,1:T(8,128)(2,1)}), bf16[64,4,1024]{2,0,1:T(8,128)(2,1)S(1)}, u32[]{:S(2)}, u32[]{:S(2)}) async-start(bf16[64,4,1024]{2,0,1:T(8,128)(2,1)} %copy.32), calls=%async_computation.1 | async-start | bytes 1048576 | tf_op jit(solution)/shard_map/all_to_all | solution.py:81
  111.0 18.8 %all-to-all-start.7 = ((bf16[8,8,4096]{2,1,0:T(8,128)(2,1)}), bf16[8,8,4096]{2,1,0:T(8,128)(2,1)S(1)}, u32[]{:S(2)}, u32[]{:S(2)}) async-start(bf16[8,8,4096]{2,1,0:T(8,128)(2,1)} %reshape.104), calls=%async_computation.7 | async-start | bytes 1048576 | tf_op jit(solution)/shard_map/all_to_all | solution.py:98
where the time goes:
time: 132 us; the launch traced here: 131 us
  blocking collectives  48.9 us (37%)
  waiting for transfers between devices  46.6 us (35%)
  starting transfers between devices  17.6 us (13%)
  local copies, waits for them, and re-layouts  9.87 us (7%)
  matrix products  4.1 us (3%)
  other arithmetic  3.96 us (3%)
    all_to_all x1, blocking collectives, shards(): lax.all_to_all(to_slots(queries), 'bag', split_axis=0, concat_axis=0, til...  21.5 us
    all_to_all x1, blocking collectives, shards(): lax.all_to_all(to_slots(keys), 'bag', split_axis=0, concat_axis=0, tiled=...  17.8 us
    all_to_all x1, waiting for transfers between devices, shards(): lax.all_to_all(merged.reshape(bag_count, span_len, row_width), 'bag', spl...  14.6 us
    all_to_all x1, waiting for transfers between devices, shards(): lax.all_to_all(to_slots(values), 'bag', split_axis=0, concat_axis=0, tile...  13.9 us
    all_to_all x1, blocking collectives, shards(): lax.all_to_all(attended_bag.reshape(group_count, bag_count * span_len, he...  9.7 us
    all_to_all x1, waiting for transfers between devices, shards(): lax.all_to_all(split_cols(arrived[0]), 'ulysses', split_axis=1, concat_ax...  6.49 us
    all_to_all x1, waiting for transfers between devices, shards(): lax.all_to_all(split_cols(arrived[2]), 'ulysses', split_axis=1, concat_ax...  5.95 us
    all_to_all x1, waiting for transfers between devices, shards(): lax.all_to_all(split_cols(arrived[1]), 'ulysses', split_axis=1, concat_ax...  5.62 us
  transfers between devices with their start and end apart: 5, of which 5 were waited for; matrix products, arithmetic and copies ran while one was open for 4% of the time, Pallas kernels for 0%

commit v1 on v0

v1 whole, which is shorter than its diff:
```python
import math

import jax
import jax.numpy as jnp
from jax import lax
from jax.experimental import pallas as pl
from jax.experimental.pallas import tpu as pltpu
from jax.sharding import PartitionSpec as P

HEADS = 32
HDIM = 128
PARTS = 1
ROW_TILE = 8
AXES = ("bag", "ulysses")


def pack_spans(route_mine, arrays, group_count, parts):
    bag_count, span_len, row_width = arrays[0].shape
    width = row_width // group_count // parts
    kinds = len(arrays)

    def kernel(route_ref, *refs):
        sources, targets, sems = refs[:kinds], refs[kinds : kinds + parts], refs[-1]
        for part in range(parts):

            def one_span(span, carry, part=part):
                bag = route_ref[span]
                for group in range(group_count):
                    first = (group * parts + part) * width
                    for kind in range(kinds):
                        pltpu.make_async_copy(
                            sources[kind].at[span, :, pl.ds(first, width)],
                            targets[part].at[bag * group_count + group, kind],
                            sems.at[part],
                        ).start()
                return carry

            lax.fori_loop(0, bag_count, one_span, 0, unroll=True)
        for part in range(parts):
            pltpu.make_async_copy(targets[part], targets[part], sems.at[part]).wait()

    shape = (bag_count * group_count, kinds, span_len, width)
    return pl.pallas_call(
        kernel,
        out_shape=[jax.ShapeDtypeStruct(shape, arrays[0].dtype)] * parts,
        in_specs=[pl.BlockSpec(memory_space=pltpu.SMEM)] + [pl.BlockSpec(memory_space=pl.ANY)] * kinds,
        out_specs=[pl.BlockSpec(memory_space=pltpu.VMEM)] * parts,
        scratch_shapes=[pltpu.SemaphoreType.DMA((parts,))],
        name="pack_spans",
    )(route_mine, *arrays)


def unpack_spans(route_mine, pieces, bag_count, group_count):
    parts = len(pieces)
    span_len, width = pieces[0].shape[1:]
    row_width = width * parts * group_count

    def kernel(route_ref, *refs):
        sources, target, sem = refs[:parts], refs[parts], refs[-1]

        def one_span(span, carry):
            bag = route_ref[span]
            for part in range(parts):
                for group in range(group_count):
                    first = (group * parts + part) * width
                    pltpu.make_async_copy(
                        sources[part].at[bag * group_count + group],
                        target.at[span, :, pl.ds(first, width)],
                        sem,
                    ).start()
            return carry

        lax.fori_loop(0, bag_count, one_span, 0, unroll=True)
        pltpu.make_async_copy(target, target, sem).wait()

    return pl.pallas_call(
        kernel,
        out_shape=jax.ShapeDtypeStruct((bag_count, span_len, row_width), pieces[0].dtype),
        in_specs=[pl.BlockSpec(memory_space=pltpu.SMEM)] + [pl.BlockSpec(memory_space=pltpu.VMEM)] * parts,
        out_specs=pl.BlockSpec(memory_space=pl.ANY),
        scratch_shapes=[pltpu.SemaphoreType.DMA],
        name="unpack_spans",
    )(route_mine, *pieces)


def attend(lengths, packed, bag_count, group_count):
    slots, _, span_len, width = packed.shape
    bag_tok = slots * span_len
    block = min(256, bag_tok)
    block_slots = block // span_len
    heads_here = width // HDIM
    seq_bag = lengths.shape[0]
    scale = 1.0 / math.sqrt(HDIM)

    def sequence_of(row, length_ref):
        slot, offset = row // span_len, row % span_len
        owner, group = slot // group_count, slot % group_count
        position = (group * bag_count + owner) * span_len + offset
        end = jnp.int32(0)
        sequence = jnp.zeros(row.shape, jnp.int32)
        for entry in range(seq_bag):
            end = end + length_ref[entry]
            sequence = sequence + (position >= end).astype(jnp.int32)
        return sequence

    def kernel(length_ref, packed_ref, out_ref):
        key_seq = sequence_of(lax.broadcasted_iota(jnp.int32, (1, bag_tok), 1), length_ref)

        def rows(kind, first, count, head):
            tile = packed_ref[pl.ds(first, count), kind, :, head * HDIM : (head + 1) * HDIM]
            return tile.astype(jnp.float32).reshape(count * span_len, HDIM).astype(jnp.bfloat16)

        for index in range(bag_tok // block):
            row = index * block + lax.broadcasted_iota(jnp.int32, (block, 1), 0)
            same = sequence_of(row, length_ref) == key_seq
            for head in range(heads_here):
                query = rows(0, index * block_slots, block_slots, head)
                key = rows(1, 0, slots, head)
                value = rows(2, 0, slots, head)
                scores = lax.dot_general(query, key, (((1,), (1,)), ((), ())), preferred_element_type=jnp.float32)
                scores = jnp.where(same, scores * scale, -jnp.inf)
                expo = jnp.exp(scores - jnp.max(scores, axis=-1, keepdims=True))
                weights = (expo / jnp.sum(expo, axis=-1, keepdims=True)).astype(jnp.bfloat16)
                output = jnp.dot(weights, value, preferred_element_type=jnp.float32)
                out_ref[pl.ds(index * block_slots, block_slots), :, head * HDIM : (head + 1) * HDIM] = output.reshape(
                    block_slots, span_len, HDIM
                ).astype(out_ref.dtype)

    return pl.pallas_call(
        kernel,
        out_shape=jax.ShapeDtypeStruct((slots, span_len, width), packed.dtype),
        in_specs=[pl.BlockSpec(memory_space=pltpu.SMEM), pl.BlockSpec(memory_space=pltpu.VMEM)],
        out_specs=pl.BlockSpec(memory_space=pltpu.VMEM),
        compiler_params=pltpu.CompilerParams(vmem_limit_bytes=32 << 20),
        cost_estimate=pl.CostEstimate(
            flops=4 * bag_tok * bag_tok * width, bytes_accessed=4 * bag_tok * width * 2, transcendentals=bag_tok * bag_tok * heads_here
        ),
        name="attend_bag",
    )(lengths, packed)


def exchange(rows):
    return lax.all_to_all(rows, AXES, split_axis=0, concat_axis=0, tiled=True)


def shards(queries, keys, values, span_route, seq_lengths):
    bag_count = lax.axis_size("bag")
    group_count = lax.axis_size("ulysses")
    tok_dev, row_width = queries.shape
    span_len = tok_dev // bag_count
    parts = PARTS
    width = row_width // group_count // parts
    route_mine = lax.dynamic_index_in_dim(span_route[0], lax.axis_index("ulysses"), 0, keepdims=False)
    arrays = [rows.reshape(bag_count, span_len, row_width) for rows in (queries, keys, values)]
    direct = span_len % ROW_TILE == 0
    if direct:
        packed = pack_spans(route_mine, arrays, group_count, parts)
    else:
        inverse = jnp.argsort(route_mine)
        stacked = jnp.stack(arrays)[:, inverse].reshape(3, bag_count, span_len, group_count, parts, width)
        stacked = stacked.transpose(4, 1, 3, 0, 2, 5).reshape(parts, bag_count * group_count, 3, span_len, width)
        packed = [stacked[part] for part in range(parts)]
    returned = []
    for part in range(parts):
        arrived = exchange(packed[part])
        returned.append(exchange(attend(seq_lengths[0], arrived, bag_count, group_count)))
    if direct:
        result = unpack_spans(route_mine, returned, bag_count, group_count)
    else:
        stacked = jnp.stack(returned).reshape(parts, bag_count, group_count, span_len, width)
        result = stacked.transpose(1, 3, 2, 0, 4)[route_mine]
    return result.reshape(tok_dev, row_width)


def solution(mesh):
    placed = (
        P(("bag", "ulysses"), None),
        P(("bag", "ulysses"), None),
        P(("bag", "ulysses"), None),
        P("bag", None, None),
        P("bag", None),
    )
    return jax.shard_map(
        shards, mesh=mesh, in_specs=placed, out_specs=P(("bag", "ulysses"), None), check_vma=False
    )
```

time: 132 us -> 73.4 us (0.56)
  waiting for transfers between devices: 46.6 us -> 0 us
  starting transfers between devices: 17.6 us -> 0 us
  blocking collectives: 48.9 us -> 64.7 us
  local copies, waits for them, and re-layouts: 9.87 us -> 1.22 us
  Pallas kernels: 0 us -> 7.14 us
  matrix products: 4.1 us -> 0 us
  other arithmetic: 3.96 us -> 0 us
    all_to_all x5 -> x0, waiting for transfers between devices: 46.6 us -> none  [the longest x1 14.6 us: shards(): lax.all_to_all(merged.reshape(bag_count, span_len, row_width), 'bag', spl...]
    all_to_all x5 -> x0, starting transfers between devices: 17.6 us -> none  [the longest x1 3.72 us: shards(): lax.all_to_all(split_cols(arrived[0]), 'ulysses', split_axis=1, concat_ax...]
    all_to_all x3 -> x2, blocking collectives: 48.9 us -> 64.7 us  [exchange(): return lax.all_to_all(rows, AXES, split_axis=0, concat_axis=0, tiled=True)]
    pallas_call x0 -> x3, Pallas kernels: none -> 7.14 us  [the longest x1 3.18 us: pack_spans(): pl.pallas_call(kernel, out_shape=[jax.ShapeDtypeStruct(shape, arrays[0].d...]
    reshape x8 -> x0, local copies, waits for them, and re-layouts: 5.39 us -> none  [the longest x6 3.99 us: split_cols(): return rows.reshape(bag_count * span_len, group_count, head_cols)]
    gather x4 -> x0, local copies, waits for them, and re-layouts: 3.36 us -> none  [the longest x3 2.78 us: to_slots(): jnp.take(rows.reshape(bag_count, span_len, row_width), inverse_mine, axis=0)]
    sub x1 -> x0, matrix products: 2.16 us -> none  [one_block(): expo = jnp.exp(scores - row_max)]
    dot_general x1 -> x0, matrix products: 1.94 us -> none  [one_block(): jnp.einsum('hqk,khd->qhd', weights, value_heads, preferred_element_type=j...]
  transfers between devices with their start and end apart: 5 -> 0, of which waited for: 5 -> 0; matrix products, arithmetic and copies ran while one was open for 4% -> 0% of each run, Pallas kernels for 0% -> 0%
where the time goes in v1:
time: 73.4 us; the launch traced here: 73.1 us
  blocking collectives  64.7 us (88%)
  Pallas kernels  7.14 us (10%)
  local copies, waits for them, and re-layouts  1.22 us (2%)
    all_to_all x2, blocking collectives, exchange(): return lax.all_to_all(rows, AXES, split_axis=0, concat_axis=0, tiled=True)  64.7 us
    pallas_call x1, Pallas kernels, pack_spans(): pl.pallas_call(kernel, out_shape=[jax.ShapeDtypeStruct(shape, arrays[0].d...  3.18 us
    pallas_call x1, Pallas kernels, attend(): pl.pallas_call(kernel, out_shape=jax.ShapeDtypeStruct((slots, span_len, w...  2.12 us
    pallas_call x1, Pallas kernels, unpack_spans(): pl.pallas_call(kernel, out_shape=jax.ShapeDtypeStruct((bag_count, span_le...  1.83 us

profile of v1, /device:TPU:0, one launch (start us, length us, event | category | flops | bytes accessed | tf_op | source)
XLA Modules:
  0.0 73.1 jit_solution(12584560645319361678)
XLA Ops:
  0.0 0.0 copy-start
  0.0 0.7 copy-done
  0.7 0.5 dynamic-slice_bitcast_fusion.route_ref
  1.2 3.2 %pack_spans.1 = bf16[32,3,8,1024]{3,2,1,0:T(8,128)(2,1)} custom-call(s32[8]{0:T(128)} %dynamic-slice_bitcast_fusion.route_ref, bf16[8,8,4096]{2,1,0:T(8,128)(2,1)} %bitcast.8, bf16[8,8,4096]{2,1,0:T(8,128)(2,1)} %bitcast.9, bf16[8,8,4096]{2,1,0:T(8,128)(2,1)} %bitcast.10), custom_call_target="tpu_custom_call" | custom-call | tf_op jit(solution)/shard_map/pack_spans/pallas_call | solution.py:43
  4.4 0.0 copy-start.1
  4.4 46.0 %all_to_all.10.packed_ref = bf16[32,3,8,1024]{3,2,1,0:T(8,128)(2,1)S(1)} all-to-all(bf16[32,3,8,1024]{3,2,1,0:T(8,128)(2,1)} %pack_spans.1), channel_id=1, replica_groups=mesh['bag'=8,'ulysses'=4] {'bag','ulysses'}, dimensions={0} | all-to-all | bytes 3145728 | tf_op jit(solution)/shard_map/all_to_all | solution.py:143
  50.5 0.0 copy-done.1
  50.5 2.1 %attend_bag.1 = bf16[32,8,1024]{2,1,0:T(8,128)(2,1)S(1)} custom-call(s32[4]{0:T(128)S(1)} %bitcast.7, bf16[32,3,8,1024]{3,2,1,0:T(8,128)(2,1)S(1)} %all_to_all.10.packed_ref), custom_call_target="tpu_custom_call" | custom-call | flops 268435456 | bytes 2097152 | tf_op jit(solution)/shard_map/attend_bag/pallas_call | solution.py:129
  52.6 18.6 %all_to_all.11.refs_0_ = bf16[32,8,1024]{2,1,0:T(8,128)(2,1)} all-to-all(bf16[32,8,1024]{2,1,0:T(8,128)(2,1)S(1)} %attend_bag.1), channel_id=1, replica_groups=mesh['bag'=8,'ulysses'=4] {'bag','ulysses'}, dimensions={0} | all-to-all | bytes 1048576 | tf_op jit(solution)/shard_map/all_to_all | solution.py:143
  71.2 1.8 %unpack_spans.1 = bf16[8,8,4096]{2,1,0:T(8,128)(2,1)} custom-call(s32[8]{0:T(128)} %dynamic-slice_bitcast_fusion.route_ref, bf16[32,8,1024]{2,1,0:T(8,128)(2,1)} %all_to_all.11.refs_0_), custom_call_target="tpu_custom_call" | custom-call | tf_op jit(solution)/shard_map/unpack_spans/pallas_call | solution.py:76
Async XLA Ops:
  0.0 0.7 copy-start
  4.4 46.0 %copy-start.1 = (s32[1,4]{1,0:T(1,128)S(1)}, s32[1,4]{1,0:T(1,128)}, u32[]{:S(2)}) copy-start(s32[1,4]{1,0:T(1,128)} %param.9) | copy-start | bytes 52

commit v2 on v1

v2 whole, which is shorter than its diff:
```python
import math

import jax
import jax.numpy as jnp
from jax import lax
from jax.experimental import pallas as pl
from jax.experimental.pallas import tpu as pltpu
from jax.sharding import PartitionSpec as P

HDIM = 128
ROW_TILE = 8
MARGIN = 1 << 20
AXES = ("bag", "ulysses")


def pack_spans(span_route, arrays):
    bag_count, group_count, heads_here, span_len, width = arrays[0].shape
    kinds = len(arrays)
    payload = sum(rows.nbytes for rows in arrays)

    def kernel(route_hbm, *refs):
        sources, target, stage, route_ref, sem = refs[:kinds], refs[kinds], refs[-3], refs[-2], refs[-1]
        group = lax.axis_index("ulysses")
        copies = [pltpu.make_async_copy(sources[k], stage.at[k], sem.at[k]) for k in range(kinds)]
        for copy in copies:
            copy.start()
        route_copy = pltpu.make_async_copy(route_hbm, route_ref, sem.at[kinds])
        route_copy.start()
        route_copy.wait()
        for kind in range(kinds):
            copies[kind].wait()
            for span in range(bag_count):
                target[route_ref[0, group, span], :, kind] = stage[kind, span]

    shape = (bag_count, group_count, kinds, heads_here, span_len, width)
    packed = pl.pallas_call(
        kernel,
        out_shape=pltpu.VMEM(shape, arrays[0].dtype),
        in_specs=[pl.BlockSpec(memory_space=pl.ANY)] * (1 + kinds),
        out_specs=pl.BlockSpec(memory_space=pltpu.VMEM),
        scratch_shapes=[pltpu.VMEM((kinds, *arrays[0].shape), arrays[0].dtype), pltpu.SMEM(span_route.shape, span_route.dtype), pltpu.SemaphoreType.DMA((kinds + 1,))],
        compiler_params=pltpu.CompilerParams(vmem_limit_bytes=2 * payload + MARGIN),
        name="pack_spans",
    )(*[pltpu.with_memory_space_constraint(rows, pltpu.HBM) for rows in (span_route, *arrays)])
    return packed.reshape(bag_count * group_count, *shape[2:])


def unpack_spans(span_route, returned):
    bag_count, group_count = returned.shape[:2]

    def kernel(route_ref, source, target, sem):
        group = lax.axis_index("ulysses")
        for span in range(bag_count):
            pltpu.make_async_copy(source.at[route_ref[0, group, span]], target.at[span], sem).start()
        pltpu.make_async_copy(target, target, sem).wait()

    return pl.pallas_call(
        kernel,
        out_shape=jax.ShapeDtypeStruct(returned.shape, returned.dtype),
        in_specs=[pl.BlockSpec(memory_space=pltpu.SMEM), pl.BlockSpec(memory_space=pltpu.VMEM)],
        out_specs=pl.BlockSpec(memory_space=pl.ANY),
        scratch_shapes=[pltpu.SemaphoreType.DMA],
        compiler_params=pltpu.CompilerParams(vmem_limit_bytes=returned.nbytes + MARGIN),
        name="unpack_spans",
    )(span_route, returned)


def attend(lengths, packed, bag_count, group_count):
    slots, _, heads_here, span_len, width = packed.shape
    bag_tok = slots * span_len
    block = min(256, bag_tok)
    block_slots = block // span_len
    seq_bag = lengths.shape[1]
    scale = 1.0 / math.sqrt(width)

    def sequence_of(row, length_ref):
        slot, offset = row // span_len, row % span_len
        owner, group = slot // group_count, slot % group_count
        position = (group * bag_count + owner) * span_len + offset
        end = jnp.int32(0)
        sequence = jnp.zeros(row.shape, jnp.int32)
        for entry in range(seq_bag):
            end = end + length_ref[0, entry]
            sequence = sequence + (position >= end).astype(jnp.int32)
        return sequence

    def kernel(length_ref, packed_ref, out_ref):
        key_seq = sequence_of(lax.broadcasted_iota(jnp.int32, (1, bag_tok), 1), length_ref)

        def rows(kind, first, count, head):
            tile = packed_ref[pl.ds(first, count), kind, head]
            return tile.astype(jnp.float32).reshape(count * span_len, width).astype(jnp.bfloat16)

        def one_block(index, carry):
            first = index * block_slots
            row = index * block + lax.broadcasted_iota(jnp.int32, (block, 1), 0)
            same = sequence_of(row, length_ref) == key_seq
            scores = [
                lax.dot_general(
                    rows(0, first, block_slots, head),
                    rows(1, 0, slots, head),
                    (((1,), (1,)), ((), ())),
                    preferred_element_type=jnp.float32,
                )
                for head in range(heads_here)
            ]
            weights = []
            for score in scores:
                score = jnp.where(same, score * scale, -jnp.inf)
                expo = jnp.exp(score - jnp.max(score, axis=-1, keepdims=True))
                weights.append((expo * (1.0 / jnp.sum(expo, axis=-1, keepdims=True))).astype(jnp.bfloat16))
            for head in range(heads_here):
                output = jnp.dot(weights[head], rows(2, 0, slots, head), preferred_element_type=jnp.float32)
                output = output.reshape(block_slots, span_len, width).astype(out_ref.dtype)
                out_ref[pl.ds(first, block_slots), head] = output
            return carry

        if bag_tok == block:
            one_block(0, 0)
        else:
            lax.fori_loop(0, bag_tok // block, one_block, 0)

    return pl.pallas_call(
        kernel,
        out_shape=jax.ShapeDtypeStruct((slots, heads_here, span_len, width), packed.dtype),
        in_specs=[pl.BlockSpec(memory_space=pltpu.SMEM), pl.BlockSpec(memory_space=pltpu.VMEM)],
        out_specs=pl.BlockSpec(memory_space=pltpu.VMEM),
        compiler_params=pltpu.CompilerParams(vmem_limit_bytes=32 << 20),
        name="attend_bag",
    )(lengths, packed)


def exchange(rows):
    return lax.all_to_all(rows, AXES, split_axis=0, concat_axis=0, tiled=True)


def shards(queries, keys, values, span_route, seq_lengths):
    bag_count = lax.axis_size("bag")
    group_count = lax.axis_size("ulysses")
    tok_dev, row_width = queries.shape
    span_len = tok_dev // bag_count
    heads_here = row_width // HDIM // group_count
    arrays = [
        rows.reshape(bag_count, span_len, group_count, heads_here, HDIM).transpose(0, 2, 3, 1, 4)
        for rows in (queries, keys, values)
    ]
    direct = span_len % ROW_TILE == 0
    if direct:
        packed = pack_spans(span_route, arrays)
    else:
        route_mine = lax.dynamic_index_in_dim(span_route[0], lax.axis_index("ulysses"), 0, keepdims=False)
        packed = jnp.stack(arrays, axis=2)[jnp.argsort(route_mine)]
        packed = packed.reshape(bag_count * group_count, *packed.shape[2:])
    attended = attend(seq_lengths, exchange(packed), bag_count, group_count)
    returned = exchange(attended).reshape(bag_count, group_count, *attended.shape[1:])
    result = unpack_spans(span_route, returned) if direct else returned[route_mine]
    return result.transpose(0, 3, 1, 2, 4).reshape(tok_dev, row_width)


def solution(mesh):
    placed = (
        P(("bag", "ulysses"), None),
        P(("bag", "ulysses"), None),
        P(("bag", "ulysses"), None),
        P("bag", None, None),
        P("bag", None),
    )
    return jax.shard_map(
        shards, mesh=mesh, in_specs=placed, out_specs=P(("bag", "ulysses"), None), check_vma=False
    )
```

time: 73.4 us -> 69 us (0.940)
  Pallas kernels: 7.14 us -> 4.52 us
  local copies, waits for them, and re-layouts: 1.22 us -> 0.01 us
    pallas_call x3, Pallas kernels: 7.14 us -> 4.52 us  [the longest x1 1.73 us: attend(): pl.pallas_call(kernel, out_shape=jax.ShapeDtypeStruct((slots, heads_here,...]
where the time goes in v2:
time: 69 us; the launch traced here: 68.8 us
  blocking collectives  64.3 us (93%)
  Pallas kernels  4.52 us (7%)
    all_to_all x2, blocking collectives, exchange(): return lax.all_to_all(rows, AXES, split_axis=0, concat_axis=0, tiled=True)  64.3 us
    pallas_call x1, Pallas kernels, attend(): pl.pallas_call(kernel, out_shape=jax.ShapeDtypeStruct((slots, heads_here,...  1.73 us
    pallas_call x1, Pallas kernels, pack_spans(): pl.pallas_call(kernel, out_shape=pltpu.VMEM(shape, arrays[0].dtype), in_s...  1.43 us

profile of v2, /device:TPU:0, one launch (start us, length us, event | category | flops | bytes accessed | tf_op | source)
XLA Modules:
  0.0 68.8 jit_solution(17233016814120407957)
XLA Ops:
  0.0 1.4 %pack_spans.1 = bf16[8,4,3,8,8,128]{5,4,3,2,1,0:T(8,128)(2,1)S(1)} custom-call(s32[1,4,8]{2,1,0:T(4,128)} %route_ref.1, bf16[8,4,8,8,128]{4,3,2,1,0:T(8,128)(2,1)} %bitcast.16, bf16[8,4,8,8,128]{4,3,2,1,0:T(8,128)(2,1)} %bitcast.17, bf16[8,4,8,8,128]{4,3,2,1,0:T(8,128)(2,1)} %bitcast.18), custom_call_target="tpu_custom_call" | custom-call | tf_op jit(solution)/shard_map/pack_spans/pallas_call | solution.py:36
  1.4 0.0 copy-start.1
  1.4 45.8 %all_to_all.10.packed_ref = bf16[32,3,8,8,128]{4,3,2,1,0:T(8,128)(2,1)S(1)} all-to-all(bf16[32,3,8,8,128]{4,3,2,1,0:T(8,128)(2,1)S(1)} %bitcast.14), channel_id=1, replica_groups=mesh['bag'=8,'ulysses'=4] {'bag','ulysses'}, dimensions={0} | all-to-all | bytes 3145728 | tf_op jit(solution)/shard_map/all_to_all | solution.py:134
  47.3 0.0 copy-done.1
  47.3 0.0 copy-start
  47.3 1.7 %attend_bag.1 = bf16[32,8,8,128]{3,2,1,0:T(8,128)(2,1)S(1)} custom-call(s32[1,4]{1,0:T(1,128)S(1)} %copy-done.1, bf16[32,3,8,8,128]{4,3,2,1,0:T(8,128)(2,1)S(1)} %all_to_all.10.packed_ref), custom_call_target="tpu_custom_call" | custom-call | tf_op jit(solution)/shard_map/attend_bag/pallas_call | solution.py:123
  49.0 18.4 %all_to_all.11 = bf16[32,8,8,128]{3,2,1,0:T(8,128)(2,1)S(1)} all-to-all(bf16[32,8,8,128]{3,2,1,0:T(8,128)(2,1)S(1)} %attend_bag.1), channel_id=1, replica_groups=mesh['bag'=8,'ulysses'=4] {'bag','ulysses'}, dimensions={0} | all-to-all | bytes 1048576 | tf_op jit(solution)/shard_map/all_to_all | solution.py:134
  67.4 0.0 copy-done
  67.5 1.4 %unpack_spans.1 = bf16[8,4,8,8,128]{4,3,2,1,0:T(8,128)(2,1)} custom-call(s32[1,4,8]{2,1,0:T(4,128)S(1)} %copy-done, bf16[8,4,8,8,128]{4,3,2,1,0:T(8,128)(2,1)S(1)} %bitcast.15), custom_call_target="tpu_custom_call" | custom-call | tf_op jit(solution)/shard_map/unpack_spans/pallas_call | solution.py:57
Async XLA Ops:
  1.4 45.8 %copy-start.1 = (s32[1,4]{1,0:T(1,128)S(1)}, s32[1,4]{1,0:T(1,128)}, u32[]{:S(2)}) copy-start(s32[1,4]{1,0:T(1,128)} %length_ref.1) | copy-start | bytes 52
  47.3 20.2 %copy-start = (s32[1,4,8]{2,1,0:T(4,128)S(1)}, s32[1,4,8]{2,1,0:T(4,128)}, u32[]{:S(2)}) copy-start(s32[1,4,8]{2,1,0:T(4,128)} %route_ref.1) | copy-start | bytes 388

commit v3 on v2

--- a/solution.py
+++ b/solution.py
@@ -22,10 +22,10 @@
         sources, target, stage, route_ref, sem = refs[:kinds], refs[kinds], refs[-3], refs[-2], refs[-1]
         group = lax.axis_index("ulysses")
         copies = [pltpu.make_async_copy(sources[k], stage.at[k], sem.at[k]) for k in range(kinds)]
+        route_copy = pltpu.make_async_copy(route_hbm, route_ref, sem.at[kinds])
+        route_copy.start()
         for copy in copies:
             copy.start()
-        route_copy = pltpu.make_async_copy(route_hbm, route_ref, sem.at[kinds])
-        route_copy.start()
         route_copy.wait()
         for kind in range(kinds):
             copies[kind].wait()
@@ -38,7 +38,11 @@
         out_shape=pltpu.VMEM(shape, arrays[0].dtype),
         in_specs=[pl.BlockSpec(memory_space=pl.ANY)] * (1 + kinds),
         out_specs=pl.BlockSpec(memory_space=pltpu.VMEM),
-        scratch_shapes=[pltpu.VMEM((kinds, *arrays[0].shape), arrays[0].dtype), pltpu.SMEM(span_route.shape, span_route.dtype), pltpu.SemaphoreType.DMA((kinds + 1,))],
+        scratch_shapes=[
+            pltpu.VMEM((kinds, *arrays[0].shape), arrays[0].dtype),
+            pltpu.SMEM(span_route.shape, span_route.dtype),
+            pltpu.SemaphoreType.DMA((kinds + 1,)),
+        ],
         compiler_params=pltpu.CompilerParams(vmem_limit_bytes=2 * payload + MARGIN),
         name="pack_spans",
     )(*[pltpu.with_memory_space_constraint(rows, pltpu.HBM) for rows in (span_route, *arrays)])
@@ -57,7 +61,7 @@
     return pl.pallas_call(
         kernel,
         out_shape=jax.ShapeDtypeStruct(returned.shape, returned.dtype),
-        in_specs=[pl.BlockSpec(memory_space=pltpu.SMEM), pl.BlockSpec(memory_space=pltpu.VMEM)],
+        in_specs=[pl.BlockSpec(memory_space=pltpu.VMEM)] * 2,
         out_specs=pl.BlockSpec(memory_space=pl.ANY),
         scratch_shapes=[pltpu.SemaphoreType.DMA],
         compiler_params=pltpu.CompilerParams(vmem_limit_bytes=returned.nbytes + MARGIN),
@@ -77,10 +81,10 @@
         slot, offset = row // span_len, row % span_len
         owner, group = slot // group_count, slot % group_count
         position = (group * bag_count + owner) * span_len + offset
-        end = jnp.int32(0)
+        end = jnp.zeros((1, 1), jnp.int32)
         sequence = jnp.zeros(row.shape, jnp.int32)
         for entry in range(seq_bag):
-            end = end + length_ref[0, entry]
+            end = end + length_ref[:, entry : entry + 1]
             sequence = sequence + (position >= end).astype(jnp.int32)
         return sequence
 
@@ -123,7 +127,7 @@
     return pl.pallas_call(
         kernel,
         out_shape=jax.ShapeDtypeStruct((slots, heads_here, span_len, width), packed.dtype),
-        in_specs=[pl.BlockSpec(memory_space=pltpu.SMEM), pl.BlockSpec(memory_space=pltpu.VMEM)],
+        in_specs=[pl.BlockSpec(memory_space=pltpu.VMEM)] * 2,
         out_specs=pl.BlockSpec(memory_space=pltpu.VMEM),
         compiler_params=pltpu.CompilerParams(vmem_limit_bytes=32 << 20),
         name="attend_bag",

time: 69 us -> 68 us (0.986)
  Pallas kernels: 4.52 us -> 3.48 us
where the time goes in v3:
time: 68 us; the launch traced here: 67.8 us
  blocking collectives  64.3 us (95%)
  Pallas kernels  3.48 us (5%)
    all_to_all x2, blocking collectives, exchange(): return lax.all_to_all(rows, AXES, split_axis=0, concat_axis=0, tiled=True)  64.3 us
    pallas_call x1, Pallas kernels, pack_spans(): pl.pallas_call(kernel, out_shape=pltpu.VMEM(shape, arrays[0].dtype), in_s...  1.43 us

profile of v3, /device:TPU:0, one launch (start us, length us, event | category | flops | bytes accessed | tf_op | source)
XLA Modules:
  0.0 67.8 jit_solution(15253705449840380373)
XLA Ops:
  0.0 1.4 %pack_spans.1 = bf16[8,4,3,8,8,128]{5,4,3,2,1,0:T(8,128)(2,1)S(1)} custom-call(s32[1,4,8]{2,1,0:T(4,128)} %route_ref.1, bf16[8,4,8,8,128]{4,3,2,1,0:T(8,128)(2,1)} %bitcast.16, bf16[8,4,8,8,128]{4,3,2,1,0:T(8,128)(2,1)} %bitcast.17, bf16[8,4,8,8,128]{4,3,2,1,0:T(8,128)(2,1)} %bitcast.18), custom_call_target="tpu_custom_call" | custom-call | tf_op jit(solution)/shard_map/pack_spans/pallas_call | solution.py:36
  1.4 0.0 copy-start.1
  1.4 45.8 %all_to_all.10.packed_ref = bf16[32,3,8,8,128]{4,3,2,1,0:T(8,128)(2,1)S(1)} all-to-all(bf16[32,3,8,8,128]{4,3,2,1,0:T(8,128)(2,1)S(1)} %bitcast.14), channel_id=1, replica_groups=mesh['bag'=8,'ulysses'=4] {'bag','ulysses'}, dimensions={0} | all-to-all | bytes 3145728 | tf_op jit(solution)/shard_map/all_to_all | solution.py:138
  47.3 0.0 copy-done.1
  47.3 0.0 copy-start
  47.3 1.2 %attend_bag.1 = bf16[32,8,8,128]{3,2,1,0:T(8,128)(2,1)S(1)} custom-call(s32[1,4]{1,0:T(1,128)S(1)} %copy-done.1, bf16[32,3,8,8,128]{4,3,2,1,0:T(8,128)(2,1)S(1)} %all_to_all.10.packed_ref), custom_call_target="tpu_custom_call" | custom-call | tf_op jit(solution)/shard_map/attend_bag/pallas_call | solution.py:127
  48.5 18.4 %all_to_all.11 = bf16[32,8,8,128]{3,2,1,0:T(8,128)(2,1)S(1)} all-to-all(bf16[32,8,8,128]{3,2,1,0:T(8,128)(2,1)S(1)} %attend_bag.1), channel_id=1, replica_groups=mesh['bag'=8,'ulysses'=4] {'bag','ulysses'}, dimensions={0} | all-to-all | bytes 1048576 | tf_op jit(solution)/shard_map/all_to_all | solution.py:138
  66.9 0.0 copy-done
  66.9 0.9 %unpack_spans.1 = bf16[8,4,8,8,128]{4,3,2,1,0:T(8,128)(2,1)} custom-call(s32[1,4,8]{2,1,0:T(4,128)S(1)} %copy-done, bf16[8,4,8,8,128]{4,3,2,1,0:T(8,128)(2,1)S(1)} %bitcast.15), custom_call_target="tpu_custom_call" | custom-call | tf_op jit(solution)/shard_map/unpack_spans/pallas_call | solution.py:61
Async XLA Ops:
  1.4 45.8 %copy-start.1 = (s32[1,4]{1,0:T(1,128)S(1)}, s32[1,4]{1,0:T(1,128)}, u32[]{:S(2)}) copy-start(s32[1,4]{1,0:T(1,128)} %length_ref.1) | copy-start | bytes 52
  47.3 19.6 %copy-start = (s32[1,4,8]{2,1,0:T(4,128)S(1)}, s32[1,4,8]{2,1,0:T(4,128)}, u32[]{:S(2)}) copy-start(s32[1,4,8]{2,1,0:T(4,128)} %route_ref.1) | copy-start | bytes 388

commit v4 on v3

--- a/solution.py
+++ b/solution.py
@@ -10,6 +10,7 @@
 HDIM = 128
 ROW_TILE = 8
 MARGIN = 1 << 20
+CORES = 2
 AXES = ("bag", "ulysses")
 
 
@@ -30,9 +31,10 @@
         for kind in range(kinds):
             copies[kind].wait()
             for span in range(bag_count):
-                target[route_ref[0, group, span], :, kind] = stage[kind, span]
+                to = route_ref[0, group, span]
+                target[:, to % CORES, to // CORES, kind] = stage[kind, span]
 
-    shape = (bag_count, group_count, kinds, heads_here, span_len, width)
+    shape = (group_count, CORES, bag_count // CORES, kinds, heads_here, span_len, width)
     packed = pl.pallas_call(
         kernel,
         out_shape=pltpu.VMEM(shape, arrays[0].dtype),
@@ -46,21 +48,23 @@
         compiler_params=pltpu.CompilerParams(vmem_limit_bytes=2 * payload + MARGIN),
         name="pack_spans",
     )(*[pltpu.with_memory_space_constraint(rows, pltpu.HBM) for rows in (span_route, *arrays)])
-    return packed.reshape(bag_count * group_count, *shape[2:])
+    return packed.reshape(bag_count * group_count, *shape[3:])
 
 
 def unpack_spans(span_route, returned):
-    bag_count, group_count = returned.shape[:2]
+    group_count, _, chips = returned.shape[:3]
+    bag_count = chips * CORES
 
     def kernel(route_ref, source, target, sem):
         group = lax.axis_index("ulysses")
         for span in range(bag_count):
-            pltpu.make_async_copy(source.at[route_ref[0, group, span]], target.at[span], sem).start()
+            bag = route_ref[0, group, span]
+            pltpu.make_async_copy(source.at[:, bag % CORES, bag // CORES], target.at[span], sem).start()
         pltpu.make_async_copy(target, target, sem).wait()
 
     return pl.pallas_call(
         kernel,
-        out_shape=jax.ShapeDtypeStruct(returned.shape, returned.dtype),
+        out_shape=jax.ShapeDtypeStruct((bag_count, group_count, *returned.shape[3:]), returned.dtype),
         in_specs=[pl.BlockSpec(memory_space=pltpu.VMEM)] * 2,
         out_specs=pl.BlockSpec(memory_space=pl.ANY),
         scratch_shapes=[pltpu.SemaphoreType.DMA],
@@ -79,7 +83,7 @@
 
     def sequence_of(row, length_ref):
         slot, offset = row // span_len, row % span_len
-        owner, group = slot // group_count, slot % group_count
+        group, owner = slot // bag_count, slot % (bag_count // CORES) * CORES + slot % bag_count // (bag_count // CORES)
         position = (group * bag_count + owner) * span_len + offset
         end = jnp.zeros((1, 1), jnp.int32)
         sequence = jnp.zeros(row.shape, jnp.int32)
@@ -135,7 +139,14 @@
 
 
 def exchange(rows):
-    return lax.all_to_all(rows, AXES, split_axis=0, concat_axis=0, tiled=True)
+    bag_count, group_count = lax.axis_size("bag"), lax.axis_size("ulysses")
+    order = [
+        bag * group_count + group
+        for group in range(group_count)
+        for core in range(CORES)
+        for bag in range(core, bag_count, CORES)
+    ]
+    return lax.all_to_all(rows, AXES, split_axis=0, concat_axis=0, tiled=True, axis_index_groups=[order])
 
 
 def shards(queries, keys, values, span_route, seq_lengths):
@@ -148,16 +159,21 @@
         rows.reshape(bag_count, span_len, group_count, heads_here, HDIM).transpose(0, 2, 3, 1, 4)
         for rows in (queries, keys, values)
     ]
+    slots = (group_count, CORES, bag_count // CORES)
     direct = span_len % ROW_TILE == 0
     if direct:
         packed = pack_spans(span_route, arrays)
     else:
         route_mine = lax.dynamic_index_in_dim(span_route[0], lax.axis_index("ulysses"), 0, keepdims=False)
         packed = jnp.stack(arrays, axis=2)[jnp.argsort(route_mine)]
-        packed = packed.reshape(bag_count * group_count, *packed.shape[2:])
+        packed = packed.reshape(*slots[:0:-1], *packed.shape[1:]).swapaxes(0, 2)
+        packed = packed.reshape(bag_count * group_count, *packed.shape[3:])
     attended = attend(seq_lengths, exchange(packed), bag_count, group_count)
-    returned = exchange(attended).reshape(bag_count, group_count, *attended.shape[1:])
-    result = unpack_spans(span_route, returned) if direct else returned[route_mine]
+    returned = exchange(attended).reshape(*slots, *attended.shape[1:])
+    if direct:
+        result = unpack_spans(span_route, returned)
+    else:
+        result = returned.swapaxes(0, 2).reshape(bag_count, group_count, *attended.shape[1:])[route_mine]
     return result.transpose(0, 3, 1, 2, 4).reshape(tok_dev, row_width)
 
 

time: 68 us -> 66.7 us (0.981); the launches traced: 67.8 us -> 65.8 us
  blocking collectives: 64.3 us -> 62.2 us
    all_to_all x2, blocking collectives: 64.3 us -> 62.2 us  [exchange(): lax.all_to_all(rows, AXES, split_axis=0, concat_axis=0, tiled=True, axis_...]
where the time goes in v4:
time: 66.7 us; the launch traced here: 65.8 us
  blocking collectives  62.2 us (93%)
  Pallas kernels  3.55 us (5%)
    all_to_all x2, blocking collectives, exchange(): lax.all_to_all(rows, AXES, split_axis=0, concat_axis=0, tiled=True, axis_...  62.2 us
    pallas_call x1, Pallas kernels, pack_spans(): pl.pallas_call(kernel, out_shape=pltpu.VMEM(shape, arrays[0].dtype), in_s...  1.45 us

profile of v4, /device:TPU:0, one launch (start us, length us, event | category | flops | bytes accessed | tf_op | source)
XLA Modules:
  0.0 65.8 jit_solution(5417047206509815899)
XLA Ops:
  0.0 1.4 %pack_spans.1 = bf16[4,2,4,3,8,8,128]{6,5,4,3,2,1,0:T(8,128)(2,1)S(1)} custom-call(s32[1,4,8]{2,1,0:T(4,128)} %route_ref.1, bf16[8,4,8,8,128]{4,3,2,1,0:T(8,128)(2,1)} %bitcast.16, bf16[8,4,8,8,128]{4,3,2,1,0:T(8,128)(2,1)} %bitcast.17, bf16[8,4,8,8,128]{4,3,2,1,0:T(8,128)(2,1)} %bitcast.18), custom_call_target="tpu_custom_call" | custom-call | tf_op jit(solution)/shard_map/pack_spans/pallas_call | solution.py:38
  1.5 0.0 copy-start.1
  1.5 43.9 %all_to_all.10.packed_ref = bf16[32,3,8,8,128]{4,3,2,1,0:T(8,128)(2,1)S(1)} all-to-all(bf16[32,3,8,8,128]{4,3,2,1,0:T(8,128)(2,1)S(1)} %bitcast.14), channel_id=1, replica_groups={{0,8,16,24,4,12,20,28,1,9,17,25,5,13,21,29,2,10,18,26,6,14,22,30,3,11,1..., dimensions={0} | all-to-all | bytes 3145728 | tf_op jit(solution)/shard_map/all_to_all | solution.py:149
  45.4 0.0 copy-done.1
  45.4 0.0 copy-start
  45.4 1.2 %attend_bag.1 = bf16[32,8,8,128]{3,2,1,0:T(8,128)(2,1)S(1)} custom-call(s32[1,4]{1,0:T(1,128)S(1)} %copy-done.1, bf16[32,3,8,8,128]{4,3,2,1,0:T(8,128)(2,1)S(1)} %all_to_all.10.packed_ref), custom_call_target="tpu_custom_call" | custom-call | tf_op jit(solution)/shard_map/attend_bag/pallas_call | solution.py:131
  46.6 18.3 %all_to_all.11 = bf16[32,8,8,128]{3,2,1,0:T(8,128)(2,1)S(1)} all-to-all(bf16[32,8,8,128]{3,2,1,0:T(8,128)(2,1)S(1)} %attend_bag.1), channel_id=1, replica_groups={{0,8,16,24,4,12,20,28,1,9,17,25,5,13,21,29,2,10,18,26,6,14,22,30,3,11,1..., dimensions={0} | all-to-all | bytes 1048576 | tf_op jit(solution)/shard_map/all_to_all | solution.py:149
  64.9 0.0 copy-done
  64.9 0.9 %unpack_spans.1 = bf16[8,4,8,8,128]{4,3,2,1,0:T(8,128)(2,1)} custom-call(s32[1,4,8]{2,1,0:T(4,128)S(1)} %copy-done, bf16[4,2,4,8,8,128]{5,4,3,2,1,0:T(8,128)(2,1)S(1)} %bitcast.15), custom_call_target="tpu_custom_call" | custom-call | tf_op jit(solution)/shard_map/unpack_spans/pallas_call | solution.py:65
Async XLA Ops:
  1.5 44.0 %copy-start.1 = (s32[1,4]{1,0:T(1,128)S(1)}, s32[1,4]{1,0:T(1,128)}, u32[]{:S(2)}) copy-start(s32[1,4]{1,0:T(1,128)} %length_ref.1) | copy-start | bytes 52
  45.4 19.5 %copy-start = (s32[1,4,8]{2,1,0:T(4,128)S(1)}, s32[1,4,8]{2,1,0:T(4,128)}, u32[]{:S(2)}) copy-start(s32[1,4,8]{2,1,0:T(4,128)} %route_ref.1) | copy-start | bytes 388

commit v5 on v4

--- a/solution.py
+++ b/solution.py
@@ -10,70 +10,225 @@
 HDIM = 128
 ROW_TILE = 8
 MARGIN = 1 << 20
+SPREAD = 1
+BASE = 128
 CORES = 2
 AXES = ("bag", "ulysses")
 
 
-def pack_spans(span_route, arrays):
+def pack_spans(span_route, seq_lengths, arrays, direct_heads):
     bag_count, group_count, heads_here, span_len, width = arrays[0].shape
-    kinds = len(arrays)
+    kinds, chips = len(arrays), bag_count // CORES
+    spread = heads_here - direct_heads
     payload = sum(rows.nbytes for rows in arrays)
 
-    def kernel(route_hbm, *refs):
-        sources, target, stage, route_ref, sem = refs[:kinds], refs[kinds], refs[-3], refs[-2], refs[-1]
-        group = lax.axis_index("ulysses")
+    seq_bag = seq_lengths.shape[1]
+    each = bag_count * group_count * spread
+
+    def kernel(route_hbm, lengths_hbm, *refs):
+        sources, (target, aside_q, aside_kv), (stage, lengths, route_ref, sem) = refs[:kinds], refs[kinds : kinds + 3], refs[-4:]
+        group, bag = lax.axis_index("ulysses"), lax.axis_index("bag")
         copies = [pltpu.make_async_copy(sources[k], stage.at[k], sem.at[k]) for k in range(kinds)]
         route_copy = pltpu.make_async_copy(route_hbm, route_ref, sem.at[kinds])
         route_copy.start()
         for copy in copies:
             copy.start()
+        lengths_copy = pltpu.make_async_copy(lengths_hbm, lengths, sem.at[kinds + 2])
+        lengths_copy.start()
         route_copy.wait()
+        lengths_copy.wait()
+        row = lax.broadcasted_iota(jnp.int32, (span_len, width), 0)
+        block = jnp.zeros((span_len, width), jnp.int32)
+        for entry in range(seq_bag):
+            length = lengths[:, entry : entry + 1]
+            block = jnp.where(row == 2 * entry, length // BASE, jnp.where(row == 2 * entry + 1, length % BASE, block))
+        aside_kv[(kinds - 1) * each] = block.astype(jnp.float32).astype(aside_kv.dtype)
         for kind in range(kinds):
             copies[kind].wait()
             for span in range(bag_count):
                 to = route_ref[0, group, span]
-                target[:, to % CORES, to // CORES, kind] = stage[kind, span]
-
-    shape = (group_count, CORES, bag_count // CORES, kinds, heads_here, span_len, width)
-    packed = pl.pallas_call(
-        kernel,
-        out_shape=pltpu.VMEM(shape, arrays[0].dtype),
-        in_specs=[pl.BlockSpec(memory_space=pl.ANY)] * (1 + kinds),
-        out_specs=pl.BlockSpec(memory_space=pltpu.VMEM),
+                pltpu.make_async_copy(
+                    stage.at[kind, span, :, pl.ds(0, direct_heads)],
+                    target.at[:, to % CORES, to // CORES, kind],
+                    sem.at[kinds + 1],
+                ).start()
+                for other in range(group_count):
+                    block = ((other ^ group) * CORES + (to % CORES ^ bag % CORES)) * chips + to // CORES
+                    block = block * spread
+                    for head in range(spread):
+                        rows = stage[kind, span, other, direct_heads + head]
+                        if kind == 0:
+                            aside_q[block + head] = rows
+                        else:
+                            aside_kv[(kind - 1) * each + block + head] = rows
+        pltpu.make_async_copy(target, target, sem.at[kinds + 1]).wait()
+
+    shape = (group_count, CORES, bag_count // CORES, kinds, direct_heads, span_len, width)
+    shape_aside = [(each, span_len, width), ((kinds - 1) * each + 1, span_len, width)]
+    dtype = arrays[0].dtype
+    packed, aside_q, aside_kv = pl.pallas_call(
+        kernel,
+        out_shape=[jax.ShapeDtypeStruct(shape, dtype)] + [pltpu.VMEM(size, dtype) for size in shape_aside],
+        in_specs=[pl.BlockSpec(memory_space=pl.ANY)] * (2 + kinds),
+        out_specs=[pl.BlockSpec(memory_space=pl.ANY)] + [pl.BlockSpec(memory_space=pltpu.VMEM)] * 2,
         scratch_shapes=[
-            pltpu.VMEM((kinds, *arrays[0].shape), arrays[0].dtype),
+            pltpu.VMEM((kinds, *arrays[0].shape), dtype),
+            pltpu.VMEM(seq_lengths.shape, seq_lengths.dtype),
             pltpu.SMEM(span_route.shape, span_route.dtype),
-            pltpu.SemaphoreType.DMA((kinds + 1,)),
+            pltpu.SemaphoreType.DMA((kinds + 3,)),
         ],
         compiler_params=pltpu.CompilerParams(vmem_limit_bytes=2 * payload + MARGIN),
         name="pack_spans",
-    )(*[pltpu.with_memory_space_constraint(rows, pltpu.HBM) for rows in (span_route, *arrays)])
-    return packed.reshape(bag_count * group_count, *shape[3:])
-
-
-def unpack_spans(span_route, returned):
-    group_count, _, chips = returned.shape[:3]
+    )(*[pltpu.with_memory_space_constraint(rows, pltpu.HBM) for rows in (span_route, seq_lengths, *arrays)])
+    return packed.reshape(bag_count * group_count, *shape[3:]), aside_q, aside_kv
+
+
+def unpack_spans(span_route, returned, pieces):
+    group_count, _, chips, direct_heads, span_len, width = returned.shape
     bag_count = chips * CORES
-
-    def kernel(route_ref, source, target, sem):
-        group = lax.axis_index("ulysses")
+    spread = pieces[0].shape[2]
+
+    def kernel(route_ref, source, *refs):
+        aside, (target, span_of, sem) = refs[:-3], refs[-3:]
+        group, bag = lax.axis_index("ulysses"), lax.axis_index("bag")
         for span in range(bag_count):
-            bag = route_ref[0, group, span]
-            pltpu.make_async_copy(source.at[:, bag % CORES, bag // CORES], target.at[span], sem).start()
+            at = route_ref[0, group, span]
+            span_of[at] = span
+            pltpu.make_async_copy(
+                source.at[:, at % CORES, at // CORES], target.at[span, :, pl.ds(0, direct_heads)], sem
+            ).start()
+        for distance, piece in enumerate(aside):
+            for core in range(CORES):
+                for chip in range(chips):
+                    pltpu.make_async_copy(
+                        piece.at[core, chip],
+                        target.at[span_of[chip * CORES + (bag % CORES ^ core)], group ^ distance, pl.ds(direct_heads, spread)],
+                        sem,
+                    ).start()
         pltpu.make_async_copy(target, target, sem).wait()
 
+    shape = (bag_count, group_count, direct_heads + spread, span_len, width)
     return pl.pallas_call(
         kernel,
-        out_shape=jax.ShapeDtypeStruct((bag_count, group_count, *returned.shape[3:]), returned.dtype),
-        in_specs=[pl.BlockSpec(memory_space=pltpu.VMEM)] * 2,
+        out_shape=jax.ShapeDtypeStruct(shape, returned.dtype),
+        in_specs=[pl.BlockSpec(memory_space=pltpu.VMEM)] * (2 + len(pieces)),
         out_specs=pl.BlockSpec(memory_space=pl.ANY),
-        scratch_shapes=[pltpu.SemaphoreType.DMA],
-        compiler_params=pltpu.CompilerParams(vmem_limit_bytes=returned.nbytes + MARGIN),
+        scratch_shapes=[pltpu.SMEM((bag_count,), jnp.int32), pltpu.SemaphoreType.DMA],
+        compiler_params=pltpu.CompilerParams(vmem_limit_bytes=2 * returned.nbytes + MARGIN),
         name="unpack_spans",
-    )(span_route, returned)
-
-
-def attend(lengths, packed, bag_count, group_count):
+    )(span_route, returned, *pieces)
+
+
+def swap(rows, axis, distance):
+    return lax.ppermute(rows, axis, [(index, index ^ distance) for index in range(lax.axis_size(axis))])
+
+
+def swap_cores(rows, axis):
+    kept, sent = (lax.index_in_dim(rows, core, axis, keepdims=False) for core in range(CORES))
+    return jnp.stack([kept, swap(sent, "bag", 1)], axis=axis)
+
+
+def swap_groups(rows):
+    return [rows[0]] + [swap(rows[distance], "ulysses", distance) for distance in range(1, rows.shape[0])]
+
+
+def merge(queries, near, across):
+    count, pair = queries.shape[0], near.shape[0] - 1
+    size = queries.shape[1:]
+
+    def kernel(query_ref, near_ref, across_ref, out_ref, length_ref):
+        out_ref[:count] = query_ref[...]
+        for index, ref in enumerate((near_ref, across_ref)):
+            out_ref[count + index * pair : count + (index + 1) * pair] = ref[:pair]
+            length_ref[index] = ref[pair]
+
+    return pl.pallas_call(
+        kernel,
+        out_shape=[pltpu.VMEM((count + 2 * pair, *size), queries.dtype), pltpu.VMEM((2, *size), queries.dtype)],
+        in_specs=[pl.BlockSpec(memory_space=pltpu.VMEM)] * 3,
+        out_specs=[pl.BlockSpec(memory_space=pltpu.VMEM)] * 2,
+        compiler_params=pltpu.CompilerParams(vmem_limit_bytes=4 << 20),
+        cost_estimate=pl.CostEstimate(flops=1 << 35, bytes_accessed=1 << 26, transcendentals=0),
+        name="merge",
+    )(queries, near, across)
+
+
+def gather_chips(near, lengths):
+    chips = lax.axis_size("bag") // CORES
+    size, distances = near.shape[1:], [0, chips // 2]
+    step = chips // 4
+    while step:
+        count = near.shape[0]
+        flat = jnp.concatenate([near.reshape(-1, *lengths.shape[1:]), lengths])
+        flat = swap(flat, "bag", step * CORES)
+        near = jnp.concatenate([near, flat[:-count].reshape(count, *size)])
+        lengths = jnp.concatenate([lengths, flat[-count:]])
+        distances, step = distances + [distance ^ step for distance in distances], step // 2
+    order = [distances.index(distance) for distance in range(chips)]
+    return jnp.stack([near[index] for index in order]), jnp.stack([lengths[index] for index in order])
+
+
+def attend_plane(lengths, queries, keys_values, seq_bag, bag_count):
+    group_count, _, chips, heads, span_len, width = queries.shape
+    block = group_count * CORES * span_len
+    scale = 1.0 / math.sqrt(width)
+
+    def kernel(length_ref, query_ref, pair_ref, out_ref):
+        bag, group = lax.axis_index("bag"), lax.axis_index("ulysses")
+        chip, core = bag // CORES, bag % CORES
+
+        def sequence_of(row, ends):
+            owner = ((row // block) ^ chip) * CORES + (row // span_len % CORES ^ core)
+            place = (row // (CORES * span_len) % group_count) ^ group
+            position = (place * bag_count + owner) * span_len + row % span_len
+            sequence = jnp.zeros(row.shape, jnp.int32)
+            for end in ends:
+                sequence = sequence + (position >= end).astype(jnp.int32)
+            return sequence
+
+        def rows(tile):
+            return tile.astype(jnp.float32).reshape(-1, width).astype(jnp.bfloat16)
+
+        masks, scores = [], []
+        for at in range(chips):
+            table = length_ref[at ^ chip].astype(jnp.float32).astype(jnp.int32)
+            end, ends = jnp.zeros((1, 1), jnp.int32), []
+            for entry in range(seq_bag):
+                end = end + table[2 * entry : 2 * entry + 1, :1] * BASE + table[2 * entry + 1 : 2 * entry + 2, :1]
+                ends.append(end)
+            query_seq = sequence_of(lax.broadcasted_iota(jnp.int32, (block, 1), 0), ends)
+            masks.append(query_seq == sequence_of(lax.broadcasted_iota(jnp.int32, (1, chips * block), 1), ends))
+        units = [(at, head) for at in range(chips) for head in range(heads)]
+        for at, head in units:
+            score = lax.dot_general(
+                rows(query_ref[:, :, at, head]),
+                rows(pair_ref[:, 0, :, :, at, head]),
+                (((1,), (1,)), ((), ())),
+                preferred_element_type=jnp.float32,
+            )
+            scores.append(jnp.where(masks[at], score * scale, -jnp.inf))
+        for (at, head), score in zip(units, scores):
+            expo = jnp.exp(score - jnp.max(score, axis=-1, keepdims=True))
+            weights = (expo * (1.0 / jnp.sum(expo, axis=-1, keepdims=True))).astype(jnp.bfloat16)
+            output = jnp.dot(weights, rows(pair_ref[:, 1, :, :, at, head]), preferred_element_type=jnp.float32)
+            out_ref[:, :, at, head] = output.reshape(group_count, CORES, span_len, width).astype(out_ref.dtype)
+
+    return pl.pallas_call(
+        kernel,
+        out_shape=jax.ShapeDtypeStruct(queries.shape, queries.dtype),
+        in_specs=[pl.BlockSpec(memory_space=pltpu.VMEM)] * 3,
+        out_specs=pl.BlockSpec(memory_space=pltpu.VMEM),
+        compiler_params=pltpu.CompilerParams(vmem_limit_bytes=8 << 20),
+        cost_estimate=pl.CostEstimate(
+            flops=4 * heads * chips * chips * block * block * width,
+            bytes_accessed=keys_values.nbytes + 2 * queries.nbytes,
+            transcendentals=heads * chips * chips * block * block,
+        ),
+        name="attend_plane",
+    )(lengths, queries, keys_values)
+
+
+def attend(lengths, packed, bag_count, group_count, after=()):
     slots, _, heads_here, span_len, width = packed.shape
     bag_tok = slots * span_len
     block = min(256, bag_tok)
@@ -92,7 +247,8 @@
             sequence = sequence + (position >= end).astype(jnp.int32)
         return sequence
 
-    def kernel(length_ref, packed_ref, out_ref):
+    def kernel(length_ref, packed_ref, *refs):
+        out_ref = refs[-1]
         key_seq = sequence_of(lax.broadcasted_iota(jnp.int32, (1, bag_tok), 1), length_ref)
 
         def rows(kind, first, count, head):
@@ -131,11 +287,11 @@
     return pl.pallas_call(
         kernel,
         out_shape=jax.ShapeDtypeStruct((slots, heads_here, span_len, width), packed.dtype),
-        in_specs=[pl.BlockSpec(memory_space=pltpu.VMEM)] * 2,
+        in_specs=[pl.BlockSpec(memory_space=pltpu.VMEM)] * 2 + [pl.BlockSpec(memory_space=pl.ANY)] * len(after),
         out_specs=pl.BlockSpec(memory_space=pltpu.VMEM),
         compiler_params=pltpu.CompilerParams(vmem_limit_bytes=32 << 20),
         name="attend_bag",
-    )(lengths, packed)
+    )(lengths, packed, *after)
 
 
 def exchange(rows):
@@ -160,19 +316,29 @@
         for rows in (queries, keys, values)
     ]
     slots = (group_count, CORES, bag_count // CORES)
-    direct = span_len % ROW_TILE == 0
-    if direct:
-        packed = pack_spans(span_route, arrays)
+    powers = all(size & (size - 1) == 0 for size in (bag_count, group_count))
+    if span_len >= 2 * seq_lengths.shape[1] and span_len % ROW_TILE == 0 and heads_here > SPREAD and bag_count > CORES and powers:
+        packed, aside_q, aside_kv = pack_spans(span_route, seq_lengths, arrays, heads_here - SPREAD)
+        across = swap(aside_kv, "bag", bag_count // 2)
+        arrived = exchange(packed)
+        blocks, tables = merge(aside_q, aside_kv, across)
+        blocks = blocks.reshape(5, group_count, CORES, -1, SPREAD, span_len, HDIM)
+        blocks = jnp.stack(swap_groups(swap_cores(blocks, 2).swapaxes(0, 1)), axis=1)
+        pairs = blocks[1:].reshape(2, 2, *blocks.shape[1:])
+        pairs, lengths = gather_chips(pairs, tables)
+        settled = attend_plane(lengths, blocks[0], pairs, seq_lengths.shape[1], bag_count)
+        settled = swap_cores(settled, 1)
+        attended = attend(seq_lengths, arrived, bag_count, group_count, (blocks,))
+        pieces = swap_groups(settled)
+        returned = exchange(attended).reshape(*slots, *attended.shape[1:])
+        result = unpack_spans(span_route, returned, pieces)
     else:
         route_mine = lax.dynamic_index_in_dim(span_route[0], lax.axis_index("ulysses"), 0, keepdims=False)
         packed = jnp.stack(arrays, axis=2)[jnp.argsort(route_mine)]
         packed = packed.reshape(*slots[:0:-1], *packed.shape[1:]).swapaxes(0, 2)
         packed = packed.reshape(bag_count * group_count, *packed.shape[3:])
-    attended = attend(seq_lengths, exchange(packed), bag_count, group_count)
-    returned = exchange(attended).reshape(*slots, *attended.shape[1:])
-    if direct:
-        result = unpack_spans(span_route, returned)
-    else:
+        attended = attend(seq_lengths, exchange(packed), bag_count, group_count)
+        returned = exchange(attended).reshape(*slots, *attended.shape[1:])
         result = returned.swapaxes(0, 2).reshape(bag_count, group_count, *attended.shape[1:])[route_mine]
     return result.transpose(0, 3, 1, 2, 4).reshape(tok_dev, row_width)
 

time: 66.7 us -> 64.3 us (0.964)
  blocking collectives: 62.2 us -> 0 us
  waiting for transfers between devices: 0 us -> 36.4 us
  starting transfers between devices: 0 us -> 20.7 us
  Pallas kernels: 3.55 us -> 5.78 us
    all_to_all x2 -> x0, blocking collectives: 62.2 us -> none  [exchange(): lax.all_to_all(rows, AXES, split_axis=0, concat_axis=0, tiled=True, axis_...]
    ppermute x0 -> x10, waiting for transfers between devices: none -> 18.7 us  [swap(): lax.ppermute(rows, axis, [(index, index ^ distance) for index in range(la...]
    all_to_all x0 -> x2, waiting for transfers between devices: none -> 17.7 us  [exchange(): lax.all_to_all(rows, AXES, split_axis=0, concat_axis=0, tiled=True, axis_...]
    ppermute x0 -> x10, starting transfers between devices: none -> 11.7 us  [swap(): lax.ppermute(rows, axis, [(index, index ^ distance) for index in range(la...]
    all_to_all x0 -> x2, starting transfers between devices: none -> 9.01 us  [exchange(): lax.all_to_all(rows, AXES, split_axis=0, concat_axis=0, tiled=True, axis_...]
    pallas_call x2 -> x4, Pallas kernels: 2.34 us -> 3.97 us  [the longest x1 2.47 us: pack_spans(): pl.pallas_call(kernel, out_shape=[jax.ShapeDtypeStruct(shape, dtype)] + [...]
  transfers between devices with their start and end apart: 0 -> 12, of which waited for: 0 -> 10; matrix products, arithmetic and copies ran while one was open for 0% -> 1% of each run, Pallas kernels for 0% -> 4%
where the time goes in v5:
time: 64.3 us; the launch traced here: 63.4 us
  waiting for transfers between devices  36.4 us (57%)
  starting transfers between devices  20.7 us (32%)
  Pallas kernels  5.78 us (9%)
    ppermute x10, waiting for transfers between devices, swap(): lax.ppermute(rows, axis, [(index, index ^ distance) for index in range(la...  18.7 us
    all_to_all x2, waiting for transfers between devices, exchange(): lax.all_to_all(rows, AXES, split_axis=0, concat_axis=0, tiled=True, axis_...  17.7 us
    ppermute x10, starting transfers between devices, swap(): lax.ppermute(rows, axis, [(index, index ^ distance) for index in range(la...  11.7 us
    all_to_all x2, starting transfers between devices, exchange(): lax.all_to_all(rows, AXES, split_axis=0, concat_axis=0, tiled=True, axis_...  9.01 us
    pallas_call x1, Pallas kernels, pack_spans(): pl.pallas_call(kernel, out_shape=[jax.ShapeDtypeStruct(shape, dtype)] + [...  2.47 us
    pallas_call x1, Pallas kernels, attend(): pl.pallas_call(kernel, out_shape=jax.ShapeDtypeStruct((slots, heads_here,...  1.81 us
  transfers between devices with their start and end apart: 12, of which 10 were waited for; matrix products, arithmetic and copies ran while one was open for 1% of the time, Pallas kernels for 4%

profile of v5, /device:TPU:0, one launch (start us, length us, event | category | flops | bytes accessed | tf_op | source)
XLA Modules:
  0.0 63.4 jit_solution(15702448153962696058)
XLA Ops:
  0.0 2.5 %pack_spans.1 = (bf16[4,2,4,3,7,8,128]{6,5,4,3,2,1,0:T(8,128)(2,1)}, bf16[32,8,128]{2,1,0:T(8,128)(2,1)S(1)}, bf16[65,8,128]{2,1,0:T(8,128)(2,1)S(1)}) custom-call(s32[1,4,8]{2,1,0:T(4,128)} %route_ref.1, s32[1,4]{1,0:T(1,128)} %length_ref.1, bf16[8,4,8,8,128]{4,3,2,1,0:T(8,128)(2,1)} %bitcast.77, bf16[8,4,8,8,128]{4,3,2,1,0:T(8,128)(2,1)} %bitcast.78, ...), custom_call_target="tpu_custom_call" | custom-call | tf_op jit(solution)/shard_map/pack_spans/pallas_call | solution.py:69
  2.5 4.1 %collective-permute-start = (bf16[65,8,128]{2,1,0:T(8,128)(2,1)S(1)}, bf16[65,8,128]{2,1,0:T(8,128)(2,1)S(1)}, u32[]{:S(2)}, u32[]{:S(2)}) collective-permute-start(bf16[65,8,128]{2,1,0:T(8,128)(2,1)S(1)} %get-tuple-element.12.near_ref), channel_id=1, source_target_pairs={{0,16},{4,20},{8,24},{12,28},{16,0},{20,4},{24,8},{28,12},{1,17},{... | collective-permute-start | bytes 399368 | tf_op jit(solution)/shard_map/ppermute | solution.py:123
  6.6 3.8 %all-to-all-start = ((bf16[32,3,7,8,128]{4,3,2,1,0:T(8,128)(2,1)}), bf16[32,3,7,8,128]{4,3,2,1,0:T(8,128)(2,1)S(1)}, u32[]{:S(2)}, u32[]{:S(2)}) async-start(bf16[32,3,7,8,128]{4,3,2,1,0:T(8,128)(2,1)} %bitcast.6), calls=%async_computation | async-start | bytes 2752512 | tf_op jit(solution)/shard_map/all_to_all | solution.py:305
  10.4 2.6 %collective-permute-done.across_ref = bf16[65,8,128]{2,1,0:T(8,128)(2,1)S(1)} collective-permute-done((bf16[65,8,128]{2,1,0:T(8,128)(2,1)S(1)}, bf16[65,8,128]{2,1,0:T(8,128)(2,1)S(1)}, u32[]{:S(2)}, u32[]{:S(2)}) %collective-permute-start) | collective-permute-done | bytes 133152 | tf_op jit(solution)/shard_map/ppermute | solution.py:123
  13.1 0.1 collective-permute-start.1
  13.1 1.4 %collective-permute-done.1 = bf16[5,4,4,1,8,128]{5,4,2,0,1,3:T(8,128)(2,1)S(1)} collective-permute-done((bf16[5,4,4,1,8,128]{5,4,2,0,1,3:T(8,128)(2,1)S(1)}, bf16[5,4,4,1,8,128]{5,4,2,0,1,3:T(8,128)(2,1)S(1)}, u32[]{:S(2)}, u32[]{:S(2)}) %collective-permute-start.1) | collective-permute-done | bytes 163872 | tf_op jit(solution)/shard_map/ppermute | solution.py:123
  14.6 0.0 copy-start.1
  14.6 2.6 %collective-permute-start.4 = (bf16[5,2,4,1,8,128]{5,4,2,1,0,3:T(8,128)(2,1)S(1)}, bf16[5,2,4,1,8,128]{5,4,2,1,0,3:T(8,128)(2,1)S(1)}, u32[]{:S(2)}, u32[]{:S(2)}) collective-permute-start(bf16[5,2,4,1,8,128]{5,4,2,1,0,3:T(8,128)(2,1)S(1)} %get-tuple-element.20), channel_id=1, source_target_pairs={{0,3},{1,2},{2,1},{3,0},{4,7},{5,6},{6,5},{7,4},{8,11},{9,10},{10,... | collective-permute-start | bytes 245768 | tf_op jit(solution)/shard_map/ppermute | solution.py:123
  17.2 0.5 collective-permute-start.3
  17.7 0.5 collective-permute-start.2
  18.2 8.3 %collective-permute-done.4 = bf16[5,2,4,1,8,128]{5,4,2,1,0,3:T(8,128)(2,1)S(1)} collective-permute-done((bf16[5,2,4,1,8,128]{5,4,2,1,0,3:T(8,128)(2,1)S(1)}, bf16[5,2,4,1,8,128]{5,4,2,1,0,3:T(8,128)(2,1)S(1)}, u32[]{:S(2)}, u32[]{:S(2)}) %collective-permute-start.4) | collective-permute-done | bytes 81952 | tf_op jit(solution)/shard_map/ppermute | solution.py:123
  26.5 1.9 %collective-permute-done.3 = bf16[5,2,4,1,8,128]{5,4,2,1,0,3:T(8,128)(2,1)S(1)} collective-permute-done((bf16[5,2,4,1,8,128]{5,4,2,1,0,3:T(8,128)(2,1)S(1)}, bf16[5,2,4,1,8,128]{5,4,2,1,0,3:T(8,128)(2,1)S(1)}, u32[]{:S(2)}, u32[]{:S(2)}) %collective-permute-start.3) | collective-permute-done | bytes 81952 | tf_op jit(solution)/shard_map/ppermute | solution.py:123
  28.4 0.0 collective-permute-done.2
  28.4 0.1 pad_maximum_fusion.1
  28.5 0.1 collective-permute-start.5
  28.6 13.7 %all-to-all-done.packed_ref = bf16[32,3,7,8,128]{4,3,2,1,0:T(8,128)(2,1)S(1)} async-done(((bf16[32,3,7,8,128]{4,3,2,1,0:T(8,128)(2,1)}), bf16[32,3,7,8,128]{4,3,2,1,0:T(8,128)(2,1)S(1)}, u32[]{:S(2)}, u32[]{:S(2)}) %all-to-all-start) | async-done | bytes 1376288 | tf_op jit(solution)/shard_map/all_to_all | solution.py:305
  42.3 1.8 %attend_bag.1 = bf16[32,7,8,128]{3,2,1,0:T(8,128)(2,1)} custom-call(s32[1,4]{1,0:T(1,128)S(1)} %copy-done.1, bf16[32,3,7,8,128]{4,3,2,1,0:T(8,128)(2,1)S(1)} %all-to-all-done.packed_ref, bf16[5,4,2,4,1,8,128]{6,5,4,3,2,1,0:T(8,128)(2,1)S(1)} %get-tuple-element.18.refs_0_), custom_call_target="tpu_custom_call" | custom-call | tf_op jit(solution)/shard_map/attend_bag/pallas_call | solution.py:287
  44.1 5.2 %all-to-all-start.1 = ((bf16[32,7,8,128]{3,2,1,0:T(8,128)(2,1)}), bf16[32,7,8,128]{3,2,1,0:T(8,128)(2,1)S(1)}, u32[]{:S(2)}, u32[]{:S(2)}) async-start(bf16[32,7,8,128]{3,2,1,0:T(8,128)(2,1)} %attend_bag.1), calls=%async_computation.1 | async-start | bytes 917504 | tf_op jit(solution)/shard_map/all_to_all | solution.py:305
  49.3 0.0 copy-start
  49.3 0.0 collective-permute-done.5
  49.4 0.1 pad_maximum_fusion.pair_ref
  49.4 0.5 attend_plane.1
  50.0 0.3 collective-permute-start.6
  50.3 1.0 %collective-permute-done.6 = bf16[4,4,1,8,128]{4,3,1,0,2:T(8,128)(2,1)S(1)} collective-permute-done((bf16[4,4,1,8,128]{4,3,1,0,2:T(8,128)(2,1)S(1)}, bf16[4,4,1,8,128]{4,3,1,0,2:T(8,128)(2,1)S(1)}, u32[]{:S(2)}, u32[]{:S(2)}) %collective-permute-start.6) | collective-permute-done | bytes 32800 | tf_op jit(solution)/shard_map/ppermute | solution.py:123
  51.2 2.7 %collective-permute-start.9 = (bf16[2,4,1,8,128]{4,3,2,1,0:T(8,128)(2,1)S(1)}, bf16[2,4,1,8,128]{4,3,2,1,0:T(8,128)(2,1)S(1)}, u32[]{:S(2)}, u32[]{:S(2)}) collective-permute-start(bf16[2,4,1,8,128]{4,3,2,1,0:T(8,128)(2,1)S(1)} %get-tuple-element.29), channel_id=1, source_target_pairs={{0,3},{1,2},{2,1},{3,0},{4,7},{5,6},{6,5},{7,4},{8,11},{9,10},{10,... | collective-permute-start | bytes 49160 | tf_op jit(solution)/shard_map/ppermute | solution.py:123
  54.0 0.6 collective-permute-start.7
  54.5 0.3 collective-permute-start.8
  54.8 1.4 %collective-permute-done.9.refs_3_ = bf16[2,4,1,8,128]{4,3,2,1,0:T(8,128)(2,1)S(1)} collective-permute-done((bf16[2,4,1,8,128]{4,3,2,1,0:T(8,128)(2,1)S(1)}, bf16[2,4,1,8,128]{4,3,2,1,0:T(8,128)(2,1)S(1)}, u32[]{:S(2)}, u32[]{:S(2)}) %collective-permute-start.9) | collective-permute-done | bytes 16416 | tf_op jit(solution)/shard_map/ppermute | solution.py:123
  56.2 1.7 %collective-permute-done.7 = bf16[2,4,1,8,128]{4,3,1,0,2:T(8,128)(2,1)S(1)} collective-permute-done((bf16[2,4,1,8,128]{4,3,1,0,2:T(8,128)(2,1)S(1)}, bf16[2,4,1,8,128]{4,3,1,0,2:T(8,128)(2,1)S(1)}, u32[]{:S(2)}, u32[]{:S(2)}) %collective-permute-start.7) | collective-permute-done | bytes 16416 | tf_op jit(solution)/shard_map/ppermute | solution.py:123
  57.9 0.5 collective-permute-done.8
  58.4 4.0 %all-to-all-done.1 = bf16[32,7,8,128]{3,2,1,0:T(8,128)(2,1)S(1)} async-done(((bf16[32,7,8,128]{3,2,1,0:T(8,128)(2,1)}), bf16[32,7,8,128]{3,2,1,0:T(8,128)(2,1)S(1)}, u32[]{:S(2)}, u32[]{:S(2)}) %all-to-all-start.1) | async-done | bytes 458784 | tf_op jit(solution)/shard_map/all_to_all | solution.py:305
  62.4 1.0 %unpack_spans.1 = bf16[8,4,8,8,128]{4,3,2,1,0:T(8,128)(2,1)} custom-call(s32[1,4,8]{2,1,0:T(4,128)S(1)} %copy-done, bf16[4,2,4,7,8,128]{5,4,3,2,1,0:T(8,128)(2,1)S(1)} %bitcast.71, bf16[2,4,1,8,128]{4,3,2,1,0:T(8,128)(2,1)S(1)} %get-tuple-element.30.refs_0_, bf16[2,4,1,8,128]{4,3,2,1,0:T(8,128)(2,1)S(1)} %bitcast.74, ...), custom_call_target="tpu_custom_call" | custom-call | tf_op jit(solution)/shard_map/unpack_spans/pallas_call | solution.py:111
  (18 shorter events, 0.2 us)
Async XLA Ops:
  2.5 10.5 %collective-permute-start = (bf16[65,8,128]{2,1,0:T(8,128)(2,1)S(1)}, bf16[65,8,128]{2,1,0:T(8,128)(2,1)S(1)}, u32[]{:S(2)}, u32[]{:S(2)}) collective-permute-start(bf16[65,8,128]{2,1,0:T(8,128)(2,1)S(1)} %get-tuple-element.12.near_ref), channel_id=1, source_target_pairs={{0,16},{4,20},{8,24},{12,28},{16,0},{20,4},{24,8},{28,12},{1,17},{... | collective-permute-start | bytes 399368 | tf_op jit(solution)/shard_map/ppermute | solution.py:123
  6.6 35.7 %all-to-all-start = ((bf16[32,3,7,8,128]{4,3,2,1,0:T(8,128)(2,1)}), bf16[32,3,7,8,128]{4,3,2,1,0:T(8,128)(2,1)S(1)}, u32[]{:S(2)}, u32[]{:S(2)}) async-start(bf16[32,3,7,8,128]{4,3,2,1,0:T(8,128)(2,1)} %bitcast.6), calls=%async_computation | async-start | bytes 2752512 | tf_op jit(solution)/shard_map/all_to_all | solution.py:305
  13.1 1.5 %collective-permute-start.1 = (bf16[5,4,4,1,8,128]{5,4,2,0,1,3:T(8,128)(2,1)S(1)}, bf16[5,4,4,1,8,128]{5,4,2,0,1,3:T(8,128)(2,1)S(1)}, u32[]{:S(2)}, u32[]{:S(2)}) collective-permute-start(bf16[5,4,4,1,8,128]{5,4,2,0,1,3:T(8,128)(2,1)S(1)} %bitcast.83), channel_id=1, source_target_pairs={{0,4},{4,0},{8,12},{12,8},{16,20},{20,16},{24,28},{28,24},{1,5},{5... | collective-permute-start | bytes 491528 | tf_op jit(solution)/shard_map/ppermute | solution.py:123
  14.6 27.7 %copy-start.1 = (s32[1,4]{1,0:T(1,128)S(1)}, s32[1,4]{1,0:T(1,128)}, u32[]{:S(2)}) copy-start(s32[1,4]{1,0:T(1,128)} %length_ref.1) | copy-start | bytes 52
  14.6 11.9 %collective-permute-start.4 = (bf16[5,2,4,1,8,128]{5,4,2,1,0,3:T(8,128)(2,1)S(1)}, bf16[5,2,4,1,8,128]{5,4,2,1,0,3:T(8,128)(2,1)S(1)}, u32[]{:S(2)}, u32[]{:S(2)}) collective-permute-start(bf16[5,2,4,1,8,128]{5,4,2,1,0,3:T(8,128)(2,1)S(1)} %get-tuple-element.20), channel_id=1, source_target_pairs={{0,3},{1,2},{2,1},{3,0},{4,7},{5,6},{6,5},{7,4},{8,11},{9,10},{10,... | collective-permute-start | bytes 245768 | tf_op jit(solution)/shard_map/ppermute | solution.py:123
  17.2 11.2 %collective-permute-start.3 = (bf16[5,2,4,1,8,128]{5,4,2,1,0,3:T(8,128)(2,1)S(1)}, bf16[5,2,4,1,8,128]{5,4,2,1,0,3:T(8,128)(2,1)S(1)}, u32[]{:S(2)}, u32[]{:S(2)}) collective-permute-start(bf16[5,2,4,1,8,128]{5,4,2,1,0,3:T(8,128)(2,1)S(1)} %get-tuple-element.21), channel_id=1, source_target_pairs={{0,2},{1,3},{2,0},{3,1},{4,6},{5,7},{6,4},{7,5},{8,10},{9,11},{10,... | collective-permute-start | bytes 245768 | tf_op jit(solution)/shard_map/ppermute | solution.py:123
  17.7 10.7 %collective-permute-start.2 = (bf16[5,2,4,1,8,128]{5,4,2,1,0,3:T(8,128)(2,1)S(1)}, bf16[5,2,4,1,8,128]{5,4,2,1,0,3:T(8,128)(2,1)S(1)}, u32[]{:S(2)}, u32[]{:S(2)}) collective-permute-start(bf16[5,2,4,1,8,128]{5,4,2,1,0,3:T(8,128)(2,1)S(1)} %get-tuple-element.22), channel_id=1, source_target_pairs={{0,1},{1,0},{2,3},{3,2},{4,5},{5,4},{6,7},{7,6},{8,9},{9,8},{10,11... | collective-permute-start | bytes 245768 | tf_op jit(solution)/shard_map/ppermute | solution.py:123
  28.5 20.8 %collective-permute-start.5 = (bf16[130,8,128]{2,1,0:T(8,128)(2,1)S(1)}, bf16[130,8,128]{2,1,0:T(8,128)(2,1)S(1)}, u32[]{:S(2)}, u32[]{:S(2)}) collective-permute-start(bf16[130,8,128]{2,1,0:T(8,128)(2,1)S(1)} %pad_maximum_fusion.2), channel_id=1, source_target_pairs={{0,8},{4,12},{8,0},{12,4},{16,24},{20,28},{24,16},{28,20},{1,9},{5... | collective-permute-start | bytes 798728 | tf_op jit(solution)/shard_map/ppermute | solution.py:123
  44.1 18.3 %all-to-all-start.1 = ((bf16[32,7,8,128]{3,2,1,0:T(8,128)(2,1)}), bf16[32,7,8,128]{3,2,1,0:T(8,128)(2,1)S(1)}, u32[]{:S(2)}, u32[]{:S(2)}) async-start(bf16[32,7,8,128]{3,2,1,0:T(8,128)(2,1)} %attend_bag.1), calls=%async_computation.1 | async-start | bytes 917504 | tf_op jit(solution)/shard_map/all_to_all | solution.py:305
  49.3 13.1 %copy-start = (s32[1,4,8]{2,1,0:T(4,128)S(1)}, s32[1,4,8]{2,1,0:T(4,128)}, u32[]{:S(2)}) copy-start(s32[1,4,8]{2,1,0:T(4,128)} %route_ref.1) | copy-start | bytes 388
  50.0 1.3 %collective-permute-start.6 = (bf16[4,4,1,8,128]{4,3,1,0,2:T(8,128)(2,1)S(1)}, bf16[4,4,1,8,128]{4,3,1,0,2:T(8,128)(2,1)S(1)}, u32[]{:S(2)}, u32[]{:S(2)}) collective-permute-start(bf16[4,4,1,8,128]{4,3,1,0,2:T(8,128)(2,1)S(1)} %slice_bitcast_fusion.7), channel_id=1, source_target_pairs={{0,4},{4,0},{8,12},{12,8},{16,20},{20,16},{24,28},{28,24},{1,5},{5... | collective-permute-start | bytes 98312 | tf_op jit(solution)/shard_map/ppermute | solution.py:123
  51.2 4.9 %collective-permute-start.9 = (bf16[2,4,1,8,128]{4,3,2,1,0:T(8,128)(2,1)S(1)}, bf16[2,4,1,8,128]{4,3,2,1,0:T(8,128)(2,1)S(1)}, u32[]{:S(2)}, u32[]{:S(2)}) collective-permute-start(bf16[2,4,1,8,128]{4,3,2,1,0:T(8,128)(2,1)S(1)} %get-tuple-element.29), channel_id=1, source_target_pairs={{0,3},{1,2},{2,1},{3,0},{4,7},{5,6},{6,5},{7,4},{8,11},{9,10},{10,... | collective-permute-start | bytes 49160 | tf_op jit(solution)/shard_map/ppermute | solution.py:123
  54.0 3.9 %collective-permute-start.7 = (bf16[2,4,1,8,128]{4,3,1,0,2:T(8,128)(2,1)S(1)}, bf16[2,4,1,8,128]{4,3,1,0,2:T(8,128)(2,1)S(1)}, u32[]{:S(2)}, u32[]{:S(2)}) collective-permute-start(bf16[2,4,1,8,128]{4,3,1,0,2:T(8,128)(2,1)S(1)} %get-tuple-element.31), channel_id=1, source_target_pairs={{0,1},{1,0},{2,3},{3,2},{4,5},{5,4},{6,7},{7,6},{8,9},{9,8},{10,11... | collective-permute-start | bytes 49160 | tf_op jit(solution)/shard_map/ppermute | solution.py:123
  54.5 3.8 %collective-permute-start.8 = (bf16[2,4,1,8,128]{4,3,1,0,2:T(8,128)(2,1)S(1)}, bf16[2,4,1,8,128]{4,3,1,0,2:T(8,128)(2,1)S(1)}, u32[]{:S(2)}, u32[]{:S(2)}) collective-permute-start(bf16[2,4,1,8,128]{4,3,1,0,2:T(8,128)(2,1)S(1)} %get-tuple-element.32), channel_id=1, source_target_pairs={{0,2},{1,3},{2,0},{3,1},{4,6},{5,7},{6,4},{7,5},{8,10},{9,11},{10,... | collective-permute-start | bytes 49160 | tf_op jit(solution)/shard_map/ppermute | solution.py:123

commit v6 on v5

--- a/solution.py
+++ b/solution.py
@@ -12,6 +12,7 @@
 MARGIN = 1 << 20
 SPREAD = 1
 BASE = 128
+PIECES = 4
 CORES = 2
 AXES = ("bag", "ulysses")
 
@@ -31,9 +32,9 @@
         copies = [pltpu.make_async_copy(sources[k], stage.at[k], sem.at[k]) for k in range(kinds)]
         route_copy = pltpu.make_async_copy(route_hbm, route_ref, sem.at[kinds])
         route_copy.start()
-        for copy in copies:
+        for copy in copies[1:] + copies[:1]:
             copy.start()
-        lengths_copy = pltpu.make_async_copy(lengths_hbm, lengths, sem.at[kinds + 2])
+        lengths_copy = pltpu.make_async_copy(lengths_hbm, lengths, sem.at[kinds + 1])
         lengths_copy.start()
         route_copy.wait()
         lengths_copy.wait()
@@ -43,39 +44,37 @@
             length = lengths[:, entry : entry + 1]
             block = jnp.where(row == 2 * entry, length // BASE, jnp.where(row == 2 * entry + 1, length % BASE, block))
         aside_kv[(kinds - 1) * each] = block.astype(jnp.float32).astype(aside_kv.dtype)
-        for kind in range(kinds):
+        places = []
+        for span in range(bag_count):
+            to = route_ref[0, group, span]
+            chip, core = lax.div(to, CORES), lax.rem(to, CORES)
+            first = ((core ^ lax.rem(bag, CORES)) * chips + chip) * spread
+            places.append((core, chip, [(other ^ group) * (CORES * chips * spread) + first for other in range(group_count)]))
+        for kind in (*range(1, kinds), 0):
             copies[kind].wait()
-            for span in range(bag_count):
-                to = route_ref[0, group, span]
-                pltpu.make_async_copy(
-                    stage.at[kind, span, :, pl.ds(0, direct_heads)],
-                    target.at[:, to % CORES, to // CORES, kind],
-                    sem.at[kinds + 1],
-                ).start()
+            for span, (core, chip, blocks) in enumerate(places):
+                target[:, core, chip, kind] = stage[kind, span, :, :direct_heads]
                 for other in range(group_count):
-                    block = ((other ^ group) * CORES + (to % CORES ^ bag % CORES)) * chips + to // CORES
-                    block = block * spread
                     for head in range(spread):
                         rows = stage[kind, span, other, direct_heads + head]
                         if kind == 0:
-                            aside_q[block + head] = rows
+                            aside_q[blocks[other] + head] = rows
                         else:
-                            aside_kv[(kind - 1) * each + block + head] = rows
-        pltpu.make_async_copy(target, target, sem.at[kinds + 1]).wait()
+                            aside_kv[(kind - 1) * each + blocks[other] + head] = rows
 
     shape = (group_count, CORES, bag_count // CORES, kinds, direct_heads, span_len, width)
     shape_aside = [(each, span_len, width), ((kinds - 1) * each + 1, span_len, width)]
     dtype = arrays[0].dtype
     packed, aside_q, aside_kv = pl.pallas_call(
         kernel,
-        out_shape=[jax.ShapeDtypeStruct(shape, dtype)] + [pltpu.VMEM(size, dtype) for size in shape_aside],
+        out_shape=[pltpu.VMEM(size, dtype) for size in (shape, *shape_aside)],
         in_specs=[pl.BlockSpec(memory_space=pl.ANY)] * (2 + kinds),
-        out_specs=[pl.BlockSpec(memory_space=pl.ANY)] + [pl.BlockSpec(memory_space=pltpu.VMEM)] * 2,
+        out_specs=[pl.BlockSpec(memory_space=pltpu.VMEM)] * 3,
         scratch_shapes=[
             pltpu.VMEM((kinds, *arrays[0].shape), dtype),
             pltpu.VMEM(seq_lengths.shape, seq_lengths.dtype),
             pltpu.SMEM(span_route.shape, span_route.dtype),
-            pltpu.SemaphoreType.DMA((kinds + 3,)),
+            pltpu.SemaphoreType.DMA((kinds + 2,)),
         ],
         compiler_params=pltpu.CompilerParams(vmem_limit_bytes=2 * payload + MARGIN),
         name="pack_spans",
@@ -130,6 +129,28 @@
 
 def swap_groups(rows):
     return [rows[0]] + [swap(rows[distance], "ulysses", distance) for distance in range(1, rows.shape[0])]
+
+
+def settle(packed):
+    slots = packed.shape[0]
+
+    def kernel(source, target, sem):
+        parts = [pl.ds(k * (slots // PIECES), slots // PIECES) for k in range(PIECES)]
+        copies = [pltpu.make_async_copy(source.at[p], target.at[p], sem.at[k]) for k, p in enumerate(parts)]
+        for copy in copies:
+            copy.start()
+        for copy in copies:
+            copy.wait()
+
+    return pl.pallas_call(
+        kernel,
+        out_shape=jax.ShapeDtypeStruct(packed.shape, packed.dtype),
+        in_specs=[pl.BlockSpec(memory_space=pltpu.VMEM)],
+        out_specs=pl.BlockSpec(memory_space=pl.ANY),
+        scratch_shapes=[pltpu.SemaphoreType.DMA((PIECES,))],
+        compiler_params=pltpu.CompilerParams(vmem_limit_bytes=2 * packed.nbytes + MARGIN),
+        name="settle",
+    )(packed)
 
 
 def merge(queries, near, across):
@@ -320,7 +341,7 @@
     if span_len >= 2 * seq_lengths.shape[1] and span_len % ROW_TILE == 0 and heads_here > SPREAD and bag_count > CORES and powers:
         packed, aside_q, aside_kv = pack_spans(span_route, seq_lengths, arrays, heads_here - SPREAD)
         across = swap(aside_kv, "bag", bag_count // 2)
-        arrived = exchange(packed)
+        arrived = exchange(settle(packed))
         blocks, tables = merge(aside_q, aside_kv, across)
         blocks = blocks.reshape(5, group_count, CORES, -1, SPREAD, span_len, HDIM)
         blocks = jnp.stack(swap_groups(swap_cores(blocks, 2).swapaxes(0, 1)), axis=1)

time: 64.3 us -> 63.8 us (level)
    pallas_call x1 -> x2, Pallas kernels: 2.47 us -> 2.58 us  [the longest x1 1.44 us: pack_spans(): pl.pallas_call(kernel, out_shape=[pltpu.VMEM(size, dtype) for size in (sh...]
  transfers between devices with their start and end apart: 12 -> 12, of which waited for: 10 -> 10; matrix products, arithmetic and copies ran while one was open for 1% -> 1% of each run, Pallas kernels for 4% -> 6%
where the time goes in v6:
time: 63.8 us; the launch traced here: 62.8 us
  waiting for transfers between devices  36.4 us (57%)
  starting transfers between devices  20.1 us (32%)
  Pallas kernels  5.87 us (9%)
    ppermute x10, waiting for transfers between devices, swap(): lax.ppermute(rows, axis, [(index, index ^ distance) for index in range(la...  18.4 us
    all_to_all x2, waiting for transfers between devices, exchange(): lax.all_to_all(rows, AXES, split_axis=0, concat_axis=0, tiled=True, axis_...  18 us
    ppermute x10, starting transfers between devices, swap(): lax.ppermute(rows, axis, [(index, index ^ distance) for index in range(la...  11.7 us
    all_to_all x2, starting transfers between devices, exchange(): lax.all_to_all(rows, AXES, split_axis=0, concat_axis=0, tiled=True, axis_...  8.39 us
    pallas_call x1, Pallas kernels, attend(): pl.pallas_call(kernel, out_shape=jax.ShapeDtypeStruct((slots, heads_here,...  1.8 us
    pallas_call x1, Pallas kernels, pack_spans(): pl.pallas_call(kernel, out_shape=[pltpu.VMEM(size, dtype) for size in (sh...  1.44 us
  transfers between devices with their start and end apart: 12, of which 10 were waited for; matrix products, arithmetic and copies ran while one was open for 1% of the time, Pallas kernels for 6%

profile of v6, /device:TPU:0, one launch (start us, length us, event | category | flops | bytes accessed | tf_op | source)
XLA Modules:
  0.0 62.8 jit_solution(16866631304370169296)
XLA Ops:
  0.0 1.4 %pack_spans.1 = (bf16[4,2,4,3,7,8,128]{6,5,4,3,2,1,0:T(8,128)(2,1)S(1)}, bf16[32,8,128]{2,1,0:T(8,128)(2,1)S(1)}, bf16[65,8,128]{2,1,0:T(8,128)(2,1)S(1)}) custom-call(s32[1,4,8]{2,1,0:T(4,128)} %route_ref.1, s32[1,4]{1,0:T(1,128)} %length_ref.1, bf16[8,4,8,8,128]{4,3,2,1,0:T(8,128)(2,1)} %bitcast.78, bf16[8,4,8,8,128]{4,3,2,1,0:T(8,128)(2,1)} %bitcast.79, ...), custom_call_target="tpu_custom_call" | custom-call | tf_op jit(solution)/shard_map/pack_spans/pallas_call | solution.py:68
  1.5 4.1 %collective-permute-start = (bf16[65,8,128]{2,1,0:T(8,128)(2,1)S(1)}, bf16[65,8,128]{2,1,0:T(8,128)(2,1)S(1)}, u32[]{:S(2)}, u32[]{:S(2)}) collective-permute-start(bf16[65,8,128]{2,1,0:T(8,128)(2,1)S(1)} %get-tuple-element.12.near_ref), channel_id=1, source_target_pairs={{0,16},{4,20},{8,24},{12,28},{16,0},{20,4},{24,8},{28,12},{1,17},{... | collective-permute-start | bytes 399368 | tf_op jit(solution)/shard_map/ppermute | solution.py:122
  5.6 1.1 %settle.1 = bf16[32,3,7,8,128]{4,3,2,1,0:T(8,128)(2,1)} custom-call(bf16[32,3,7,8,128]{4,3,2,1,0:T(8,128)(2,1)S(1)} %bitcast.72), custom_call_target="tpu_custom_call" | custom-call | tf_op jit(solution)/shard_map/settle/pallas_call | solution.py:145
  6.7 3.8 %all-to-all-start = ((bf16[32,3,7,8,128]{4,3,2,1,0:T(8,128)(2,1)}), bf16[32,3,7,8,128]{4,3,2,1,0:T(8,128)(2,1)S(1)}, u32[]{:S(2)}, u32[]{:S(2)}) async-start(bf16[32,3,7,8,128]{4,3,2,1,0:T(8,128)(2,1)} %settle.1), calls=%async_computation | async-start | bytes 2752512 | tf_op jit(solution)/shard_map/all_to_all | solution.py:326
  10.5 1.4 %collective-permute-done.across_ref = bf16[65,8,128]{2,1,0:T(8,128)(2,1)S(1)} collective-permute-done((bf16[65,8,128]{2,1,0:T(8,128)(2,1)S(1)}, bf16[65,8,128]{2,1,0:T(8,128)(2,1)S(1)}, u32[]{:S(2)}, u32[]{:S(2)}) %collective-permute-start) | collective-permute-done | bytes 133152 | tf_op jit(solution)/shard_map/ppermute | solution.py:122
  12.0 0.1 collective-permute-start.1
  12.1 1.4 %collective-permute-done.1 = bf16[5,4,4,1,8,128]{5,4,2,0,1,3:T(8,128)(2,1)S(1)} collective-permute-done((bf16[5,4,4,1,8,128]{5,4,2,0,1,3:T(8,128)(2,1)S(1)}, bf16[5,4,4,1,8,128]{5,4,2,0,1,3:T(8,128)(2,1)S(1)}, u32[]{:S(2)}, u32[]{:S(2)}) %collective-permute-start.1) | collective-permute-done | bytes 163872 | tf_op jit(solution)/shard_map/ppermute | solution.py:122
  13.5 0.0 copy-start.1
  13.6 2.6 %collective-permute-start.4 = (bf16[5,2,4,1,8,128]{5,4,2,1,0,3:T(8,128)(2,1)S(1)}, bf16[5,2,4,1,8,128]{5,4,2,1,0,3:T(8,128)(2,1)S(1)}, u32[]{:S(2)}, u32[]{:S(2)}) collective-permute-start(bf16[5,2,4,1,8,128]{5,4,2,1,0,3:T(8,128)(2,1)S(1)} %get-tuple-element.20), channel_id=1, source_target_pairs={{0,3},{1,2},{2,1},{3,0},{4,7},{5,6},{6,5},{7,4},{8,11},{9,10},{10,... | collective-permute-start | bytes 245768 | tf_op jit(solution)/shard_map/ppermute | solution.py:122
  16.1 0.5 collective-permute-start.3
  16.6 0.5 collective-permute-start.2
  17.1 9.5 %collective-permute-done.4 = bf16[5,2,4,1,8,128]{5,4,2,1,0,3:T(8,128)(2,1)S(1)} collective-permute-done((bf16[5,2,4,1,8,128]{5,4,2,1,0,3:T(8,128)(2,1)S(1)}, bf16[5,2,4,1,8,128]{5,4,2,1,0,3:T(8,128)(2,1)S(1)}, u32[]{:S(2)}, u32[]{:S(2)}) %collective-permute-start.4) | collective-permute-done | bytes 81952 | tf_op jit(solution)/shard_map/ppermute | solution.py:122
  26.6 1.6 %collective-permute-done.3 = bf16[5,2,4,1,8,128]{5,4,2,1,0,3:T(8,128)(2,1)S(1)} collective-permute-done((bf16[5,2,4,1,8,128]{5,4,2,1,0,3:T(8,128)(2,1)S(1)}, bf16[5,2,4,1,8,128]{5,4,2,1,0,3:T(8,128)(2,1)S(1)}, u32[]{:S(2)}, u32[]{:S(2)}) %collective-permute-start.3) | collective-permute-done | bytes 81952 | tf_op jit(solution)/shard_map/ppermute | solution.py:122
  28.2 0.0 collective-permute-done.2
  28.2 0.1 pad_maximum_fusion.1
  28.3 0.1 collective-permute-start.5
  28.4 14.0 %all-to-all-done.packed_ref = bf16[32,3,7,8,128]{4,3,2,1,0:T(8,128)(2,1)S(1)} async-done(((bf16[32,3,7,8,128]{4,3,2,1,0:T(8,128)(2,1)}), bf16[32,3,7,8,128]{4,3,2,1,0:T(8,128)(2,1)S(1)}, u32[]{:S(2)}, u32[]{:S(2)}) %all-to-all-start) | async-done | bytes 1376288 | tf_op jit(solution)/shard_map/all_to_all | solution.py:326
  42.4 1.8 %attend_bag.1 = bf16[32,7,8,128]{3,2,1,0:T(8,128)(2,1)} custom-call(s32[1,4]{1,0:T(1,128)S(1)} %copy-done.1, bf16[32,3,7,8,128]{4,3,2,1,0:T(8,128)(2,1)S(1)} %all-to-all-done.packed_ref, bf16[5,4,2,4,1,8,128]{6,5,4,3,2,1,0:T(8,128)(2,1)S(1)} %get-tuple-element.18.refs_0_), custom_call_target="tpu_custom_call" | custom-call | tf_op jit(solution)/shard_map/attend_bag/pallas_call | solution.py:308
  44.2 4.6 %all-to-all-start.1 = ((bf16[32,7,8,128]{3,2,1,0:T(8,128)(2,1)}), bf16[32,7,8,128]{3,2,1,0:T(8,128)(2,1)S(1)}, u32[]{:S(2)}, u32[]{:S(2)}) async-start(bf16[32,7,8,128]{3,2,1,0:T(8,128)(2,1)} %attend_bag.1), calls=%async_computation.1 | async-start | bytes 917504 | tf_op jit(solution)/shard_map/all_to_all | solution.py:326
  48.8 0.0 copy-start
  48.8 0.1 pad_maximum_fusion.pair_ref
  48.9 0.5 attend_plane.1
  49.4 0.3 collective-permute-start.6
  49.8 1.0 %collective-permute-done.6 = bf16[4,4,1,8,128]{4,3,1,0,2:T(8,128)(2,1)S(1)} collective-permute-done((bf16[4,4,1,8,128]{4,3,1,0,2:T(8,128)(2,1)S(1)}, bf16[4,4,1,8,128]{4,3,1,0,2:T(8,128)(2,1)S(1)}, u32[]{:S(2)}, u32[]{:S(2)}) %collective-permute-start.6) | collective-permute-done | bytes 32800 | tf_op jit(solution)/shard_map/ppermute | solution.py:122
  50.7 2.7 %collective-permute-start.9 = (bf16[2,4,1,8,128]{4,3,2,1,0:T(8,128)(2,1)S(1)}, bf16[2,4,1,8,128]{4,3,2,1,0:T(8,128)(2,1)S(1)}, u32[]{:S(2)}, u32[]{:S(2)}) collective-permute-start(bf16[2,4,1,8,128]{4,3,2,1,0:T(8,128)(2,1)S(1)} %get-tuple-element.29), channel_id=1, source_target_pairs={{0,3},{1,2},{2,1},{3,0},{4,7},{5,6},{6,5},{7,4},{8,11},{9,10},{10,... | collective-permute-start | bytes 49160 | tf_op jit(solution)/shard_map/ppermute | solution.py:122
  53.5 0.6 collective-permute-start.7
  54.0 0.3 collective-permute-start.8
  54.3 1.4 %collective-permute-done.9.refs_3_ = bf16[2,4,1,8,128]{4,3,2,1,0:T(8,128)(2,1)S(1)} collective-permute-done((bf16[2,4,1,8,128]{4,3,2,1,0:T(8,128)(2,1)S(1)}, bf16[2,4,1,8,128]{4,3,2,1,0:T(8,128)(2,1)S(1)}, u32[]{:S(2)}, u32[]{:S(2)}) %collective-permute-start.9) | collective-permute-done | bytes 16416 | tf_op jit(solution)/shard_map/ppermute | solution.py:122
  55.6 1.7 %collective-permute-done.7 = bf16[2,4,1,8,128]{4,3,1,0,2:T(8,128)(2,1)S(1)} collective-permute-done((bf16[2,4,1,8,128]{4,3,1,0,2:T(8,128)(2,1)S(1)}, bf16[2,4,1,8,128]{4,3,1,0,2:T(8,128)(2,1)S(1)}, u32[]{:S(2)}, u32[]{:S(2)}) %collective-permute-start.7) | collective-permute-done | bytes 16416 | tf_op jit(solution)/shard_map/ppermute | solution.py:122
  57.4 0.5 collective-permute-done.8
  57.9 4.0 %all-to-all-done.1 = bf16[32,7,8,128]{3,2,1,0:T(8,128)(2,1)S(1)} async-done(((bf16[32,7,8,128]{3,2,1,0:T(8,128)(2,1)}), bf16[32,7,8,128]{3,2,1,0:T(8,128)(2,1)S(1)}, u32[]{:S(2)}, u32[]{:S(2)}) %all-to-all-start.1) | async-done | bytes 458784 | tf_op jit(solution)/shard_map/all_to_all | solution.py:326
  61.9 1.0 %unpack_spans.1 = bf16[8,4,8,8,128]{4,3,2,1,0:T(8,128)(2,1)} custom-call(s32[1,4,8]{2,1,0:T(4,128)S(1)} %copy-done, bf16[4,2,4,7,8,128]{5,4,3,2,1,0:T(8,128)(2,1)S(1)} %bitcast.71, bf16[2,4,1,8,128]{4,3,2,1,0:T(8,128)(2,1)S(1)} %get-tuple-element.30.refs_0_, bf16[2,4,1,8,128]{4,3,2,1,0:T(8,128)(2,1)S(1)} %bitcast.75, ...), custom_call_target="tpu_custom_call" | custom-call | tf_op jit(solution)/shard_map/unpack_spans/pallas_call | solution.py:110
  (19 shorter events, 0.2 us)
Async XLA Ops:
  1.5 10.5 %collective-permute-start = (bf16[65,8,128]{2,1,0:T(8,128)(2,1)S(1)}, bf16[65,8,128]{2,1,0:T(8,128)(2,1)S(1)}, u32[]{:S(2)}, u32[]{:S(2)}) collective-permute-start(bf16[65,8,128]{2,1,0:T(8,128)(2,1)S(1)} %get-tuple-element.12.near_ref), channel_id=1, source_target_pairs={{0,16},{4,20},{8,24},{12,28},{16,0},{20,4},{24,8},{28,12},{1,17},{... | collective-permute-start | bytes 399368 | tf_op jit(solution)/shard_map/ppermute | solution.py:122
  6.7 35.7 %all-to-all-start = ((bf16[32,3,7,8,128]{4,3,2,1,0:T(8,128)(2,1)}), bf16[32,3,7,8,128]{4,3,2,1,0:T(8,128)(2,1)S(1)}, u32[]{:S(2)}, u32[]{:S(2)}) async-start(bf16[32,3,7,8,128]{4,3,2,1,0:T(8,128)(2,1)} %settle.1), calls=%async_computation | async-start | bytes 2752512 | tf_op jit(solution)/shard_map/all_to_all | solution.py:326
  12.0 1.5 %collective-permute-start.1 = (bf16[5,4,4,1,8,128]{5,4,2,0,1,3:T(8,128)(2,1)S(1)}, bf16[5,4,4,1,8,128]{5,4,2,0,1,3:T(8,128)(2,1)S(1)}, u32[]{:S(2)}, u32[]{:S(2)}) collective-permute-start(bf16[5,4,4,1,8,128]{5,4,2,0,1,3:T(8,128)(2,1)S(1)} %bitcast.84), channel_id=1, source_target_pairs={{0,4},{4,0},{8,12},{12,8},{16,20},{20,16},{24,28},{28,24},{1,5},{5... | collective-permute-start | bytes 491528 | tf_op jit(solution)/shard_map/ppermute | solution.py:122
  13.5 28.8 %copy-start.1 = (s32[1,4]{1,0:T(1,128)S(1)}, s32[1,4]{1,0:T(1,128)}, u32[]{:S(2)}) copy-start(s32[1,4]{1,0:T(1,128)} %length_ref.1) | copy-start | bytes 52
  13.6 13.0 %collective-permute-start.4 = (bf16[5,2,4,1,8,128]{5,4,2,1,0,3:T(8,128)(2,1)S(1)}, bf16[5,2,4,1,8,128]{5,4,2,1,0,3:T(8,128)(2,1)S(1)}, u32[]{:S(2)}, u32[]{:S(2)}) collective-permute-start(bf16[5,2,4,1,8,128]{5,4,2,1,0,3:T(8,128)(2,1)S(1)} %get-tuple-element.20), channel_id=1, source_target_pairs={{0,3},{1,2},{2,1},{3,0},{4,7},{5,6},{6,5},{7,4},{8,11},{9,10},{10,... | collective-permute-start | bytes 245768 | tf_op jit(solution)/shard_map/ppermute | solution.py:122
  16.1 12.0 %collective-permute-start.3 = (bf16[5,2,4,1,8,128]{5,4,2,1,0,3:T(8,128)(2,1)S(1)}, bf16[5,2,4,1,8,128]{5,4,2,1,0,3:T(8,128)(2,1)S(1)}, u32[]{:S(2)}, u32[]{:S(2)}) collective-permute-start(bf16[5,2,4,1,8,128]{5,4,2,1,0,3:T(8,128)(2,1)S(1)} %get-tuple-element.21), channel_id=1, source_target_pairs={{0,2},{1,3},{2,0},{3,1},{4,6},{5,7},{6,4},{7,5},{8,10},{9,11},{10,... | collective-permute-start | bytes 245768 | tf_op jit(solution)/shard_map/ppermute | solution.py:122
  16.6 11.5 %collective-permute-start.2 = (bf16[5,2,4,1,8,128]{5,4,2,1,0,3:T(8,128)(2,1)S(1)}, bf16[5,2,4,1,8,128]{5,4,2,1,0,3:T(8,128)(2,1)S(1)}, u32[]{:S(2)}, u32[]{:S(2)}) collective-permute-start(bf16[5,2,4,1,8,128]{5,4,2,1,0,3:T(8,128)(2,1)S(1)} %get-tuple-element.22), channel_id=1, source_target_pairs={{0,1},{1,0},{2,3},{3,2},{4,5},{5,4},{6,7},{7,6},{8,9},{9,8},{10,11... | collective-permute-start | bytes 245768 | tf_op jit(solution)/shard_map/ppermute | solution.py:122
  28.3 20.5 %collective-permute-start.5 = (bf16[130,8,128]{2,1,0:T(8,128)(2,1)S(1)}, bf16[130,8,128]{2,1,0:T(8,128)(2,1)S(1)}, u32[]{:S(2)}, u32[]{:S(2)}) collective-permute-start(bf16[130,8,128]{2,1,0:T(8,128)(2,1)S(1)} %pad_maximum_fusion.2), channel_id=1, source_target_pairs={{0,8},{4,12},{8,0},{12,4},{16,24},{20,28},{24,16},{28,20},{1,9},{5... | collective-permute-start | bytes 798728 | tf_op jit(solution)/shard_map/ppermute | solution.py:122
  44.2 17.7 %all-to-all-start.1 = ((bf16[32,7,8,128]{3,2,1,0:T(8,128)(2,1)}), bf16[32,7,8,128]{3,2,1,0:T(8,128)(2,1)S(1)}, u32[]{:S(2)}, u32[]{:S(2)}) async-start(bf16[32,7,8,128]{3,2,1,0:T(8,128)(2,1)} %attend_bag.1), calls=%async_computation.1 | async-start | bytes 917504 | tf_op jit(solution)/shard_map/all_to_all | solution.py:326
  48.8 13.1 %copy-start = (s32[1,4,8]{2,1,0:T(4,128)S(1)}, s32[1,4,8]{2,1,0:T(4,128)}, u32[]{:S(2)}) copy-start(s32[1,4,8]{2,1,0:T(4,128)} %route_ref.1) | copy-start | bytes 388
  49.4 1.3 %collective-permute-start.6 = (bf16[4,4,1,8,128]{4,3,1,0,2:T(8,128)(2,1)S(1)}, bf16[4,4,1,8,128]{4,3,1,0,2:T(8,128)(2,1)S(1)}, u32[]{:S(2)}, u32[]{:S(2)}) collective-permute-start(bf16[4,4,1,8,128]{4,3,1,0,2:T(8,128)(2,1)S(1)} %slice_bitcast_fusion.7), channel_id=1, source_target_pairs={{0,4},{4,0},{8,12},{12,8},{16,20},{20,16},{24,28},{28,24},{1,5},{5... | collective-permute-start | bytes 98312 | tf_op jit(solution)/shard_map/ppermute | solution.py:122
  50.7 4.9 %collective-permute-start.9 = (bf16[2,4,1,8,128]{4,3,2,1,0:T(8,128)(2,1)S(1)}, bf16[2,4,1,8,128]{4,3,2,1,0:T(8,128)(2,1)S(1)}, u32[]{:S(2)}, u32[]{:S(2)}) collective-permute-start(bf16[2,4,1,8,128]{4,3,2,1,0:T(8,128)(2,1)S(1)} %get-tuple-element.29), channel_id=1, source_target_pairs={{0,3},{1,2},{2,1},{3,0},{4,7},{5,6},{6,5},{7,4},{8,11},{9,10},{10,... | collective-permute-start | bytes 49160 | tf_op jit(solution)/shard_map/ppermute | solution.py:122
  53.5 3.9 %collective-permute-start.7 = (bf16[2,4,1,8,128]{4,3,1,0,2:T(8,128)(2,1)S(1)}, bf16[2,4,1,8,128]{4,3,1,0,2:T(8,128)(2,1)S(1)}, u32[]{:S(2)}, u32[]{:S(2)}) collective-permute-start(bf16[2,4,1,8,128]{4,3,1,0,2:T(8,128)(2,1)S(1)} %get-tuple-element.31), channel_id=1, source_target_pairs={{0,1},{1,0},{2,3},{3,2},{4,5},{5,4},{6,7},{7,6},{8,9},{9,8},{10,11... | collective-permute-start | bytes 49160 | tf_op jit(solution)/shard_map/ppermute | solution.py:122
  54.0 3.8 %collective-permute-start.8 = (bf16[2,4,1,8,128]{4,3,1,0,2:T(8,128)(2,1)S(1)}, bf16[2,4,1,8,128]{4,3,1,0,2:T(8,128)(2,1)S(1)}, u32[]{:S(2)}, u32[]{:S(2)}) collective-permute-start(bf16[2,4,1,8,128]{4,3,1,0,2:T(8,128)(2,1)S(1)} %get-tuple-element.32), channel_id=1, source_target_pairs={{0,2},{1,3},{2,0},{3,1},{4,6},{5,7},{6,4},{7,5},{8,10},{9,11},{10,... | collective-permute-start | bytes 49160 | tf_op jit(solution)/shard_map/ppermute | solution.py:122

commit v7 on v6

--- a/solution.py
+++ b/solution.py
@@ -14,6 +14,7 @@
 BASE = 128
 PIECES = 4
 CORES = 2
+PAIR = 1
 AXES = ("bag", "ulysses")
 
 
@@ -53,7 +54,7 @@
         for kind in (*range(1, kinds), 0):
             copies[kind].wait()
             for span, (core, chip, blocks) in enumerate(places):
-                target[:, core, chip, kind] = stage[kind, span, :, :direct_heads]
+                target[:, core, chip ^ PAIR, kind] = stage[kind, span, :, :direct_heads]
                 for other in range(group_count):
                     for head in range(spread):
                         rows = stage[kind, span, other, direct_heads + head]
@@ -82,40 +83,58 @@
     return packed.reshape(bag_count * group_count, *shape[3:]), aside_q, aside_kv
 
 
-def unpack_spans(span_route, returned, pieces):
-    group_count, _, chips, direct_heads, span_len, width = returned.shape
-    bag_count = chips * CORES
-    spread = pieces[0].shape[2]
-
-    def kernel(route_ref, source, *refs):
-        aside, (target, span_of, sem) = refs[:-3], refs[-3:]
+def unpack_aside(span_route, shape, pieces):
+    bag_count, group_count, heads_here = shape[:3]
+    chips, spread = bag_count // CORES, pieces[0].shape[2]
+
+    def kernel(route_ref, *refs):
+        aside, (target, stage, sem) = refs[:-3], refs[-3:]
         group, bag = lax.axis_index("ulysses"), lax.axis_index("bag")
+        part = pl.ds(heads_here - spread, spread)
         for span in range(bag_count):
             at = route_ref[0, group, span]
-            span_of[at] = span
-            pltpu.make_async_copy(
-                source.at[:, at % CORES, at // CORES], target.at[span, :, pl.ds(0, direct_heads)], sem
-            ).start()
-        for distance, piece in enumerate(aside):
-            for core in range(CORES):
-                for chip in range(chips):
-                    pltpu.make_async_copy(
-                        piece.at[core, chip],
-                        target.at[span_of[chip * CORES + (bag % CORES ^ core)], group ^ distance, pl.ds(direct_heads, spread)],
-                        sem,
-                    ).start()
-        pltpu.make_async_copy(target, target, sem).wait()
-
-    shape = (bag_count, group_count, direct_heads + spread, span_len, width)
-    return pl.pallas_call(
-        kernel,
-        out_shape=jax.ShapeDtypeStruct(shape, returned.dtype),
-        in_specs=[pl.BlockSpec(memory_space=pltpu.VMEM)] * (2 + len(pieces)),
+            chip, core = lax.div(at, CORES), lax.rem(at, CORES) ^ lax.rem(bag, CORES)
+            for distance, piece in enumerate(aside):
+                stage[span, group ^ distance] = piece[core, chip]
+            pltpu.make_async_copy(stage.at[span], target.at[span, :, part], sem).start()
+        pltpu.make_async_copy(stage, stage, sem).wait()
+
+    return pl.pallas_call(
+        kernel,
+        out_shape=jax.ShapeDtypeStruct(shape, pieces[0].dtype),
+        in_specs=[pl.BlockSpec(memory_space=pltpu.VMEM)] * (1 + len(pieces)),
         out_specs=pl.BlockSpec(memory_space=pl.ANY),
-        scratch_shapes=[pltpu.SMEM((bag_count,), jnp.int32), pltpu.SemaphoreType.DMA],
+        scratch_shapes=[
+            pltpu.VMEM((bag_count, group_count, spread, *shape[3:]), pieces[0].dtype),
+            pltpu.SemaphoreType.DMA,
+        ],
+        compiler_params=pltpu.CompilerParams(vmem_limit_bytes=4 * MARGIN),
+        name="unpack_aside",
+    )(span_route, *pieces)
+
+
+def unpack_spans(span_route, returned, output):
+    group_count, _, chips, direct_heads = returned.shape[:4]
+    bag_count = chips * CORES
+
+    def kernel(route_ref, source, _, target, sem):
+        group = lax.axis_index("ulysses")
+        part = pl.ds(0, direct_heads)
+        for span in range(bag_count):
+            at = route_ref[0, group, span]
+            pltpu.make_async_copy(source.at[:, at % CORES, (at // CORES) ^ PAIR], target.at[span, :, part], sem).start()
+        pltpu.make_async_copy(source, source, sem).wait()
+
+    return pl.pallas_call(
+        kernel,
+        out_shape=jax.ShapeDtypeStruct(output.shape, output.dtype),
+        in_specs=[pl.BlockSpec(memory_space=pltpu.VMEM)] * 2 + [pl.BlockSpec(memory_space=pl.ANY)],
+        out_specs=pl.BlockSpec(memory_space=pl.ANY),
+        scratch_shapes=[pltpu.SemaphoreType.DMA],
+        input_output_aliases={2: 0},
         compiler_params=pltpu.CompilerParams(vmem_limit_bytes=2 * returned.nbytes + MARGIN),
         name="unpack_spans",
-    )(span_route, returned, *pieces)
+    )(span_route, returned, output)
 
 
 def swap(rows, axis, distance):
@@ -259,7 +278,7 @@
 
     def sequence_of(row, length_ref):
         slot, offset = row // span_len, row % span_len
-        group, owner = slot // bag_count, slot % (bag_count // CORES) * CORES + slot % bag_count // (bag_count // CORES)
+        group, owner = slot // bag_count, (slot % (bag_count // CORES) ^ PAIR) * CORES + slot % bag_count // (bag_count // CORES)
         position = (group * bag_count + owner) * span_len + offset
         end = jnp.zeros((1, 1), jnp.int32)
         sequence = jnp.zeros(row.shape, jnp.int32)
@@ -321,7 +340,7 @@
         bag * group_count + group
         for group in range(group_count)
         for core in range(CORES)
-        for bag in range(core, bag_count, CORES)
+        for bag in [(chip ^ PAIR) * CORES + core for chip in range(bag_count // CORES)]
     ]
     return lax.all_to_all(rows, AXES, split_axis=0, concat_axis=0, tiled=True, axis_index_groups=[order])
 
@@ -337,6 +356,7 @@
         for rows in (queries, keys, values)
     ]
     slots = (group_count, CORES, bag_count // CORES)
+    paired = jnp.array([chip ^ PAIR for chip in range(bag_count // CORES)])
     powers = all(size & (size - 1) == 0 for size in (bag_count, group_count))
     if span_len >= 2 * seq_lengths.shape[1] and span_len % ROW_TILE == 0 and heads_here > SPREAD and bag_count > CORES and powers:
         packed, aside_q, aside_kv = pack_spans(span_route, seq_lengths, arrays, heads_here - SPREAD)
@@ -352,14 +372,15 @@
         attended = attend(seq_lengths, arrived, bag_count, group_count, (blocks,))
         pieces = swap_groups(settled)
         returned = exchange(attended).reshape(*slots, *attended.shape[1:])
-        result = unpack_spans(span_route, returned, pieces)
+        output = unpack_aside(span_route, arrays[0].shape, pieces)
+        result = unpack_spans(span_route, returned, output)
     else:
         route_mine = lax.dynamic_index_in_dim(span_route[0], lax.axis_index("ulysses"), 0, keepdims=False)
         packed = jnp.stack(arrays, axis=2)[jnp.argsort(route_mine)]
-        packed = packed.reshape(*slots[:0:-1], *packed.shape[1:]).swapaxes(0, 2)
+        packed = packed.reshape(*slots[:0:-1], *packed.shape[1:]).swapaxes(0, 2)[:, :, paired]
         packed = packed.reshape(bag_count * group_count, *packed.shape[3:])
         attended = attend(seq_lengths, exchange(packed), bag_count, group_count)
-        returned = exchange(attended).reshape(*slots, *attended.shape[1:])
+        returned = exchange(attended).reshape(*slots, *attended.shape[1:])[:, :, paired]
         result = returned.swapaxes(0, 2).reshape(bag_count, group_count, *attended.shape[1:])[route_mine]
     return result.transpose(0, 3, 1, 2, 4).reshape(tok_dev, row_width)
 

time: 63.8 us -> 63.3 us (level)
  Pallas kernels: 5.87 us -> 6.56 us
    all_to_all x2, waiting for transfers between devices: 18 us -> 17.2 us  [exchange(): lax.all_to_all(rows, AXES, split_axis=0, concat_axis=0, tiled=True, axis_...]
    pallas_call x1 -> x2, Pallas kernels: 0.97 us -> 1.63 us  [the longest x1 0.87 us: unpack_spans(): pl.pallas_call(kernel, out_shape=jax.ShapeDtypeStruct(output.shape, outpu...]
  transfers between devices with their start and end apart: 12 -> 12, of which waited for: 10 -> 10; matrix products, arithmetic and copies ran while one was open for 1% -> 1% of each run, Pallas kernels for 6% -> 7%
where the time goes in v7:
time: 63.3 us; the launch traced here: 62.8 us
  waiting for transfers between devices  36 us (57%)
  starting transfers between devices  19.7 us (31%)
  Pallas kernels  6.56 us (10%)
    ppermute x10, waiting for transfers between devices, swap(): lax.ppermute(rows, axis, [(index, index ^ distance) for index in range(la...  18.8 us
    all_to_all x2, waiting for transfers between devices, exchange(): lax.all_to_all(rows, AXES, split_axis=0, concat_axis=0, tiled=True, axis_...  17.2 us
    ppermute x10, starting transfers between devices, swap(): lax.ppermute(rows, axis, [(index, index ^ distance) for index in range(la...  11.7 us
    all_to_all x2, starting transfers between devices, exchange(): lax.all_to_all(rows, AXES, split_axis=0, concat_axis=0, tiled=True, axis_...  8.03 us
    pallas_call x1, Pallas kernels, attend(): pl.pallas_call(kernel, out_shape=jax.ShapeDtypeStruct((slots, heads_here,...  1.83 us
    pallas_call x1, Pallas kernels, pack_spans(): pl.pallas_call(kernel, out_shape=[pltpu.VMEM(size, dtype) for size in (sh...  1.44 us
  transfers between devices with their start and end apart: 12, of which 10 were waited for; matrix products, arithmetic and copies ran while one was open for 1% of the time, Pallas kernels for 7%

profile of v7, /device:TPU:0, one launch (start us, length us, event | category | flops | bytes accessed | tf_op | source)
XLA Modules:
  0.0 62.8 jit_solution(9952468091514316066)
XLA Ops:
  0.0 1.4 %pack_spans.1 = (bf16[4,2,4,3,7,8,128]{6,5,4,3,2,1,0:T(8,128)(2,1)S(1)}, bf16[32,8,128]{2,1,0:T(8,128)(2,1)S(1)}, bf16[65,8,128]{2,1,0:T(8,128)(2,1)S(1)}) custom-call(s32[1,4,8]{2,1,0:T(4,128)} %route_ref.3, s32[1,4]{1,0:T(1,128)} %length_ref.1, bf16[8,4,8,8,128]{4,3,2,1,0:T(8,128)(2,1)} %bitcast.78, bf16[8,4,8,8,128]{4,3,2,1,0:T(8,128)(2,1)} %bitcast.79, ...), custom_call_target="tpu_custom_call" | custom-call | tf_op jit(solution)/shard_map/pack_spans/pallas_call | solution.py:69
  1.5 4.1 %collective-permute-start = (bf16[65,8,128]{2,1,0:T(8,128)(2,1)S(1)}, bf16[65,8,128]{2,1,0:T(8,128)(2,1)S(1)}, u32[]{:S(2)}, u32[]{:S(2)}) collective-permute-start(bf16[65,8,128]{2,1,0:T(8,128)(2,1)S(1)} %get-tuple-element.12.near_ref), channel_id=1, source_target_pairs={{0,16},{4,20},{8,24},{12,28},{16,0},{20,4},{24,8},{28,12},{1,17},{... | collective-permute-start | bytes 399368 | tf_op jit(solution)/shard_map/ppermute | solution.py:141
  5.6 1.1 %settle.1 = bf16[32,3,7,8,128]{4,3,2,1,0:T(8,128)(2,1)} custom-call(bf16[32,3,7,8,128]{4,3,2,1,0:T(8,128)(2,1)S(1)} %bitcast.72), custom_call_target="tpu_custom_call" | custom-call | tf_op jit(solution)/shard_map/settle/pallas_call | solution.py:164
  6.7 3.8 %all-to-all-start = ((bf16[32,3,7,8,128]{4,3,2,1,0:T(8,128)(2,1)}), bf16[32,3,7,8,128]{4,3,2,1,0:T(8,128)(2,1)S(1)}, u32[]{:S(2)}, u32[]{:S(2)}) async-start(bf16[32,3,7,8,128]{4,3,2,1,0:T(8,128)(2,1)} %settle.1), calls=%async_computation | async-start | bytes 2752512 | tf_op jit(solution)/shard_map/all_to_all | solution.py:345
  10.5 1.4 %collective-permute-done.across_ref = bf16[65,8,128]{2,1,0:T(8,128)(2,1)S(1)} collective-permute-done((bf16[65,8,128]{2,1,0:T(8,128)(2,1)S(1)}, bf16[65,8,128]{2,1,0:T(8,128)(2,1)S(1)}, u32[]{:S(2)}, u32[]{:S(2)}) %collective-permute-start) | collective-permute-done | bytes 133152 | tf_op jit(solution)/shard_map/ppermute | solution.py:141
  12.0 0.1 collective-permute-start.1
  12.1 1.4 %collective-permute-done.1 = bf16[5,4,4,1,8,128]{5,4,2,0,1,3:T(8,128)(2,1)S(1)} collective-permute-done((bf16[5,4,4,1,8,128]{5,4,2,0,1,3:T(8,128)(2,1)S(1)}, bf16[5,4,4,1,8,128]{5,4,2,0,1,3:T(8,128)(2,1)S(1)}, u32[]{:S(2)}, u32[]{:S(2)}) %collective-permute-start.1) | collective-permute-done | bytes 163872 | tf_op jit(solution)/shard_map/ppermute | solution.py:141
  13.5 0.0 copy-start.1
  13.6 2.6 %collective-permute-start.4 = (bf16[5,2,4,1,8,128]{5,4,2,1,0,3:T(8,128)(2,1)S(1)}, bf16[5,2,4,1,8,128]{5,4,2,1,0,3:T(8,128)(2,1)S(1)}, u32[]{:S(2)}, u32[]{:S(2)}) collective-permute-start(bf16[5,2,4,1,8,128]{5,4,2,1,0,3:T(8,128)(2,1)S(1)} %get-tuple-element.20), channel_id=1, source_target_pairs={{0,3},{1,2},{2,1},{3,0},{4,7},{5,6},{6,5},{7,4},{8,11},{9,10},{10,... | collective-permute-start | bytes 245768 | tf_op jit(solution)/shard_map/ppermute | solution.py:141
  16.1 0.5 collective-permute-start.3
  16.6 0.5 collective-permute-start.2
  17.1 8.4 %collective-permute-done.4 = bf16[5,2,4,1,8,128]{5,4,2,1,0,3:T(8,128)(2,1)S(1)} collective-permute-done((bf16[5,2,4,1,8,128]{5,4,2,1,0,3:T(8,128)(2,1)S(1)}, bf16[5,2,4,1,8,128]{5,4,2,1,0,3:T(8,128)(2,1)S(1)}, u32[]{:S(2)}, u32[]{:S(2)}) %collective-permute-start.4) | collective-permute-done | bytes 81952 | tf_op jit(solution)/shard_map/ppermute | solution.py:141
  25.5 3.1 %collective-permute-done.3 = bf16[5,2,4,1,8,128]{5,4,2,1,0,3:T(8,128)(2,1)S(1)} collective-permute-done((bf16[5,2,4,1,8,128]{5,4,2,1,0,3:T(8,128)(2,1)S(1)}, bf16[5,2,4,1,8,128]{5,4,2,1,0,3:T(8,128)(2,1)S(1)}, u32[]{:S(2)}, u32[]{:S(2)}) %collective-permute-start.3) | collective-permute-done | bytes 81952 | tf_op jit(solution)/shard_map/ppermute | solution.py:141
  28.7 0.1 pad_maximum_fusion.1
  28.8 0.1 collective-permute-start.5
  28.9 13.5 %all-to-all-done.packed_ref = bf16[32,3,7,8,128]{4,3,2,1,0:T(8,128)(2,1)S(1)} async-done(((bf16[32,3,7,8,128]{4,3,2,1,0:T(8,128)(2,1)}), bf16[32,3,7,8,128]{4,3,2,1,0:T(8,128)(2,1)S(1)}, u32[]{:S(2)}, u32[]{:S(2)}) %all-to-all-start) | async-done | bytes 1376288 | tf_op jit(solution)/shard_map/all_to_all | solution.py:345
  42.4 1.8 %attend_bag.1 = bf16[32,7,8,128]{3,2,1,0:T(8,128)(2,1)} custom-call(s32[1,4]{1,0:T(1,128)S(1)} %copy-done.1, bf16[32,3,7,8,128]{4,3,2,1,0:T(8,128)(2,1)S(1)} %all-to-all-done.packed_ref, bf16[5,4,2,4,1,8,128]{6,5,4,3,2,1,0:T(8,128)(2,1)S(1)} %get-tuple-element.18.refs_0_), custom_call_target="tpu_custom_call" | custom-call | tf_op jit(solution)/shard_map/attend_bag/pallas_call | solution.py:327
  44.2 4.2 %all-to-all-start.1 = ((bf16[32,7,8,128]{3,2,1,0:T(8,128)(2,1)}), bf16[32,7,8,128]{3,2,1,0:T(8,128)(2,1)S(1)}, u32[]{:S(2)}, u32[]{:S(2)}) async-start(bf16[32,7,8,128]{3,2,1,0:T(8,128)(2,1)} %attend_bag.1), calls=%async_computation.1 | async-start | bytes 917504 | tf_op jit(solution)/shard_map/all_to_all | solution.py:345
  48.4 0.0 copy-start
  48.5 0.1 pad_maximum_fusion.pair_ref
  48.6 0.5 attend_plane.1
  49.1 0.3 collective-permute-start.6
  49.4 1.0 %collective-permute-done.6 = bf16[4,4,1,8,128]{4,3,1,0,2:T(8,128)(2,1)S(1)} collective-permute-done((bf16[4,4,1,8,128]{4,3,1,0,2:T(8,128)(2,1)S(1)}, bf16[4,4,1,8,128]{4,3,1,0,2:T(8,128)(2,1)S(1)}, u32[]{:S(2)}, u32[]{:S(2)}) %collective-permute-start.6) | collective-permute-done | bytes 32800 | tf_op jit(solution)/shard_map/ppermute | solution.py:141
  50.4 2.7 %collective-permute-start.9 = (bf16[2,4,1,8,128]{4,3,2,1,0:T(8,128)(2,1)S(1)}, bf16[2,4,1,8,128]{4,3,2,1,0:T(8,128)(2,1)S(1)}, u32[]{:S(2)}, u32[]{:S(2)}) collective-permute-start(bf16[2,4,1,8,128]{4,3,2,1,0:T(8,128)(2,1)S(1)} %get-tuple-element.29), channel_id=1, source_target_pairs={{0,3},{1,2},{2,1},{3,0},{4,7},{5,6},{6,5},{7,4},{8,11},{9,10},{10,... | collective-permute-start | bytes 49160 | tf_op jit(solution)/shard_map/ppermute | solution.py:141
  53.1 0.6 collective-permute-start.7
  53.7 0.3 collective-permute-start.8
  53.9 1.5 %collective-permute-done.9.refs_3_ = bf16[2,4,1,8,128]{4,3,2,1,0:T(8,128)(2,1)S(1)} collective-permute-done((bf16[2,4,1,8,128]{4,3,2,1,0:T(8,128)(2,1)S(1)}, bf16[2,4,1,8,128]{4,3,2,1,0:T(8,128)(2,1)S(1)}, u32[]{:S(2)}, u32[]{:S(2)}) %collective-permute-start.9) | collective-permute-done | bytes 16416 | tf_op jit(solution)/shard_map/ppermute | solution.py:141
  55.5 1.4 %collective-permute-done.7 = bf16[2,4,1,8,128]{4,3,1,0,2:T(8,128)(2,1)S(1)} collective-permute-done((bf16[2,4,1,8,128]{4,3,1,0,2:T(8,128)(2,1)S(1)}, bf16[2,4,1,8,128]{4,3,1,0,2:T(8,128)(2,1)S(1)}, u32[]{:S(2)}, u32[]{:S(2)}) %collective-permute-start.7) | collective-permute-done | bytes 16416 | tf_op jit(solution)/shard_map/ppermute | solution.py:141
  56.9 0.6 collective-permute-done.8
  57.4 0.8 %unpack_aside.1._ = bf16[8,4,8,8,128]{4,3,2,1,0:T(8,128)(2,1)} custom-call(s32[1,4,8]{2,1,0:T(4,128)S(1)} %copy-done, bf16[2,4,1,8,128]{4,3,2,1,0:T(8,128)(2,1)S(1)} %get-tuple-element.30.refs_0_, bf16[2,4,1,8,128]{4,3,2,1,0:T(8,128)(2,1)S(1)} %bitcast.75, bf16[2,4,1,8,128]{4,3,2,1,0:T(8,128)(2,1)S(1)} %bitcast.76, ...), custom_call_target="tpu_custom_call" | custom-call | tf_op jit(solution)/shard_map/unpack_aside/pallas_call | solution.py:102
  58.2 3.7 %all-to-all-done.1 = bf16[32,7,8,128]{3,2,1,0:T(8,128)(2,1)S(1)} async-done(((bf16[32,7,8,128]{3,2,1,0:T(8,128)(2,1)}), bf16[32,7,8,128]{3,2,1,0:T(8,128)(2,1)S(1)}, u32[]{:S(2)}, u32[]{:S(2)}) %all-to-all-start.1) | async-done | bytes 458784 | tf_op jit(solution)/shard_map/all_to_all | solution.py:345
  61.9 0.9 %unpack_spans.1 = bf16[8,4,8,8,128]{4,3,2,1,0:T(8,128)(2,1)} custom-call(s32[1,4,8]{2,1,0:T(4,128)S(1)} %copy-done, bf16[4,2,4,7,8,128]{5,4,3,2,1,0:T(8,128)(2,1)S(1)} %bitcast.71, bf16[8,4,8,8,128]{4,3,2,1,0:T(8,128)(2,1)} %unpack_aside.1._), custom_call_target="tpu_custom_call", output_to_operand_aliasing={{}: (2, {})} | custom-call | tf_op jit(solution)/shard_map/unpack_spans/pallas_call | solution.py:128
  (20 shorter events, 0.2 us)
Async XLA Ops:
  1.5 10.5 %collective-permute-start = (bf16[65,8,128]{2,1,0:T(8,128)(2,1)S(1)}, bf16[65,8,128]{2,1,0:T(8,128)(2,1)S(1)}, u32[]{:S(2)}, u32[]{:S(2)}) collective-permute-start(bf16[65,8,128]{2,1,0:T(8,128)(2,1)S(1)} %get-tuple-element.12.near_ref), channel_id=1, source_target_pairs={{0,16},{4,20},{8,24},{12,28},{16,0},{20,4},{24,8},{28,12},{1,17},{... | collective-permute-start | bytes 399368 | tf_op jit(solution)/shard_map/ppermute | solution.py:141
  6.7 35.7 %all-to-all-start = ((bf16[32,3,7,8,128]{4,3,2,1,0:T(8,128)(2,1)}), bf16[32,3,7,8,128]{4,3,2,1,0:T(8,128)(2,1)S(1)}, u32[]{:S(2)}, u32[]{:S(2)}) async-start(bf16[32,3,7,8,128]{4,3,2,1,0:T(8,128)(2,1)} %settle.1), calls=%async_computation | async-start | bytes 2752512 | tf_op jit(solution)/shard_map/all_to_all | solution.py:345
  12.0 1.5 %collective-permute-start.1 = (bf16[5,4,4,1,8,128]{5,4,2,0,1,3:T(8,128)(2,1)S(1)}, bf16[5,4,4,1,8,128]{5,4,2,0,1,3:T(8,128)(2,1)S(1)}, u32[]{:S(2)}, u32[]{:S(2)}) collective-permute-start(bf16[5,4,4,1,8,128]{5,4,2,0,1,3:T(8,128)(2,1)S(1)} %bitcast.84), channel_id=1, source_target_pairs={{0,4},{4,0},{8,12},{12,8},{16,20},{20,16},{24,28},{28,24},{1,5},{5... | collective-permute-start | bytes 491528 | tf_op jit(solution)/shard_map/ppermute | solution.py:141
  13.5 28.8 %copy-start.1 = (s32[1,4]{1,0:T(1,128)S(1)}, s32[1,4]{1,0:T(1,128)}, u32[]{:S(2)}) copy-start(s32[1,4]{1,0:T(1,128)} %length_ref.1) | copy-start | bytes 52
  13.6 12.0 %collective-permute-start.4 = (bf16[5,2,4,1,8,128]{5,4,2,1,0,3:T(8,128)(2,1)S(1)}, bf16[5,2,4,1,8,128]{5,4,2,1,0,3:T(8,128)(2,1)S(1)}, u32[]{:S(2)}, u32[]{:S(2)}) collective-permute-start(bf16[5,2,4,1,8,128]{5,4,2,1,0,3:T(8,128)(2,1)S(1)} %get-tuple-element.20), channel_id=1, source_target_pairs={{0,3},{1,2},{2,1},{3,0},{4,7},{5,6},{6,5},{7,4},{8,11},{9,10},{10,... | collective-permute-start | bytes 245768 | tf_op jit(solution)/shard_map/ppermute | solution.py:141
  16.1 12.5 %collective-permute-start.3 = (bf16[5,2,4,1,8,128]{5,4,2,1,0,3:T(8,128)(2,1)S(1)}, bf16[5,2,4,1,8,128]{5,4,2,1,0,3:T(8,128)(2,1)S(1)}, u32[]{:S(2)}, u32[]{:S(2)}) collective-permute-start(bf16[5,2,4,1,8,128]{5,4,2,1,0,3:T(8,128)(2,1)S(1)} %get-tuple-element.21), channel_id=1, source_target_pairs={{0,2},{1,3},{2,0},{3,1},{4,6},{5,7},{6,4},{7,5},{8,10},{9,11},{10,... | collective-permute-start | bytes 245768 | tf_op jit(solution)/shard_map/ppermute | solution.py:141
  16.6 12.0 %collective-permute-start.2 = (bf16[5,2,4,1,8,128]{5,4,2,1,0,3:T(8,128)(2,1)S(1)}, bf16[5,2,4,1,8,128]{5,4,2,1,0,3:T(8,128)(2,1)S(1)}, u32[]{:S(2)}, u32[]{:S(2)}) collective-permute-start(bf16[5,2,4,1,8,128]{5,4,2,1,0,3:T(8,128)(2,1)S(1)} %get-tuple-element.22), channel_id=1, source_target_pairs={{0,1},{1,0},{2,3},{3,2},{4,5},{5,4},{6,7},{7,6},{8,9},{9,8},{10,11... | collective-permute-start | bytes 245768 | tf_op jit(solution)/shard_map/ppermute | solution.py:141
  28.8 19.7 %collective-permute-start.5 = (bf16[130,8,128]{2,1,0:T(8,128)(2,1)S(1)}, bf16[130,8,128]{2,1,0:T(8,128)(2,1)S(1)}, u32[]{:S(2)}, u32[]{:S(2)}) collective-permute-start(bf16[130,8,128]{2,1,0:T(8,128)(2,1)S(1)} %pad_maximum_fusion.2), channel_id=1, source_target_pairs={{0,8},{4,12},{8,0},{12,4},{16,24},{20,28},{24,16},{28,20},{1,9},{5... | collective-permute-start | bytes 798728 | tf_op jit(solution)/shard_map/ppermute | solution.py:141
  44.2 17.7 %all-to-all-start.1 = ((bf16[32,7,8,128]{3,2,1,0:T(8,128)(2,1)}), bf16[32,7,8,128]{3,2,1,0:T(8,128)(2,1)S(1)}, u32[]{:S(2)}, u32[]{:S(2)}) async-start(bf16[32,7,8,128]{3,2,1,0:T(8,128)(2,1)} %attend_bag.1), calls=%async_computation.1 | async-start | bytes 917504 | tf_op jit(solution)/shard_map/all_to_all | solution.py:345
  48.4 9.0 %copy-start = (s32[1,4,8]{2,1,0:T(4,128)S(1)}, s32[1,4,8]{2,1,0:T(4,128)}, u32[]{:S(2)}) copy-start(s32[1,4,8]{2,1,0:T(4,128)} %route_ref.3) | copy-start | bytes 388
  49.1 1.3 %collective-permute-start.6 = (bf16[4,4,1,8,128]{4,3,1,0,2:T(8,128)(2,1)S(1)}, bf16[4,4,1,8,128]{4,3,1,0,2:T(8,128)(2,1)S(1)}, u32[]{:S(2)}, u32[]{:S(2)}) collective-permute-start(bf16[4,4,1,8,128]{4,3,1,0,2:T(8,128)(2,1)S(1)} %slice_bitcast_fusion.7), channel_id=1, source_target_pairs={{0,4},{4,0},{8,12},{12,8},{16,20},{20,16},{24,28},{28,24},{1,5},{5... | collective-permute-start | bytes 98312 | tf_op jit(solution)/shard_map/ppermute | solution.py:141
  50.4 5.1 %collective-permute-start.9 = (bf16[2,4,1,8,128]{4,3,2,1,0:T(8,128)(2,1)S(1)}, bf16[2,4,1,8,128]{4,3,2,1,0:T(8,128)(2,1)S(1)}, u32[]{:S(2)}, u32[]{:S(2)}) collective-permute-start(bf16[2,4,1,8,128]{4,3,2,1,0:T(8,128)(2,1)S(1)} %get-tuple-element.29), channel_id=1, source_target_pairs={{0,3},{1,2},{2,1},{3,0},{4,7},{5,6},{6,5},{7,4},{8,11},{9,10},{10,... | collective-permute-start | bytes 49160 | tf_op jit(solution)/shard_map/ppermute | solution.py:141
  53.1 3.7 %collective-permute-start.7 = (bf16[2,4,1,8,128]{4,3,1,0,2:T(8,128)(2,1)S(1)}, bf16[2,4,1,8,128]{4,3,1,0,2:T(8,128)(2,1)S(1)}, u32[]{:S(2)}, u32[]{:S(2)}) collective-permute-start(bf16[2,4,1,8,128]{4,3,1,0,2:T(8,128)(2,1)S(1)} %get-tuple-element.31), channel_id=1, source_target_pairs={{0,1},{1,0},{2,3},{3,2},{4,5},{5,4},{6,7},{7,6},{8,9},{9,8},{10,11... | collective-permute-start | bytes 49160 | tf_op jit(solution)/shard_map/ppermute | solution.py:141
  53.7 3.7 %collective-permute-start.8 = (bf16[2,4,1,8,128]{4,3,1,0,2:T(8,128)(2,1)S(1)}, bf16[2,4,1,8,128]{4,3,1,0,2:T(8,128)(2,1)S(1)}, u32[]{:S(2)}, u32[]{:S(2)}) collective-permute-start(bf16[2,4,1,8,128]{4,3,1,0,2:T(8,128)(2,1)S(1)} %get-tuple-element.32), channel_id=1, source_target_pairs={{0,2},{1,3},{2,0},{3,1},{4,6},{5,7},{6,4},{7,5},{8,10},{9,11},{10,... | collective-permute-start | bytes 49160 | tf_op jit(solution)/shard_map/ppermute | solution.py:141

commit v8 on v7

--- a/solution.py
+++ b/solution.py
@@ -15,6 +15,7 @@
 PIECES = 4
 CORES = 2
 PAIR = 1
+ROWS = 256
 AXES = ("bag", "ulysses")
 
 
@@ -122,7 +123,7 @@
         part = pl.ds(0, direct_heads)
         for span in range(bag_count):
             at = route_ref[0, group, span]
-            pltpu.make_async_copy(source.at[:, at % CORES, (at // CORES) ^ PAIR], target.at[span, :, part], sem).start()
+            pltpu.make_async_copy(source.at[:, at % CORES, at // CORES], target.at[span, :, part], sem).start()
         pltpu.make_async_copy(source, source, sem).wait()
 
     return pl.pallas_call(
@@ -268,10 +269,10 @@
     )(lengths, queries, keys_values)
 
 
-def attend(lengths, packed, bag_count, group_count, after=()):
+def attend(lengths, packed, bag_count, group_count, after=(), back=None):
     slots, _, heads_here, span_len, width = packed.shape
     bag_tok = slots * span_len
-    block = min(256, bag_tok)
+    block = min(ROWS, bag_tok)
     block_slots = block // span_len
     seq_bag = lengths.shape[1]
     scale = 1.0 / math.sqrt(width)
@@ -316,7 +317,12 @@
             for head in range(heads_here):
                 output = jnp.dot(weights[head], rows(2, 0, slots, head), preferred_element_type=jnp.float32)
                 output = output.reshape(block_slots, span_len, width).astype(out_ref.dtype)
-                out_ref[pl.ds(first, block_slots), head] = output
+                if back:
+                    output = output.reshape(group_count, CORES, len(back), span_len, width)
+                    for slot, chip in enumerate(back):
+                        out_ref[:, :, slot, head] = output[:, :, chip ^ PAIR]
+                else:
+                    out_ref[pl.ds(first, block_slots), head] = output
             return carry
 
         if bag_tok == block:
@@ -326,7 +332,9 @@
 
     return pl.pallas_call(
         kernel,
-        out_shape=jax.ShapeDtypeStruct((slots, heads_here, span_len, width), packed.dtype),
+        out_shape=jax.ShapeDtypeStruct(
+            (*((group_count, CORES, len(back)) if back else (slots,)), heads_here, span_len, width), packed.dtype
+        ),
         in_specs=[pl.BlockSpec(memory_space=pltpu.VMEM)] * 2 + [pl.BlockSpec(memory_space=pl.ANY)] * len(after),
         out_specs=pl.BlockSpec(memory_space=pltpu.VMEM),
         compiler_params=pltpu.CompilerParams(vmem_limit_bytes=32 << 20),
@@ -334,13 +342,13 @@
     )(lengths, packed, *after)
 
 
-def exchange(rows):
+def exchange(rows, chips=None):
     bag_count, group_count = lax.axis_size("bag"), lax.axis_size("ulysses")
     order = [
         bag * group_count + group
         for group in range(group_count)
         for core in range(CORES)
-        for bag in [(chip ^ PAIR) * CORES + core for chip in range(bag_count // CORES)]
+        for bag in [chip * CORES + core for chip in chips or [k ^ PAIR for k in range(bag_count // CORES)]]
     ]
     return lax.all_to_all(rows, AXES, split_axis=0, concat_axis=0, tiled=True, axis_index_groups=[order])
 
@@ -358,7 +366,7 @@
     slots = (group_count, CORES, bag_count // CORES)
     paired = jnp.array([chip ^ PAIR for chip in range(bag_count // CORES)])
     powers = all(size & (size - 1) == 0 for size in (bag_count, group_count))
-    if span_len >= 2 * seq_lengths.shape[1] and span_len % ROW_TILE == 0 and heads_here > SPREAD and bag_count > CORES and powers:
+    if span_len >= 2 * seq_lengths.shape[1] and span_len % ROW_TILE == 0 and bag_count * group_count * span_len <= ROWS and heads_here > SPREAD and bag_count > CORES and powers:
         packed, aside_q, aside_kv = pack_spans(span_route, seq_lengths, arrays, heads_here - SPREAD)
         across = swap(aside_kv, "bag", bag_count // 2)
         arrived = exchange(settle(packed))
@@ -369,9 +377,11 @@
         pairs, lengths = gather_chips(pairs, tables)
         settled = attend_plane(lengths, blocks[0], pairs, seq_lengths.shape[1], bag_count)
         settled = swap_cores(settled, 1)
-        attended = attend(seq_lengths, arrived, bag_count, group_count, (blocks,))
+        back = list(range(bag_count // CORES))
+        attended = attend(seq_lengths, arrived, bag_count, group_count, (blocks,), back)
+        attended = attended.reshape(bag_count * group_count, *attended.shape[3:])
         pieces = swap_groups(settled)
-        returned = exchange(attended).reshape(*slots, *attended.shape[1:])
+        returned = exchange(attended, back).reshape(*slots, *attended.shape[1:])
         output = unpack_aside(span_route, arrays[0].shape, pieces)
         result = unpack_spans(span_route, returned, output)
     else:

time: 63.3 us -> 63.3 us (level)
  no operation moved by 1% of the time
where the time goes in v8:
time: 63.3 us; the launch traced here: 62.4 us
  waiting for transfers between devices  35.6 us (56%)
  starting transfers between devices  19.7 us (31%)
  Pallas kernels  6.56 us (10%)
    ppermute x10, waiting for transfers between devices, swap(): lax.ppermute(rows, axis, [(index, index ^ distance) for index in range(la...  18.9 us
    all_to_all x2, waiting for transfers between devices, exchange(): lax.all_to_all(rows, AXES, split_axis=0, concat_axis=0, tiled=True, axis_...  16.7 us
    ppermute x10, starting transfers between devices, swap(): lax.ppermute(rows, axis, [(index, index ^ distance) for index in range(la...  11.7 us
    all_to_all x2, starting transfers between devices, exchange(): lax.all_to_all(rows, AXES, split_axis=0, concat_axis=0, tiled=True, axis_...  8.03 us
    pallas_call x1, Pallas kernels, attend(): pl.pallas_call(kernel, out_shape=jax.ShapeDtypeStruct((*((group_count, CO...  1.83 us
    pallas_call x1, Pallas kernels, pack_spans(): pl.pallas_call(kernel, out_shape=[pltpu.VMEM(size, dtype) for size in (sh...  1.44 us
  transfers between devices with their start and end apart: 12, of which 10 were waited for; matrix products, arithmetic and copies ran while one was open for 1% of the time, Pallas kernels for 7%

profile of v8, /device:TPU:0, one launch (start us, length us, event | category | flops | bytes accessed | tf_op | source)
XLA Modules:
  0.0 62.4 jit_solution(3056074844238049029)
XLA Ops:
  0.0 1.4 %pack_spans.1 = (bf16[4,2,4,3,7,8,128]{6,5,4,3,2,1,0:T(8,128)(2,1)S(1)}, bf16[32,8,128]{2,1,0:T(8,128)(2,1)S(1)}, bf16[65,8,128]{2,1,0:T(8,128)(2,1)S(1)}) custom-call(s32[1,4,8]{2,1,0:T(4,128)} %route_ref.3, s32[1,4]{1,0:T(1,128)} %length_ref.1, bf16[8,4,8,8,128]{4,3,2,1,0:T(8,128)(2,1)} %bitcast.79, bf16[8,4,8,8,128]{4,3,2,1,0:T(8,128)(2,1)} %bitcast.80, ...), custom_call_target="tpu_custom_call" | custom-call | tf_op jit(solution)/shard_map/pack_spans/pallas_call | solution.py:70
  1.5 4.1 %collective-permute-start = (bf16[65,8,128]{2,1,0:T(8,128)(2,1)S(1)}, bf16[65,8,128]{2,1,0:T(8,128)(2,1)S(1)}, u32[]{:S(2)}, u32[]{:S(2)}) collective-permute-start(bf16[65,8,128]{2,1,0:T(8,128)(2,1)S(1)} %get-tuple-element.12.near_ref), channel_id=1, source_target_pairs={{0,16},{4,20},{8,24},{12,28},{16,0},{20,4},{24,8},{28,12},{1,17},{... | collective-permute-start | bytes 399368 | tf_op jit(solution)/shard_map/ppermute | solution.py:142
  5.6 1.1 %settle.1 = bf16[32,3,7,8,128]{4,3,2,1,0:T(8,128)(2,1)} custom-call(bf16[32,3,7,8,128]{4,3,2,1,0:T(8,128)(2,1)S(1)} %bitcast.73), custom_call_target="tpu_custom_call" | custom-call | tf_op jit(solution)/shard_map/settle/pallas_call | solution.py:165
  6.7 3.8 %all-to-all-start = ((bf16[32,3,7,8,128]{4,3,2,1,0:T(8,128)(2,1)}), bf16[32,3,7,8,128]{4,3,2,1,0:T(8,128)(2,1)S(1)}, u32[]{:S(2)}, u32[]{:S(2)}) async-start(bf16[32,3,7,8,128]{4,3,2,1,0:T(8,128)(2,1)} %settle.1), calls=%async_computation | async-start | bytes 2752512 | tf_op jit(solution)/shard_map/all_to_all | solution.py:353
  10.5 1.4 %collective-permute-done.across_ref = bf16[65,8,128]{2,1,0:T(8,128)(2,1)S(1)} collective-permute-done((bf16[65,8,128]{2,1,0:T(8,128)(2,1)S(1)}, bf16[65,8,128]{2,1,0:T(8,128)(2,1)S(1)}, u32[]{:S(2)}, u32[]{:S(2)}) %collective-permute-start) | collective-permute-done | bytes 133152 | tf_op jit(solution)/shard_map/ppermute | solution.py:142
  12.0 0.1 collective-permute-start.1
  12.1 1.4 %collective-permute-done.1 = bf16[5,4,4,1,8,128]{5,4,2,0,1,3:T(8,128)(2,1)S(1)} collective-permute-done((bf16[5,4,4,1,8,128]{5,4,2,0,1,3:T(8,128)(2,1)S(1)}, bf16[5,4,4,1,8,128]{5,4,2,0,1,3:T(8,128)(2,1)S(1)}, u32[]{:S(2)}, u32[]{:S(2)}) %collective-permute-start.1) | collective-permute-done | bytes 163872 | tf_op jit(solution)/shard_map/ppermute | solution.py:142
  13.5 0.0 copy-start.1
  13.6 2.6 %collective-permute-start.4 = (bf16[5,2,4,1,8,128]{5,4,2,1,0,3:T(8,128)(2,1)S(1)}, bf16[5,2,4,1,8,128]{5,4,2,1,0,3:T(8,128)(2,1)S(1)}, u32[]{:S(2)}, u32[]{:S(2)}) collective-permute-start(bf16[5,2,4,1,8,128]{5,4,2,1,0,3:T(8,128)(2,1)S(1)} %get-tuple-element.20), channel_id=1, source_target_pairs={{0,3},{1,2},{2,1},{3,0},{4,7},{5,6},{6,5},{7,4},{8,11},{9,10},{10,... | collective-permute-start | bytes 245768 | tf_op jit(solution)/shard_map/ppermute | solution.py:142
  16.1 0.5 collective-permute-start.3
  16.6 0.5 collective-permute-start.2
  17.1 8.4 %collective-permute-done.4 = bf16[5,2,4,1,8,128]{5,4,2,1,0,3:T(8,128)(2,1)S(1)} collective-permute-done((bf16[5,2,4,1,8,128]{5,4,2,1,0,3:T(8,128)(2,1)S(1)}, bf16[5,2,4,1,8,128]{5,4,2,1,0,3:T(8,128)(2,1)S(1)}, u32[]{:S(2)}, u32[]{:S(2)}) %collective-permute-start.4) | collective-permute-done | bytes 81952 | tf_op jit(solution)/shard_map/ppermute | solution.py:142
  25.5 3.1 %collective-permute-done.3 = bf16[5,2,4,1,8,128]{5,4,2,1,0,3:T(8,128)(2,1)S(1)} collective-permute-done((bf16[5,2,4,1,8,128]{5,4,2,1,0,3:T(8,128)(2,1)S(1)}, bf16[5,2,4,1,8,128]{5,4,2,1,0,3:T(8,128)(2,1)S(1)}, u32[]{:S(2)}, u32[]{:S(2)}) %collective-permute-start.3) | collective-permute-done | bytes 81952 | tf_op jit(solution)/shard_map/ppermute | solution.py:142
  28.7 0.1 pad_maximum_fusion.1
  28.8 0.1 collective-permute-start.5
  28.9 13.5 %all-to-all-done.packed_ref = bf16[32,3,7,8,128]{4,3,2,1,0:T(8,128)(2,1)S(1)} async-done(((bf16[32,3,7,8,128]{4,3,2,1,0:T(8,128)(2,1)}), bf16[32,3,7,8,128]{4,3,2,1,0:T(8,128)(2,1)S(1)}, u32[]{:S(2)}, u32[]{:S(2)}) %all-to-all-start) | async-done | bytes 1376288 | tf_op jit(solution)/shard_map/all_to_all | solution.py:353
  42.4 1.8 %attend_bag.1 = bf16[4,2,4,7,8,128]{5,4,3,2,1,0:T(8,128)(2,1)} custom-call(s32[1,4]{1,0:T(1,128)S(1)} %copy-done.1, bf16[32,3,7,8,128]{4,3,2,1,0:T(8,128)(2,1)S(1)} %all-to-all-done.packed_ref, bf16[5,4,2,4,1,8,128]{6,5,4,3,2,1,0:T(8,128)(2,1)S(1)} %get-tuple-element.18.refs_0_), custom_call_target="tpu_custom_call" | custom-call | tf_op jit(solution)/shard_map/attend_bag/pallas_call | solution.py:333
  44.2 4.2 %all-to-all-start.1 = ((bf16[32,7,8,128]{3,2,1,0:T(8,128)(2,1)}), bf16[32,7,8,128]{3,2,1,0:T(8,128)(2,1)S(1)}, u32[]{:S(2)}, u32[]{:S(2)}) async-start(bf16[32,7,8,128]{3,2,1,0:T(8,128)(2,1)} %bitcast.22), calls=%async_computation.1 | async-start | bytes 917504 | tf_op jit(solution)/shard_map/all_to_all | solution.py:353
  48.4 0.0 copy-start
  48.5 0.1 pad_maximum_fusion.pair_ref
  48.6 0.5 attend_plane.1
  49.1 0.3 collective-permute-start.6
  49.4 1.0 %collective-permute-done.6 = bf16[4,4,1,8,128]{4,3,1,0,2:T(8,128)(2,1)S(1)} collective-permute-done((bf16[4,4,1,8,128]{4,3,1,0,2:T(8,128)(2,1)S(1)}, bf16[4,4,1,8,128]{4,3,1,0,2:T(8,128)(2,1)S(1)}, u32[]{:S(2)}, u32[]{:S(2)}) %collective-permute-start.6) | collective-permute-done | bytes 32800 | tf_op jit(solution)/shard_map/ppermute | solution.py:142
  50.4 2.7 %collective-permute-start.9 = (bf16[2,4,1,8,128]{4,3,2,1,0:T(8,128)(2,1)S(1)}, bf16[2,4,1,8,128]{4,3,2,1,0:T(8,128)(2,1)S(1)}, u32[]{:S(2)}, u32[]{:S(2)}) collective-permute-start(bf16[2,4,1,8,128]{4,3,2,1,0:T(8,128)(2,1)S(1)} %get-tuple-element.29), channel_id=1, source_target_pairs={{0,3},{1,2},{2,1},{3,0},{4,7},{5,6},{6,5},{7,4},{8,11},{9,10},{10,... | collective-permute-start | bytes 49160 | tf_op jit(solution)/shard_map/ppermute | solution.py:142
  53.1 0.6 collective-permute-start.7
  53.7 0.3 collective-permute-start.8
  53.9 1.4 %collective-permute-done.9.refs_3_ = bf16[2,4,1,8,128]{4,3,2,1,0:T(8,128)(2,1)S(1)} collective-permute-done((bf16[2,4,1,8,128]{4,3,2,1,0:T(8,128)(2,1)S(1)}, bf16[2,4,1,8,128]{4,3,2,1,0:T(8,128)(2,1)S(1)}, u32[]{:S(2)}, u32[]{:S(2)}) %collective-permute-start.9) | collective-permute-done | bytes 16416 | tf_op jit(solution)/shard_map/ppermute | solution.py:142
  55.3 1.7 %collective-permute-done.7 = bf16[2,4,1,8,128]{4,3,1,0,2:T(8,128)(2,1)S(1)} collective-permute-done((bf16[2,4,1,8,128]{4,3,1,0,2:T(8,128)(2,1)S(1)}, bf16[2,4,1,8,128]{4,3,1,0,2:T(8,128)(2,1)S(1)}, u32[]{:S(2)}, u32[]{:S(2)}) %collective-permute-start.7) | collective-permute-done | bytes 16416 | tf_op jit(solution)/shard_map/ppermute | solution.py:142
  57.0 0.5 collective-permute-done.8
  57.5 0.8 %unpack_aside.1._ = bf16[8,4,8,8,128]{4,3,2,1,0:T(8,128)(2,1)} custom-call(s32[1,4,8]{2,1,0:T(4,128)S(1)} %copy-done, bf16[2,4,1,8,128]{4,3,2,1,0:T(8,128)(2,1)S(1)} %get-tuple-element.30.refs_0_, bf16[2,4,1,8,128]{4,3,2,1,0:T(8,128)(2,1)S(1)} %bitcast.76, bf16[2,4,1,8,128]{4,3,2,1,0:T(8,128)(2,1)S(1)} %bitcast.77, ...), custom_call_target="tpu_custom_call" | custom-call | tf_op jit(solution)/shard_map/unpack_aside/pallas_call | solution.py:103
  58.3 3.2 %all-to-all-done.1 = bf16[32,7,8,128]{3,2,1,0:T(8,128)(2,1)S(1)} async-done(((bf16[32,7,8,128]{3,2,1,0:T(8,128)(2,1)}), bf16[32,7,8,128]{3,2,1,0:T(8,128)(2,1)S(1)}, u32[]{:S(2)}, u32[]{:S(2)}) %all-to-all-start.1) | async-done | bytes 458784 | tf_op jit(solution)/shard_map/all_to_all | solution.py:353
  61.5 0.9 %unpack_spans.1 = bf16[8,4,8,8,128]{4,3,2,1,0:T(8,128)(2,1)} custom-call(s32[1,4,8]{2,1,0:T(4,128)S(1)} %copy-done, bf16[4,2,4,7,8,128]{5,4,3,2,1,0:T(8,128)(2,1)S(1)} %bitcast.72, bf16[8,4,8,8,128]{4,3,2,1,0:T(8,128)(2,1)} %unpack_aside.1._), custom_call_target="tpu_custom_call", output_to_operand_aliasing={{}: (2, {})} | custom-call | tf_op jit(solution)/shard_map/unpack_spans/pallas_call | solution.py:129
  (20 shorter events, 0.2 us)
Async XLA Ops:
  1.5 10.5 %collective-permute-start = (bf16[65,8,128]{2,1,0:T(8,128)(2,1)S(1)}, bf16[65,8,128]{2,1,0:T(8,128)(2,1)S(1)}, u32[]{:S(2)}, u32[]{:S(2)}) collective-permute-start(bf16[65,8,128]{2,1,0:T(8,128)(2,1)S(1)} %get-tuple-element.12.near_ref), channel_id=1, source_target_pairs={{0,16},{4,20},{8,24},{12,28},{16,0},{20,4},{24,8},{28,12},{1,17},{... | collective-permute-start | bytes 399368 | tf_op jit(solution)/shard_map/ppermute | solution.py:142
  6.7 35.7 %all-to-all-start = ((bf16[32,3,7,8,128]{4,3,2,1,0:T(8,128)(2,1)}), bf16[32,3,7,8,128]{4,3,2,1,0:T(8,128)(2,1)S(1)}, u32[]{:S(2)}, u32[]{:S(2)}) async-start(bf16[32,3,7,8,128]{4,3,2,1,0:T(8,128)(2,1)} %settle.1), calls=%async_computation | async-start | bytes 2752512 | tf_op jit(solution)/shard_map/all_to_all | solution.py:353
  12.0 1.5 %collective-permute-start.1 = (bf16[5,4,4,1,8,128]{5,4,2,0,1,3:T(8,128)(2,1)S(1)}, bf16[5,4,4,1,8,128]{5,4,2,0,1,3:T(8,128)(2,1)S(1)}, u32[]{:S(2)}, u32[]{:S(2)}) collective-permute-start(bf16[5,4,4,1,8,128]{5,4,2,0,1,3:T(8,128)(2,1)S(1)} %bitcast.85), channel_id=1, source_target_pairs={{0,4},{4,0},{8,12},{12,8},{16,20},{20,16},{24,28},{28,24},{1,5},{5... | collective-permute-start | bytes 491528 | tf_op jit(solution)/shard_map/ppermute | solution.py:142
  13.5 28.8 %copy-start.1 = (s32[1,4]{1,0:T(1,128)S(1)}, s32[1,4]{1,0:T(1,128)}, u32[]{:S(2)}) copy-start(s32[1,4]{1,0:T(1,128)} %length_ref.1) | copy-start | bytes 52
  13.6 12.0 %collective-permute-start.4 = (bf16[5,2,4,1,8,128]{5,4,2,1,0,3:T(8,128)(2,1)S(1)}, bf16[5,2,4,1,8,128]{5,4,2,1,0,3:T(8,128)(2,1)S(1)}, u32[]{:S(2)}, u32[]{:S(2)}) collective-permute-start(bf16[5,2,4,1,8,128]{5,4,2,1,0,3:T(8,128)(2,1)S(1)} %get-tuple-element.20), channel_id=1, source_target_pairs={{0,3},{1,2},{2,1},{3,0},{4,7},{5,6},{6,5},{7,4},{8,11},{9,10},{10,... | collective-permute-start | bytes 245768 | tf_op jit(solution)/shard_map/ppermute | solution.py:142
  16.1 12.5 %collective-permute-start.3 = (bf16[5,2,4,1,8,128]{5,4,2,1,0,3:T(8,128)(2,1)S(1)}, bf16[5,2,4,1,8,128]{5,4,2,1,0,3:T(8,128)(2,1)S(1)}, u32[]{:S(2)}, u32[]{:S(2)}) collective-permute-start(bf16[5,2,4,1,8,128]{5,4,2,1,0,3:T(8,128)(2,1)S(1)} %get-tuple-element.21), channel_id=1, source_target_pairs={{0,2},{1,3},{2,0},{3,1},{4,6},{5,7},{6,4},{7,5},{8,10},{9,11},{10,... | collective-permute-start | bytes 245768 | tf_op jit(solution)/shard_map/ppermute | solution.py:142
  16.6 12.0 %collective-permute-start.2 = (bf16[5,2,4,1,8,128]{5,4,2,1,0,3:T(8,128)(2,1)S(1)}, bf16[5,2,4,1,8,128]{5,4,2,1,0,3:T(8,128)(2,1)S(1)}, u32[]{:S(2)}, u32[]{:S(2)}) collective-permute-start(bf16[5,2,4,1,8,128]{5,4,2,1,0,3:T(8,128)(2,1)S(1)} %get-tuple-element.22), channel_id=1, source_target_pairs={{0,1},{1,0},{2,3},{3,2},{4,5},{5,4},{6,7},{7,6},{8,9},{9,8},{10,11... | collective-permute-start | bytes 245768 | tf_op jit(solution)/shard_map/ppermute | solution.py:142
  28.8 19.7 %collective-permute-start.5 = (bf16[130,8,128]{2,1,0:T(8,128)(2,1)S(1)}, bf16[130,8,128]{2,1,0:T(8,128)(2,1)S(1)}, u32[]{:S(2)}, u32[]{:S(2)}) collective-permute-start(bf16[130,8,128]{2,1,0:T(8,128)(2,1)S(1)} %pad_maximum_fusion.2), channel_id=1, source_target_pairs={{0,8},{4,12},{8,0},{12,4},{16,24},{20,28},{24,16},{28,20},{1,9},{5... | collective-permute-start | bytes 798728 | tf_op jit(solution)/shard_map/ppermute | solution.py:142
  44.2 17.3 %all-to-all-start.1 = ((bf16[32,7,8,128]{3,2,1,0:T(8,128)(2,1)}), bf16[32,7,8,128]{3,2,1,0:T(8,128)(2,1)S(1)}, u32[]{:S(2)}, u32[]{:S(2)}) async-start(bf16[32,7,8,128]{3,2,1,0:T(8,128)(2,1)} %bitcast.22), calls=%async_computation.1 | async-start | bytes 917504 | tf_op jit(solution)/shard_map/all_to_all | solution.py:353
  48.4 9.1 %copy-start = (s32[1,4,8]{2,1,0:T(4,128)S(1)}, s32[1,4,8]{2,1,0:T(4,128)}, u32[]{:S(2)}) copy-start(s32[1,4,8]{2,1,0:T(4,128)} %route_ref.3) | copy-start | bytes 388
  49.1 1.3 %collective-permute-start.6 = (bf16[4,4,1,8,128]{4,3,1,0,2:T(8,128)(2,1)S(1)}, bf16[4,4,1,8,128]{4,3,1,0,2:T(8,128)(2,1)S(1)}, u32[]{:S(2)}, u32[]{:S(2)}) collective-permute-start(bf16[4,4,1,8,128]{4,3,1,0,2:T(8,128)(2,1)S(1)} %slice_bitcast_fusion.7), channel_id=1, source_target_pairs={{0,4},{4,0},{8,12},{12,8},{16,20},{20,16},{24,28},{28,24},{1,5},{5... | collective-permute-start | bytes 98312 | tf_op jit(solution)/shard_map/ppermute | solution.py:142
  50.4 4.9 %collective-permute-start.9 = (bf16[2,4,1,8,128]{4,3,2,1,0:T(8,128)(2,1)S(1)}, bf16[2,4,1,8,128]{4,3,2,1,0:T(8,128)(2,1)S(1)}, u32[]{:S(2)}, u32[]{:S(2)}) collective-permute-start(bf16[2,4,1,8,128]{4,3,2,1,0:T(8,128)(2,1)S(1)} %get-tuple-element.29), channel_id=1, source_target_pairs={{0,3},{1,2},{2,1},{3,0},{4,7},{5,6},{6,5},{7,4},{8,11},{9,10},{10,... | collective-permute-start | bytes 49160 | tf_op jit(solution)/shard_map/ppermute | solution.py:142
  53.1 3.9 %collective-permute-start.7 = (bf16[2,4,1,8,128]{4,3,1,0,2:T(8,128)(2,1)S(1)}, bf16[2,4,1,8,128]{4,3,1,0,2:T(8,128)(2,1)S(1)}, u32[]{:S(2)}, u32[]{:S(2)}) collective-permute-start(bf16[2,4,1,8,128]{4,3,1,0,2:T(8,128)(2,1)S(1)} %get-tuple-element.31), channel_id=1, source_target_pairs={{0,1},{1,0},{2,3},{3,2},{4,5},{5,4},{6,7},{7,6},{8,9},{9,8},{10,11... | collective-permute-start | bytes 49160 | tf_op jit(solution)/shard_map/ppermute | solution.py:142
  53.7 3.8 %collective-permute-start.8 = (bf16[2,4,1,8,128]{4,3,1,0,2:T(8,128)(2,1)S(1)}, bf16[2,4,1,8,128]{4,3,1,0,2:T(8,128)(2,1)S(1)}, u32[]{:S(2)}, u32[]{:S(2)}) collective-permute-start(bf16[2,4,1,8,128]{4,3,1,0,2:T(8,128)(2,1)S(1)} %get-tuple-element.32), channel_id=1, source_target_pairs={{0,2},{1,3},{2,0},{3,1},{4,6},{5,7},{6,4},{7,5},{8,10},{9,11},{10,... | collective-permute-start | bytes 49160 | tf_op jit(solution)/shard_map/ppermute | solution.py:142

commit v9 on v8

--- a/solution.py
+++ b/solution.py
@@ -123,7 +123,9 @@
         part = pl.ds(0, direct_heads)
         for span in range(bag_count):
             at = route_ref[0, group, span]
-            pltpu.make_async_copy(source.at[:, at % CORES, at // CORES], target.at[span, :, part], sem).start()
+            pltpu.make_async_copy(
+                source.at[:, lax.rem(at, CORES), lax.div(at, CORES)], target.at[span, :, part], sem
+            ).start()
         pltpu.make_async_copy(source, source, sem).wait()
 
     return pl.pallas_call(

time: 63.3 us -> 63.3 us (level)
  no operation moved by 1% of the time
where the time goes in v9:
time: 63.3 us; the launch traced here: 62.4 us
  waiting for transfers between devices  35.6 us (56%)
  starting transfers between devices  19.7 us (31%)
  Pallas kernels  6.56 us (10%)
    ppermute x10, waiting for transfers between devices, swap(): lax.ppermute(rows, axis, [(index, index ^ distance) for index in range(la...  18.9 us
    all_to_all x2, waiting for transfers between devices, exchange(): lax.all_to_all(rows, AXES, split_axis=0, concat_axis=0, tiled=True, axis_...  16.7 us
    ppermute x10, starting transfers between devices, swap(): lax.ppermute(rows, axis, [(index, index ^ distance) for index in range(la...  11.7 us
    all_to_all x2, starting transfers between devices, exchange(): lax.all_to_all(rows, AXES, split_axis=0, concat_axis=0, tiled=True, axis_...  8.03 us
    pallas_call x1, Pallas kernels, attend(): pl.pallas_call(kernel, out_shape=jax.ShapeDtypeStruct((*((group_count, CO...  1.83 us
    pallas_call x1, Pallas kernels, pack_spans(): pl.pallas_call(kernel, out_shape=[pltpu.VMEM(size, dtype) for size in (sh...  1.44 us
  transfers between devices with their start and end apart: 12, of which 10 were waited for; matrix products, arithmetic and copies ran while one was open for 1% of the time, Pallas kernels for 7%

profile of v9, /device:TPU:0, one launch (start us, length us, event | category | flops | bytes accessed | tf_op | source)
XLA Modules:
  0.0 62.4 jit_solution(10563570667700539553)
XLA Ops:
  0.0 1.4 %pack_spans.1 = (bf16[4,2,4,3,7,8,128]{6,5,4,3,2,1,0:T(8,128)(2,1)S(1)}, bf16[32,8,128]{2,1,0:T(8,128)(2,1)S(1)}, bf16[65,8,128]{2,1,0:T(8,128)(2,1)S(1)}) custom-call(s32[1,4,8]{2,1,0:T(4,128)} %route_ref.3, s32[1,4]{1,0:T(1,128)} %length_ref.1, bf16[8,4,8,8,128]{4,3,2,1,0:T(8,128)(2,1)} %bitcast.79, bf16[8,4,8,8,128]{4,3,2,1,0:T(8,128)(2,1)} %bitcast.80, ...), custom_call_target="tpu_custom_call" | custom-call | tf_op jit(solution)/shard_map/pack_spans/pallas_call | solution.py:70
  1.5 4.1 %collective-permute-start = (bf16[65,8,128]{2,1,0:T(8,128)(2,1)S(1)}, bf16[65,8,128]{2,1,0:T(8,128)(2,1)S(1)}, u32[]{:S(2)}, u32[]{:S(2)}) collective-permute-start(bf16[65,8,128]{2,1,0:T(8,128)(2,1)S(1)} %get-tuple-element.12.near_ref), channel_id=1, source_target_pairs={{0,16},{4,20},{8,24},{12,28},{16,0},{20,4},{24,8},{28,12},{1,17},{... | collective-permute-start | bytes 399368 | tf_op jit(solution)/shard_map/ppermute | solution.py:144
  5.6 1.1 %settle.1 = bf16[32,3,7,8,128]{4,3,2,1,0:T(8,128)(2,1)} custom-call(bf16[32,3,7,8,128]{4,3,2,1,0:T(8,128)(2,1)S(1)} %bitcast.73), custom_call_target="tpu_custom_call" | custom-call | tf_op jit(solution)/shard_map/settle/pallas_call | solution.py:167
  6.7 3.8 %all-to-all-start = ((bf16[32,3,7,8,128]{4,3,2,1,0:T(8,128)(2,1)}), bf16[32,3,7,8,128]{4,3,2,1,0:T(8,128)(2,1)S(1)}, u32[]{:S(2)}, u32[]{:S(2)}) async-start(bf16[32,3,7,8,128]{4,3,2,1,0:T(8,128)(2,1)} %settle.1), calls=%async_computation | async-start | bytes 2752512 | tf_op jit(solution)/shard_map/all_to_all | solution.py:355
  10.5 1.4 %collective-permute-done.across_ref = bf16[65,8,128]{2,1,0:T(8,128)(2,1)S(1)} collective-permute-done((bf16[65,8,128]{2,1,0:T(8,128)(2,1)S(1)}, bf16[65,8,128]{2,1,0:T(8,128)(2,1)S(1)}, u32[]{:S(2)}, u32[]{:S(2)}) %collective-permute-start) | collective-permute-done | bytes 133152 | tf_op jit(solution)/shard_map/ppermute | solution.py:144
  12.0 0.1 collective-permute-start.1
  12.1 1.4 %collective-permute-done.1 = bf16[5,4,4,1,8,128]{5,4,2,0,1,3:T(8,128)(2,1)S(1)} collective-permute-done((bf16[5,4,4,1,8,128]{5,4,2,0,1,3:T(8,128)(2,1)S(1)}, bf16[5,4,4,1,8,128]{5,4,2,0,1,3:T(8,128)(2,1)S(1)}, u32[]{:S(2)}, u32[]{:S(2)}) %collective-permute-start.1) | collective-permute-done | bytes 163872 | tf_op jit(solution)/shard_map/ppermute | solution.py:144
  13.5 0.0 copy-start.1
  13.6 2.6 %collective-permute-start.4 = (bf16[5,2,4,1,8,128]{5,4,2,1,0,3:T(8,128)(2,1)S(1)}, bf16[5,2,4,1,8,128]{5,4,2,1,0,3:T(8,128)(2,1)S(1)}, u32[]{:S(2)}, u32[]{:S(2)}) collective-permute-start(bf16[5,2,4,1,8,128]{5,4,2,1,0,3:T(8,128)(2,1)S(1)} %get-tuple-element.20), channel_id=1, source_target_pairs={{0,3},{1,2},{2,1},{3,0},{4,7},{5,6},{6,5},{7,4},{8,11},{9,10},{10,... | collective-permute-start | bytes 245768 | tf_op jit(solution)/shard_map/ppermute | solution.py:144
  16.1 0.5 collective-permute-start.3
  16.6 0.5 collective-permute-start.2
  17.1 8.4 %collective-permute-done.4 = bf16[5,2,4,1,8,128]{5,4,2,1,0,3:T(8,128)(2,1)S(1)} collective-permute-done((bf16[5,2,4,1,8,128]{5,4,2,1,0,3:T(8,128)(2,1)S(1)}, bf16[5,2,4,1,8,128]{5,4,2,1,0,3:T(8,128)(2,1)S(1)}, u32[]{:S(2)}, u32[]{:S(2)}) %collective-permute-start.4) | collective-permute-done | bytes 81952 | tf_op jit(solution)/shard_map/ppermute | solution.py:144
  25.5 3.1 %collective-permute-done.3 = bf16[5,2,4,1,8,128]{5,4,2,1,0,3:T(8,128)(2,1)S(1)} collective-permute-done((bf16[5,2,4,1,8,128]{5,4,2,1,0,3:T(8,128)(2,1)S(1)}, bf16[5,2,4,1,8,128]{5,4,2,1,0,3:T(8,128)(2,1)S(1)}, u32[]{:S(2)}, u32[]{:S(2)}) %collective-permute-start.3) | collective-permute-done | bytes 81952 | tf_op jit(solution)/shard_map/ppermute | solution.py:144
  28.7 0.1 pad_maximum_fusion.1
  28.8 0.1 collective-permute-start.5
  28.9 13.5 %all-to-all-done.packed_ref = bf16[32,3,7,8,128]{4,3,2,1,0:T(8,128)(2,1)S(1)} async-done(((bf16[32,3,7,8,128]{4,3,2,1,0:T(8,128)(2,1)}), bf16[32,3,7,8,128]{4,3,2,1,0:T(8,128)(2,1)S(1)}, u32[]{:S(2)}, u32[]{:S(2)}) %all-to-all-start) | async-done | bytes 1376288 | tf_op jit(solution)/shard_map/all_to_all | solution.py:355
  42.4 1.8 %attend_bag.1 = bf16[4,2,4,7,8,128]{5,4,3,2,1,0:T(8,128)(2,1)} custom-call(s32[1,4]{1,0:T(1,128)S(1)} %copy-done.1, bf16[32,3,7,8,128]{4,3,2,1,0:T(8,128)(2,1)S(1)} %all-to-all-done.packed_ref, bf16[5,4,2,4,1,8,128]{6,5,4,3,2,1,0:T(8,128)(2,1)S(1)} %get-tuple-element.18.refs_0_), custom_call_target="tpu_custom_call" | custom-call | tf_op jit(solution)/shard_map/attend_bag/pallas_call | solution.py:335
  44.2 4.2 %all-to-all-start.1 = ((bf16[32,7,8,128]{3,2,1,0:T(8,128)(2,1)}), bf16[32,7,8,128]{3,2,1,0:T(8,128)(2,1)S(1)}, u32[]{:S(2)}, u32[]{:S(2)}) async-start(bf16[32,7,8,128]{3,2,1,0:T(8,128)(2,1)} %bitcast.22), calls=%async_computation.1 | async-start | bytes 917504 | tf_op jit(solution)/shard_map/all_to_all | solution.py:355
  48.4 0.0 copy-start
  48.5 0.1 pad_maximum_fusion.pair_ref
  48.6 0.5 attend_plane.1
  49.1 0.3 collective-permute-start.6
  49.4 1.0 %collective-permute-done.6 = bf16[4,4,1,8,128]{4,3,1,0,2:T(8,128)(2,1)S(1)} collective-permute-done((bf16[4,4,1,8,128]{4,3,1,0,2:T(8,128)(2,1)S(1)}, bf16[4,4,1,8,128]{4,3,1,0,2:T(8,128)(2,1)S(1)}, u32[]{:S(2)}, u32[]{:S(2)}) %collective-permute-start.6) | collective-permute-done | bytes 32800 | tf_op jit(solution)/shard_map/ppermute | solution.py:144
  50.4 2.7 %collective-permute-start.9 = (bf16[2,4,1,8,128]{4,3,2,1,0:T(8,128)(2,1)S(1)}, bf16[2,4,1,8,128]{4,3,2,1,0:T(8,128)(2,1)S(1)}, u32[]{:S(2)}, u32[]{:S(2)}) collective-permute-start(bf16[2,4,1,8,128]{4,3,2,1,0:T(8,128)(2,1)S(1)} %get-tuple-element.29), channel_id=1, source_target_pairs={{0,3},{1,2},{2,1},{3,0},{4,7},{5,6},{6,5},{7,4},{8,11},{9,10},{10,... | collective-permute-start | bytes 49160 | tf_op jit(solution)/shard_map/ppermute | solution.py:144
  53.1 0.6 collective-permute-start.7
  53.7 0.3 collective-permute-start.8
  53.9 1.4 %collective-permute-done.9.refs_3_ = bf16[2,4,1,8,128]{4,3,2,1,0:T(8,128)(2,1)S(1)} collective-permute-done((bf16[2,4,1,8,128]{4,3,2,1,0:T(8,128)(2,1)S(1)}, bf16[2,4,1,8,128]{4,3,2,1,0:T(8,128)(2,1)S(1)}, u32[]{:S(2)}, u32[]{:S(2)}) %collective-permute-start.9) | collective-permute-done | bytes 16416 | tf_op jit(solution)/shard_map/ppermute | solution.py:144
  55.3 1.7 %collective-permute-done.7 = bf16[2,4,1,8,128]{4,3,1,0,2:T(8,128)(2,1)S(1)} collective-permute-done((bf16[2,4,1,8,128]{4,3,1,0,2:T(8,128)(2,1)S(1)}, bf16[2,4,1,8,128]{4,3,1,0,2:T(8,128)(2,1)S(1)}, u32[]{:S(2)}, u32[]{:S(2)}) %collective-permute-start.7) | collective-permute-done | bytes 16416 | tf_op jit(solution)/shard_map/ppermute | solution.py:144
  57.0 0.5 collective-permute-done.8
  57.5 0.8 %unpack_aside.1._ = bf16[8,4,8,8,128]{4,3,2,1,0:T(8,128)(2,1)} custom-call(s32[1,4,8]{2,1,0:T(4,128)S(1)} %copy-done, bf16[2,4,1,8,128]{4,3,2,1,0:T(8,128)(2,1)S(1)} %get-tuple-element.30.refs_0_, bf16[2,4,1,8,128]{4,3,2,1,0:T(8,128)(2,1)S(1)} %bitcast.76, bf16[2,4,1,8,128]{4,3,2,1,0:T(8,128)(2,1)S(1)} %bitcast.77, ...), custom_call_target="tpu_custom_call" | custom-call | tf_op jit(solution)/shard_map/unpack_aside/pallas_call | solution.py:103
  58.3 3.2 %all-to-all-done.1 = bf16[32,7,8,128]{3,2,1,0:T(8,128)(2,1)S(1)} async-done(((bf16[32,7,8,128]{3,2,1,0:T(8,128)(2,1)}), bf16[32,7,8,128]{3,2,1,0:T(8,128)(2,1)S(1)}, u32[]{:S(2)}, u32[]{:S(2)}) %all-to-all-start.1) | async-done | bytes 458784 | tf_op jit(solution)/shard_map/all_to_all | solution.py:355
  61.5 0.9 %unpack_spans.1 = bf16[8,4,8,8,128]{4,3,2,1,0:T(8,128)(2,1)} custom-call(s32[1,4,8]{2,1,0:T(4,128)S(1)} %copy-done, bf16[4,2,4,7,8,128]{5,4,3,2,1,0:T(8,128)(2,1)S(1)} %bitcast.72, bf16[8,4,8,8,128]{4,3,2,1,0:T(8,128)(2,1)} %unpack_aside.1._), custom_call_target="tpu_custom_call", output_to_operand_aliasing={{}: (2, {})} | custom-call | tf_op jit(solution)/shard_map/unpack_spans/pallas_call | solution.py:131
  (20 shorter events, 0.2 us)
Async XLA Ops:
  1.5 10.5 %collective-permute-start = (bf16[65,8,128]{2,1,0:T(8,128)(2,1)S(1)}, bf16[65,8,128]{2,1,0:T(8,128)(2,1)S(1)}, u32[]{:S(2)}, u32[]{:S(2)}) collective-permute-start(bf16[65,8,128]{2,1,0:T(8,128)(2,1)S(1)} %get-tuple-element.12.near_ref), channel_id=1, source_target_pairs={{0,16},{4,20},{8,24},{12,28},{16,0},{20,4},{24,8},{28,12},{1,17},{... | collective-permute-start | bytes 399368 | tf_op jit(solution)/shard_map/ppermute | solution.py:144
  6.7 35.7 %all-to-all-start = ((bf16[32,3,7,8,128]{4,3,2,1,0:T(8,128)(2,1)}), bf16[32,3,7,8,128]{4,3,2,1,0:T(8,128)(2,1)S(1)}, u32[]{:S(2)}, u32[]{:S(2)}) async-start(bf16[32,3,7,8,128]{4,3,2,1,0:T(8,128)(2,1)} %settle.1), calls=%async_computation | async-start | bytes 2752512 | tf_op jit(solution)/shard_map/all_to_all | solution.py:355
  12.0 1.5 %collective-permute-start.1 = (bf16[5,4,4,1,8,128]{5,4,2,0,1,3:T(8,128)(2,1)S(1)}, bf16[5,4,4,1,8,128]{5,4,2,0,1,3:T(8,128)(2,1)S(1)}, u32[]{:S(2)}, u32[]{:S(2)}) collective-permute-start(bf16[5,4,4,1,8,128]{5,4,2,0,1,3:T(8,128)(2,1)S(1)} %bitcast.85), channel_id=1, source_target_pairs={{0,4},{4,0},{8,12},{12,8},{16,20},{20,16},{24,28},{28,24},{1,5},{5... | collective-permute-start | bytes 491528 | tf_op jit(solution)/shard_map/ppermute | solution.py:144
  13.5 28.8 %copy-start.1 = (s32[1,4]{1,0:T(1,128)S(1)}, s32[1,4]{1,0:T(1,128)}, u32[]{:S(2)}) copy-start(s32[1,4]{1,0:T(1,128)} %length_ref.1) | copy-start | bytes 52
  13.6 12.0 %collective-permute-start.4 = (bf16[5,2,4,1,8,128]{5,4,2,1,0,3:T(8,128)(2,1)S(1)}, bf16[5,2,4,1,8,128]{5,4,2,1,0,3:T(8,128)(2,1)S(1)}, u32[]{:S(2)}, u32[]{:S(2)}) collective-permute-start(bf16[5,2,4,1,8,128]{5,4,2,1,0,3:T(8,128)(2,1)S(1)} %get-tuple-element.20), channel_id=1, source_target_pairs={{0,3},{1,2},{2,1},{3,0},{4,7},{5,6},{6,5},{7,4},{8,11},{9,10},{10,... | collective-permute-start | bytes 245768 | tf_op jit(solution)/shard_map/ppermute | solution.py:144
  16.1 12.5 %collective-permute-start.3 = (bf16[5,2,4,1,8,128]{5,4,2,1,0,3:T(8,128)(2,1)S(1)}, bf16[5,2,4,1,8,128]{5,4,2,1,0,3:T(8,128)(2,1)S(1)}, u32[]{:S(2)}, u32[]{:S(2)}) collective-permute-start(bf16[5,2,4,1,8,128]{5,4,2,1,0,3:T(8,128)(2,1)S(1)} %get-tuple-element.21), channel_id=1, source_target_pairs={{0,2},{1,3},{2,0},{3,1},{4,6},{5,7},{6,4},{7,5},{8,10},{9,11},{10,... | collective-permute-start | bytes 245768 | tf_op jit(solution)/shard_map/ppermute | solution.py:144
  16.6 12.0 %collective-permute-start.2 = (bf16[5,2,4,1,8,128]{5,4,2,1,0,3:T(8,128)(2,1)S(1)}, bf16[5,2,4,1,8,128]{5,4,2,1,0,3:T(8,128)(2,1)S(1)}, u32[]{:S(2)}, u32[]{:S(2)}) collective-permute-start(bf16[5,2,4,1,8,128]{5,4,2,1,0,3:T(8,128)(2,1)S(1)} %get-tuple-element.22), channel_id=1, source_target_pairs={{0,1},{1,0},{2,3},{3,2},{4,5},{5,4},{6,7},{7,6},{8,9},{9,8},{10,11... | collective-permute-start | bytes 245768 | tf_op jit(solution)/shard_map/ppermute | solution.py:144
  28.8 19.7 %collective-permute-start.5 = (bf16[130,8,128]{2,1,0:T(8,128)(2,1)S(1)}, bf16[130,8,128]{2,1,0:T(8,128)(2,1)S(1)}, u32[]{:S(2)}, u32[]{:S(2)}) collective-permute-start(bf16[130,8,128]{2,1,0:T(8,128)(2,1)S(1)} %pad_maximum_fusion.2), channel_id=1, source_target_pairs={{0,8},{4,12},{8,0},{12,4},{16,24},{20,28},{24,16},{28,20},{1,9},{5... | collective-permute-start | bytes 798728 | tf_op jit(solution)/shard_map/ppermute | solution.py:144
  44.2 17.3 %all-to-all-start.1 = ((bf16[32,7,8,128]{3,2,1,0:T(8,128)(2,1)}), bf16[32,7,8,128]{3,2,1,0:T(8,128)(2,1)S(1)}, u32[]{:S(2)}, u32[]{:S(2)}) async-start(bf16[32,7,8,128]{3,2,1,0:T(8,128)(2,1)} %bitcast.22), calls=%async_computation.1 | async-start | bytes 917504 | tf_op jit(solution)/shard_map/all_to_all | solution.py:355
  48.4 9.1 %copy-start = (s32[1,4,8]{2,1,0:T(4,128)S(1)}, s32[1,4,8]{2,1,0:T(4,128)}, u32[]{:S(2)}) copy-start(s32[1,4,8]{2,1,0:T(4,128)} %route_ref.3) | copy-start | bytes 388
  49.1 1.3 %collective-permute-start.6 = (bf16[4,4,1,8,128]{4,3,1,0,2:T(8,128)(2,1)S(1)}, bf16[4,4,1,8,128]{4,3,1,0,2:T(8,128)(2,1)S(1)}, u32[]{:S(2)}, u32[]{:S(2)}) collective-permute-start(bf16[4,4,1,8,128]{4,3,1,0,2:T(8,128)(2,1)S(1)} %slice_bitcast_fusion.7), channel_id=1, source_target_pairs={{0,4},{4,0},{8,12},{12,8},{16,20},{20,16},{24,28},{28,24},{1,5},{5... | collective-permute-start | bytes 98312 | tf_op jit(solution)/shard_map/ppermute | solution.py:144
  50.4 4.9 %collective-permute-start.9 = (bf16[2,4,1,8,128]{4,3,2,1,0:T(8,128)(2,1)S(1)}, bf16[2,4,1,8,128]{4,3,2,1,0:T(8,128)(2,1)S(1)}, u32[]{:S(2)}, u32[]{:S(2)}) collective-permute-start(bf16[2,4,1,8,128]{4,3,2,1,0:T(8,128)(2,1)S(1)} %get-tuple-element.29), channel_id=1, source_target_pairs={{0,3},{1,2},{2,1},{3,0},{4,7},{5,6},{6,5},{7,4},{8,11},{9,10},{10,... | collective-permute-start | bytes 49160 | tf_op jit(solution)/shard_map/ppermute | solution.py:144
  53.1 3.9 %collective-permute-start.7 = (bf16[2,4,1,8,128]{4,3,1,0,2:T(8,128)(2,1)S(1)}, bf16[2,4,1,8,128]{4,3,1,0,2:T(8,128)(2,1)S(1)}, u32[]{:S(2)}, u32[]{:S(2)}) collective-permute-start(bf16[2,4,1,8,128]{4,3,1,0,2:T(8,128)(2,1)S(1)} %get-tuple-element.31), channel_id=1, source_target_pairs={{0,1},{1,0},{2,3},{3,2},{4,5},{5,4},{6,7},{7,6},{8,9},{9,8},{10,11... | collective-permute-start | bytes 49160 | tf_op jit(solution)/shard_map/ppermute | solution.py:144
  53.7 3.8 %collective-permute-start.8 = (bf16[2,4,1,8,128]{4,3,1,0,2:T(8,128)(2,1)S(1)}, bf16[2,4,1,8,128]{4,3,1,0,2:T(8,128)(2,1)S(1)}, u32[]{:S(2)}, u32[]{:S(2)}) collective-permute-start(bf16[2,4,1,8,128]{4,3,1,0,2:T(8,128)(2,1)S(1)} %get-tuple-element.32), channel_id=1, source_target_pairs={{0,2},{1,3},{2,0},{3,1},{4,6},{5,7},{6,4},{7,5},{8,10},{9,11},{10,... | collective-permute-start | bytes 49160 | tf_op jit(solution)/shard_map/ppermute | solution.py:144
